TPU v7x, 32 devices: a whole 2x2x4 slice. The times are simulated.
32 devices in a mesh: rep: 2 (over x), ga: 16 (over z, y, core).
Axes of the slice: x: 2, y: 2, z: 4, core: 2. Of those that a mesh axis runs over, the one named last changes fastest.
Arguments:
- positions: float32 [64, 3, 768], P('rep', None, 'ga'), parts along dimension 0, may hold values from -3 to 23, as said below
- weights: int32 [1, 32], replicated, may hold values from 1 to 16
- psi: bfloat16 [2, 512, 2, 32768], P('rep', None, None, 'ga'), parts along dimension 0, may hold values from -5 to 5
- vloc: float32 [2, 32768], P('rep'), parts along dimension 0, may hold values from -8 to 8
Outputs:
- psi_new: bfloat16 [2, 512, 2, 32768], P('rep', None, None, 'ga'), parts along dimension 0
- bead_forces: float32 [64, 3, 768], P('rep', None, 'ga'), parts along dimension 0
There are 2 independent parts, one for each index of `rep`. A program takes and returns all parts, laid end to end along the dimension named above; an argument that names none is the same for every part. Nothing has to cross between parts.
Inputs may be any that keep to these rules, and one draw needn't show every extreme that they name: `positions`: atom 3w is the oxygen of water w and atoms 3w+1 and 3w+2 are its hydrogens; in every bead each hydrogen lies between 1.0 and 2.6 from its oxygen.
All inputs are finite; a program needn't handle non-finite values.
Results may differ from a plain program's by a relative error of at most 0.0037.
The roundings to bfloat16 on the way count: a program that leaves them out, or rounds other values in their place, can miss the bound.
Values may be sent and summed in bfloat16 or wider, within the bound.
No kernel may reach another device: no remote copies, remote signals or barrier semaphores. Data moves between devices by JAX's collectives and lax.ppermute only.
A program may use at most 192 MiB of HBM per device.

v0:
```python
import jax
import jax.numpy as jnp
from jax import lax
from jax.sharding import PartitionSpec as P

BEADS = 32
CBEADS = 1
WATERS = 256
NGRID = 32
GVECS = 32768


box_length = 20.0
bond_stiff = 0.5
bond_rest = 1.8
spring_stiff = 2.0
width_square = 0.09
step_size = 0.02
nonlocal_strength = 250.0
occupation = 2.0
highest = lax.Precision.HIGHEST


def frequency(index, count):
    signed = jnp.where(index < count // 2, index, index - count)
    return signed.astype(jnp.float32) * (2.0 * jnp.pi / box_length)


def field_forces(positions):
    oxygen = positions[:, :, 0::3]
    toward_one = positions[:, :, 1::3] - oxygen
    toward_two = positions[:, :, 2::3] - oxygen

    def stretch(offset):
        length = jnp.sqrt(jnp.sum(offset * offset, axis=1, keepdims=True))
        return -bond_stiff * (length - bond_rest) * offset / length

    pull_one = stretch(toward_one)
    pull_two = stretch(toward_two)
    bonds = jnp.stack([-(pull_one + pull_two), pull_one, pull_two], axis=3).reshape(positions.shape)
    springs = 2.0 * positions - jnp.roll(positions, 1, axis=0) - jnp.roll(positions, -1, axis=0)
    return bonds - spring_stiff * springs


def inner(left_mat, right_mat):
    return lax.dot_general(
        left_mat, right_mat, (((1,), (1,)), ((), ())), preferred_element_type=jnp.float32
    )


def real_form(freq_index, group_index):
    product = freq_index[:, None] * freq_index[None, :] % NGRID
    angle = product.astype(jnp.float32) * (2.0 * jnp.pi / NGRID)
    same = (group_index[:, None] == group_index[None, :]).astype(jnp.float32)
    cosines = jnp.cos(angle) * same
    sines = jnp.sin(angle) * same
    return jnp.stack([jnp.stack([cosines, sines], 1), jnp.stack([-sines, cosines], 1)], 0)


def plane_table():
    index = jnp.arange(NGRID, dtype=jnp.int32)
    return real_form(index, jnp.zeros_like(index))


def block_table(length, within):
    index = jnp.arange(length, dtype=jnp.int32)
    if within:
        return real_form(index % NGRID, index // NGRID)
    return real_form(index // NGRID, index % NGRID)


def per_device(positions, weights, psi, vloc):
    near_forces = field_forces(positions)
    weight_float = weights.astype(jnp.float32)
    mixing = weight_float / jnp.sum(weight_float, axis=1, keepdims=True)
    centres = jnp.einsum("cj,jan->can", mixing, positions, precision=highest)
    everyone = lax.all_gather(centres, "ga", axis=2, tiled=True)
    parts = lax.axis_size("ga")
    bands = psi.shape[1]
    local_g = psi.shape[3]
    flat_index = lax.axis_index("ga") * local_g + jnp.arange(local_g, dtype=jnp.int32)
    gvectors = jnp.stack(
        [
            frequency(flat_index // (NGRID * NGRID), NGRID),
            frequency(flat_index // NGRID % NGRID, NGRID),
            frequency(flat_index % NGRID, NGRID),
        ]
    )
    square = jnp.sum(gvectors * gvectors, axis=0)
    profile = jnp.exp(-0.5 * width_square * square)
    kinetic = 0.5 * square
    x_table = plane_table()
    y_table = block_table(NGRID * NGRID, False)
    z_table = block_table(local_g, True)
    oxygens = everyone[0][:, 0::3]
    phases = jnp.einsum("ai,ag->ig", oxygens, gvectors, precision=highest)
    wave_cos = profile * jnp.cos(phases)
    wave_sin = profile * jnp.sin(phases)
    table = jnp.concatenate(
        [jnp.concatenate([wave_cos, -wave_sin], 1), jnp.concatenate([wave_sin, wave_cos], 1)], 0
    ).astype(jnp.bfloat16)
    wavefunc = psi[0].reshape(bands, 2 * local_g)
    real_part = wavefunc[:, :local_g]
    imag_part = wavefunc[:, local_g:]
    partial_proj = (inner(table, wavefunc) * (1.0 / GVECS)).reshape(2, WATERS, bands)
    share = lax.psum_scatter(partial_proj, "ga", scatter_dimension=1, tiled=True).astype(
        jnp.bfloat16
    )
    paired = jnp.concatenate([wavefunc, jnp.concatenate([imag_part, -real_part], 1)], 0).reshape(
        2, bands, 2 * local_g
    )
    table_blocks = table.reshape(2, WATERS, 2 * local_g)
    all_proj = lax.all_gather(share, "ga", axis=1, tiled=True)
    nonlocal_term = jnp.einsum(
        "kib,kig->bg", all_proj, table_blocks, preferred_element_type=jnp.float32
    )
    weighted = jnp.einsum("kib,kbg->ig", all_proj, paired, preferred_element_type=jnp.float32)
    mixed_wave = wave_cos * weighted[:, local_g:] + wave_sin * weighted[:, :local_g]
    force_part = (
        2.0
        * occupation
        * nonlocal_strength
        / GVECS
        * jnp.einsum("ag,ig->ai", gvectors, mixed_wave, precision=highest)
    )
    oxygen_force = lax.psum_scatter(force_part, "ga", scatter_dimension=1, tiled=True)
    hydrogen_zero = jnp.zeros_like(oxygen_force)
    dft_forces = [jnp.stack([oxygen_force, hydrogen_zero, hydrogen_zero], axis=2).reshape(3, -1)]
    wave_float = psi[0].astype(jnp.float32)
    grid_potential = vloc[0].reshape(1, 1, NGRID, NGRID * NGRID)
    grouped_raw = psi[0].reshape(parts, bands // parts, 2, local_g)
    planes = lax.all_to_all(grouped_raw, "ga", split_axis=0, concat_axis=3, tiled=True)
    band_count = planes.shape[1]
    blocks_whole = planes.astype(jnp.float32).reshape(band_count, 2, NGRID**3 // local_g, local_g)
    along_z = jnp.einsum("mckp,cpdq->mdkq", blocks_whole, z_table, precision=highest) * (
        1.0 / NGRID
    )
    grid = along_z.reshape(band_count, 2, NGRID, NGRID * NGRID)
    grid = jnp.einsum("mcxr,cxdw->mdwr", grid, x_table, precision=highest) * (1.0 / NGRID)
    grid = jnp.einsum("mcxp,cpdq->mdxq", grid, y_table, precision=highest) * (1.0 / NGRID)
    grid = grid * grid_potential
    grid = jnp.einsum("mdxq,cpdq->mcxp", grid, y_table, precision=highest)
    grid = jnp.einsum("mdwr,cxdw->mcxr", grid, x_table, precision=highest)
    returning = grid.reshape(1, band_count, 2, NGRID**3)
    returned = lax.all_to_all(
        returning.astype(jnp.bfloat16), "ga", split_axis=3, concat_axis=0, tiled=True
    ).astype(returning.dtype)
    returned = returned.reshape(bands, 2, local_g)
    potential = jnp.einsum("bdq,cpdq->bcp", returned, z_table, precision=highest)
    hamil_re = (
        kinetic * wave_float[:, 0]
        + potential[:, 0]
        + nonlocal_strength * nonlocal_term[:, :local_g]
    )
    hamil_im = (
        kinetic * wave_float[:, 1]
        + potential[:, 1]
        + nonlocal_strength * nonlocal_term[:, local_g:]
    )
    trial = jnp.concatenate(
        [wave_float[:, 0] - step_size * hamil_re, wave_float[:, 1] - step_size * hamil_im], 1
    ).astype(jnp.bfloat16)
    rotated = jnp.concatenate(
        [trial, jnp.concatenate([-trial[:, local_g:], trial[:, :local_g]], 1)], 0
    )
    margin = lax.psum(inner(trial, rotated) * (1.0 / GVECS), "ga")
    identity_rows = jnp.concatenate(
        [jnp.eye(bands, dtype=jnp.float32), jnp.zeros((bands, bands), jnp.float32)], 1
    )
    mixer = (1.5 * identity_rows - 0.5 * margin).astype(jnp.bfloat16)
    updated = jnp.dot(mixer, rotated, preferred_element_type=jnp.float32)
    new_waves = [updated.astype(jnp.bfloat16).reshape(bands, 2, local_g)]
    contracted_force = jnp.einsum("cj,can->jan", mixing, jnp.stack(dft_forces), precision=highest)
    bead_forces = near_forces + BEADS / CBEADS * contracted_force
    return (jnp.stack(new_waves), bead_forces)


def solution(mesh):
    placed = (P("rep", None, "ga"), P(), P("rep", None, None, "ga"), P("rep", None))
    return jax.shard_map(
        per_device,
        mesh=mesh,
        in_specs=placed,
        out_specs=(P("rep", None, None, "ga"), P("rep", None, "ga")),
        check_vma=False,
    )
```

profile of v0, /device:TPU:0, one launch (start us, length us, event | category | flops | bytes accessed | tf_op | source)
XLA Modules:
  0.0 955.1 jit_solution(13431449668949625740)
XLA Ops:
  7.2 6.1 copy.56
  13.3 7.6 all-to-all-start
  21.6 17.4 %compare_select_fusion.2 = (f32[1024,1,1024]{2,0,1:T(8,128)S(1)}, f32[1024,1,1024]{2,0,1:T(8,128)S(1)}, f32[1024,1,1024]{2,0,1:T(8,128)S(1)}) fusion(s32[1024]{0:T(1024)S(1)} %get-tuple-element.51, s32[1024]{0:T(1024)S(1)} %get-tuple-element.52), kind=kLoop, calls=%fused_computation.48 | loop fusion | flops 18874368 | bytes 12591104 | tf_op jit(solution)/shard_map/mul | solution.py:56
  38.9 6.8 maximum_bitcast_fusion.2
  45.7 70.9 %compare_select_fusion = (f32[2048,1,2048]{2,0,1:T(8,128)S(1)}, f32[2048,1,2048]{2,0,1:T(8,128)}, f32[2048,1,2048]{2,0,1:T(8,128)}) fusion(s32[2048]{0:T(1024)S(1)} %get-tuple-element.53, s32[2048]{0:T(1024)S(1)} %get-tuple-element.54), kind=kLoop, calls=%fused_computation.11 | loop fusion | flops 75497472 | bytes 50348032 | tf_op jit(solution)/shard_map/mul | solution.py:56
  116.6 38.3 %maximum_bitcast_fusion = (f32[1,2048,2,2048]{3,1,0,2:T(8,128)}, f32[1,2048,2,2048]{3,1,0,2:T(8,128)}) fusion(f32[2048,1,2048]{2,0,1:T(8,128)S(1)} %get-tuple-element.37, f32[2048,1,2048]{2,0,1:T(8,128)} %get-tuple-element.39, f32[2048,1,2048]{2,0,1:T(8,128)} %get-tuple-element.38), kind=kLoop, calls=%fused_computation.4 | loop fusion | flops 16777216 | bytes 117440512 | tf_op jit(solution)/shard_map/stack | solution.py:57
  155.0 59.7 %fusion.17 = f32[32,2,16,2048]{3,0,2,1:T(8,128)S(1)} fusion(f32[1,2048,2,2048]{3,1,0,2:T(8,128)} %get-tuple-element.17, f32[1,2048,2,2048]{3,1,0,2:T(8,128)} %get-tuple-element.16, bf16[16,32,2,2048]{3,1,2,0:T(8,128)(2,1)} %all-to-all-done), kind=kOutput, calls=%fused_computation.37 | convolution fusion | flops 103098089472 | bytes 79691776 | tf_op jit(solution)/shard_map/mckp,cpdq->mdkq/dot_general | solution.py:135
  214.6 8.2 copy.57
  222.8 9.4 reshape.1000
  232.2 11.9 %fusion.16 = f32[32,2,32,1024]{3,2,0,1:T(8,128)} fusion(f32[32,2,32,1024,1]{3,2,1,0,4:T(8,128)} %reshape.1000, f32[1,32,2,32]{1,3,0,2:T(8,128)S(1)} %get-tuple-element.36, f32[1,32,2,32]{1,3,0,2:T(8,128)S(1)} %get-tuple-element.35), kind=kOutput, calls=%fused_computation.35 | convolution fusion | flops 1612713984 | bytes 16793600 | tf_op jit(solution)/shard_map/mcxr,cxdw->mdwr/dot_general | solution.py:139
  244.0 78.9 %fusion.13 = f32[32,2,32,1024,1]{3,0,2,1,4:T(8,128)} fusion(f32[32,1024]{1,0:T(8,128)S(1)} %mul.488, f32[32,2,32,1024]{3,2,0,1:T(8,128)} %fusion.16, f32[1,1024,2,1024]{3,1,0,2:T(8,128)} %get-tuple-element.21, f32[1,1024,2,1024]{3,1,0,2:T(8,128)} %get-tuple-element.20), kind=kOutput, calls=%fused_computation.30 | convolution fusion | flops 51545899008 | bytes 33685504 | tf_op jit(solution)/shard_map/mcxp,cpdq->mdxq/dot_general | solution.py:140
  323.0 72.7 %fusion.8 = f32[2,1024,32,32,1]{1,3,4,0,2:T(8,128)} fusion(f32[32,2,32,1024,1]{3,0,2,1,4:T(8,128)} %fusion.13, f32[1,1024,2,1024]{3,1,0,2:T(8,128)S(1)} %bitcast.215, f32[1,1024,2,1024]{3,1,0,2:T(8,128)S(1)} %bitcast.213), kind=kOutput, calls=%fused_computation.19 | convolution fusion | flops 51543801856 | bytes 33554432 | tf_op jit(solution)/shard_map/mdxq,cpdq->mcxp/dot_general | solution.py:142
  395.7 10.3 %fusion.26 = bf16[32,2,32,1024]{3,2,0,1:T(8,128)(2,1)} fusion(f32[2,1024,32,32,1]{1,3,4,0,2:T(8,128)} %fusion.8, f32[1,32,2,32]{1,3,0,2:T(8,128)S(1)} %get-tuple-element.36, f32[1,32,2,32]{1,3,0,2:T(8,128)S(1)} %get-tuple-element.35), kind=kOutput, calls=%fused_computation.54 | convolution fusion | flops 1612713984 | bytes 12599296 | tf_op jit(solution)/shard_map/mdwr,cxdw->mcxr/dot_general | solution.py:143
  406.0 26.3 %copy.92 = bf16[32,2,32,1024]{0,1,3,2:T(2,128)(2,1)} copy(bf16[32,2,32,1024]{3,2,0,1:T(8,128)(2,1)} %fusion.26) | data formatting | bytes 8388608 | tf_op jit(solution)/shard_map/convert_element_type | solution.py:146
  432.4 20.7 %reshape.1027 = bf16[16,2,65536]{2,1,0:T(2,128)(2,1)} reshape(bf16[32768,1,2,32]{3,2,1,0:T(2,128)(2,1)} %bitcast.203) | data formatting | bytes 8388608
  453.1 6.3 all-to-all-start.1
  460.8 82.9 %all-gather.1 = f32[16,48,3]{1,2,0:T(4,128)S(1)} all-gather(f32[1,48,3]{1,2,0:T(4,128)S(1)} %bitcast.220), channel_id=2, replica_groups=mesh['rep'=2,'ga'=16] {'ga'}, dimensions={0}, use_global_device_ids=true | all-gather | bytes 9792 | tf_op jit(solution)/shard_map/all_gather | solution.py:77
  544.0 6.6 copy.96
  550.8 9.9 %cosine_multiply_fusion = (f32[256,2048]{1,0:T(8,128)}, f32[256,2048]{1,0:T(8,128)S(1)}) fusion(f32[2048]{0:T(1024)S(1)} %get-tuple-element.41, f32[3,256]{1,0:T(4,128)S(1)} %slice.68, f32[1,2048]{1,0:T(1,128)S(1)} %fusion.86, f32[1,2048]{1,0:T(1,128)S(1)} %get-tuple-element.50, f32[1,2048]{1,0:T(1,128)S(1)} %get-tuple-element.49), kind=kOutput, calls=%fused_computation.84 | convolution fusion | flops 19410944 | bytes 4230144 | tf_op jit(solution)/shard_map/ai,ag->ig/dot_general | solution.py:96
  560.7 7.6 fusion.116
  583.5 21.5 %maximum_maximum_fusion.1 = bf16[1024,4096]{1,0:T(8,128)(2,1)} fusion(bf16[512,2048]{1,0:T(8,128)(2,1)S(1)} %get-tuple-element.19, bf16[512,2048]{1,0:T(8,128)(2,1)S(1)} %get-tuple-element.18, bf16[512,4096]{1,0:T(8,128)(2,1)S(1)} %bitcast.209), kind=kLoop, calls=%fused_computation.26 | loop fusion | flops 25165824 | bytes 16777216 | tf_op jit(solution)/shard_map/concatenate | solution.py:109
  610.2 44.3 %reduce-scatter.5.cloned.1.call-done = f32[2,16,512]{2,1,0:T(8,128)} async-done(((f32[2,256,512]{2,1,0:T(8,128)}), f32[2,16,512]{2,1,0:T(8,128)}) %reduce-scatter.5.cloned.1.call-update) | async-done | bytes 65552 | tf_op jit(solution)/shard_map/reduce_scatter | solution.py:106
  655.5 20.8 %all_gather.7 = bf16[2,256,512]{2,1,0:T(8,128)(2,1)S(1)} all-gather(bf16[2,16,512]{2,1,0:T(8,128)(2,1)S(1)} %convert_element_type.163), channel_id=1, replica_groups=mesh['rep'=2,'ga'=16] {'ga'}, dimensions={1}, use_global_device_ids=true | all-gather | bytes 557056 | tf_op jit(solution)/shard_map/all_gather | solution.py:113
  684.9 7.9 convolution_bitcast_fusion
  692.8 16.1 %reshape.1028 = bf16[32768,1,2,32]{3,2,1,0:T(2,128)(2,1)} reshape(bf16[16,2,65536]{2,1,0:T(2,128)(2,1)} %all-to-all-done.1) | data formatting | bytes 8388608
  708.9 38.1 %copy.63 = bf16[1,32,2,16,2048]{4,1,3,2,0:T(8,128)(2,1)} copy(bf16[1,32,2,16,2048]{1,2,4,3,0:T(2,128)(2,1)} %bitcast.204) | data formatting | bytes 8388608 | tf_op jit(solution)/shard_map/all_to_all | solution.py:145
  746.9 59.1 %fusion.20 = f32[512,2,2048]{2,0,1:T(8,128)S(1)} fusion(bf16[512,2,2048,1]{2,0,3,1:T(8,128)(2,1)} %bitcast.216, f32[1,2048,2,2048]{3,1,0,2:T(8,128)} %get-tuple-element.17, f32[1,2048,2,2048]{3,1,0,2:T(8,128)} %get-tuple-element.16), kind=kOutput, calls=%fused_computation.50 | convolution fusion | flops 103095992320 | bytes 79691776 | tf_op jit(solution)/shard_map/bdq,cpdq->bcp/dot_general | solution.py:149
  810.6 6.5 fusion.35
  817.2 5.9 broadcast_multiply_fusion
  826.2 92.0 %all-reduce.4.cloned.1.call-done = f32[512,1024]{1,0:T(8,128)} async-done(((f32[512,1024]{1,0:T(8,128)}), f32[512,1024]{1,0:T(8,128)}) %all-reduce.4.cloned.1.call-update) | async-done | bytes 2097168 | tf_op jit(solution)/shard_map/psum | solution.py:166
  918.2 22.2 %convolution_convert_fusion = bf16[512,4096]{1,0:T(8,128)(2,1)} fusion(bf16[512,2048]{1,0:T(8,128)(2,1)S(1)} %fusion.35, bf16[512,2048]{1,0:T(8,128)(2,1)} %copy-done.4, bf16[512,2048]{1,0:T(8,128)(2,1)} %copy-done.5, f32[512,1024]{1,0:T(8,128)} %all-reduce.4.cloned.1.call-done, pred[512,512]{1,0:T(32,128)(4,1)S(1)} %iota_compare_fusion), kind=kOutput, calls=%fused_computation.45 | convolution fusion | flops 4332716032 | bytes 12845056 | tf_op jit(solution)/shard_map/dot_general | solution.py:171
  940.5 7.8 stack_reshape.4
  (85 shorter events, 40.1 us)
Async XLA Ops:
  7.2 13.8 %copy-start.7 = (f32[1,32768]{1,0:T(1,128)S(1)}, f32[1,32768]{1,0:T(1,128)}, u32[]{:S(2)}) copy-start(f32[1,32768]{1,0:T(1,128)} %param.7) | copy-start | bytes 393220
  13.3 141.7 %all-to-all-start = ((bf16[16,32,2,2048]{3,1,2,0:T(8,128)(2,1)}), bf16[16,32,2,2048]{3,1,2,0:T(8,128)(2,1)}, u32[]{:S(2)}, u32[]{:S(2)}) async-start(bf16[16,32,2,2048]{3,1,2,0:T(8,128)(2,1)} %copy.56), calls=%async_computation | async-start | bytes 8388608 | tf_op jit(solution)/shard_map/all_to_all | solution.py:132
  232.2 90.8 %slice-start = ((s8[8388608]{0:T(1024)(128)(4,1)}), s8[4194304]{0:T(1024)(128)(4,1)S(1)}, s32[]{:S(2)}) async-start(s8[8388608]{0:T(1024)(128)(4,1)} %bitcast.212), calls=%async_computation.7 | async-start | bytes 8388608
  232.2 90.8 %slice-start.2 = ((s8[8388608]{0:T(1024)(128)(4,1)}), s8[4194304]{0:T(1024)(128)(4,1)S(1)}, s32[]{:S(2)}) async-start(s8[8388608]{0:T(1024)(128)(4,1)} %bitcast.214), calls=%async_computation.9 | async-start | bytes 8388608
  244.0 78.9 %slice-start.1 = ((s8[8388608]{0:T(1024)(128)(4,1)}), s8[4194304]{0:T(1024)(128)(4,1)S(1)}, s32[]{:S(2)}) async-start(s8[8388608]{0:T(1024)(128)(4,1)} %bitcast.212), calls=%async_computation.8 | async-start | bytes 8388608
  244.0 78.9 %slice-start.3 = ((s8[8388608]{0:T(1024)(128)(4,1)}), s8[4194304]{0:T(1024)(128)(4,1)S(1)}, s32[]{:S(2)}) async-start(s8[8388608]{0:T(1024)(128)(4,1)} %bitcast.214), calls=%async_computation.10 | async-start | bytes 8388608
  453.1 6.3 copy-start.8
  453.1 7.0 copy-start.6
  453.1 239.7 %all-to-all-start.1 = ((bf16[16,2,65536]{2,1,0:T(2,128)(2,1)}), bf16[16,2,65536]{2,1,0:T(2,128)(2,1)}, u32[]{:S(2)}, u32[]{:S(2)}) async-start(bf16[16,2,65536]{2,1,0:T(2,128)(2,1)} %reshape.1027), calls=%async_computation.1 | async-start | bytes 8388608 | tf_op jit(solution)/shard_map/all_to_all | solution.py:145
  459.4 195.1 %reduce-scatter.5.cloned.1.call-start = ((), (), s32[]{:S(2)}) async-start(), calls=%async_computation.4 | async-start | bytes 1114112 | tf_op jit(solution)/shard_map/reduce_scatter | solution.py:106
  560.7 12.8 %copy-start.1 = (bf16[64,8,2,2048]{3,1,2,0:T(8,128)(2,1)S(1)}, bf16[64,8,2,2048]{3,1,2,0:T(8,128)(2,1)}, u32[]{:S(2)}) copy-start(bf16[64,8,2,2048]{3,1,2,0:T(8,128)(2,1)} %copy.96) | copy-start | bytes 12582916
  579.1 245.3 %reduce-scatter.7.cloned.1.call-start = ((), (), s32[]{:S(2)}) async-start(), calls=%async_computation.6 | async-start | bytes 139264
  580.0 3.5 copy-start.2
  583.5 21.5 %copy-start = (bf16[1,512,2,2048]{3,2,1,0:T(2,128)(2,1)S(1)}, bf16[1,512,2,2048]{3,2,1,0:T(2,128)(2,1)}, u32[]{:S(2)}) copy-start(bf16[1,512,2,2048]{3,2,1,0:T(2,128)(2,1)} %param.6) | copy-start | bytes 12582916
  654.5 27.5 %copy-start.3 = (f32[256,2048]{1,0:T(8,128)S(1)}, f32[256,2048]{1,0:T(8,128)}, u32[]{:S(2)}) copy-start(f32[256,2048]{1,0:T(8,128)} %get-tuple-element.45) | copy-start | bytes 6291460
  684.6 233.6 %all-reduce.4.cloned.1.call-start = ((), (), s32[]{:S(2)}) async-start(), calls=%async_computation.5 | async-start | bytes 4194304 | tf_op jit(solution)/shard_map/psum | solution.py:166
  810.6 6.6 copy-start.4
  810.6 6.6 copy-start.5
Sparse Core Ops, SparseCore 0:
  579.3 75.1 reduce-scatter.4
  684.8 52.3 reduce-scatter.6
  823.2 95.0 all-reduce.3
where the time goes:
time: 961 us; the launch traced here: 955 us
  matrix products  352 us (37%)
  other arithmetic  190 us (20%)
  local copies, waits for them, and re-layouts  144 us (15%)
  waiting for transfers between devices  136 us (14%)
  blocking collectives  104 us (11%)
  between operations  14.4 us (1%)
  starting transfers between devices  14.2 us (1%)
    psum x1, waiting for transfers between devices, per_device(): margin = lax.psum(inner(trial, rotated) * (1.0 / GVECS), 'ga')  92 us
    mul x2, other arithmetic, real_form(): sines = jnp.sin(angle) * same  88.3 us
    all_gather x1, blocking collectives, per_device(): everyone = lax.all_gather(centres, 'ga', axis=2, tiled=True)  82.9 us
    dot_general x1, matrix products, per_device(): jnp.einsum('mcxp,cpdq->mdxq', grid, y_table, precision=highest)  78.9 us
    dot_general x1, matrix products, per_device(): grid = jnp.einsum('mdxq,cpdq->mcxp', grid, y_table, precision=highest)  72.7 us
    dot_general x1, matrix products, per_device(): jnp.einsum('mckp,cpdq->mdkq', blocks_whole, z_table, precision=highest)  59.7 us
    dot_general x1, matrix products, per_device(): jnp.einsum('bdq,cpdq->bcp', returned, z_table, precision=highest)  59.1 us
    unnamed x35, local copies, waits for them, and re-layouts  46.7 us
  transfers between devices with their start and end apart: 5, of which 2 were waited for; matrix products, arithmetic and copies ran while one was open for 37% of the time, Pallas kernels for 0%

commit v1 on v0

v1 whole, which is shorter than its diff:
```python
import functools

import jax
import jax.numpy as jnp
import numpy as np
from jax import lax
from jax.experimental import pallas as pl
from jax.experimental.pallas import tpu as pltpu
from jax.sharding import PartitionSpec as P

BEADS = 32
CBEADS = 1
WATERS = 256
NGRID = 32
GVECS = 32768


box_length = 20.0
bond_stiff = 0.5
bond_rest = 1.8
spring_stiff = 2.0
width_square = 0.09
step_size = 0.02
nonlocal_strength = 250.0
occupation = 2.0
highest = lax.Precision.HIGHEST
bf16 = jnp.bfloat16
f32 = jnp.float32

PLANE = NGRID * NGRID
GROUP = 8
LANES = 256
VMEM_BYTES = 56 * 2**20


def frequency(index, count):
    signed = jnp.where(index < count // 2, index, index - count)
    return signed.astype(jnp.float32) * (2.0 * jnp.pi / box_length)


def field_forces(positions):
    oxygen = positions[:, :, 0::3]
    toward_one = positions[:, :, 1::3] - oxygen
    toward_two = positions[:, :, 2::3] - oxygen

    def stretch(offset):
        length = jnp.sqrt(jnp.sum(offset * offset, axis=1, keepdims=True))
        return -bond_stiff * (length - bond_rest) * offset / length

    pull_one = stretch(toward_one)
    pull_two = stretch(toward_two)
    bonds = jnp.stack([-(pull_one + pull_two), pull_one, pull_two], axis=3).reshape(positions.shape)
    springs = 2.0 * positions - jnp.roll(positions, 1, axis=0) - jnp.roll(positions, -1, axis=0)
    return bonds - spring_stiff * springs


def inner(left_mat, right_mat):
    return lax.dot_general(
        left_mat, right_mat, (((1,), (1,)), ((), ())), preferred_element_type=jnp.float32
    )


def matmul(left_mat, right_mat):
    return jnp.dot(left_mat, right_mat, preferred_element_type=jnp.float32)


def exchange(blocks):
    return lax.all_to_all(blocks, "ga", split_axis=0, concat_axis=0, tiled=True)


def transform_tables():
    index = np.arange(PLANE)
    first, second = index // NGRID, index % NGRID
    product = (first[:, None] * first[None, :] + second[:, None] * second[None, :]) % NGRID
    angle = product * (2.0 * np.pi / NGRID)
    line = np.arange(NGRID)
    x_angle = (line[:, None] * line[None, :] % NGRID) * (2.0 * np.pi / NGRID)
    cosine, sine = np.cos(x_angle), np.sin(x_angle)
    same = np.eye(GROUP)
    rows = 2 * NGRID * GROUP

    def spread(mixing, order):
        return np.einsum("xycd,bm->" + order, mixing, same).reshape(rows, rows)

    def mixed(rr, ri, ir, ii):
        return np.stack([np.stack([rr, ri], -1), np.stack([ir, ii], -1)], -2)

    on_cosine = spread(mixed(cosine, -sine, sine, cosine), "xcbymd")
    on_sine = spread(mixed(-sine, -cosine, cosine, -sine), "xcbymd")
    backward = np.concatenate([on_cosine, on_sine], 1)
    forward = spread(mixed(cosine, sine, -sine, cosine), "xcbydm")
    return [
        jnp.asarray(table.astype(np.float32), dtype=bf16)
        for table in (np.cos(angle), np.sin(angle), backward, forward)
    ]


def potential_kernel(
    wave_ref, cos_ref, sin_ref, back_ref, fore_ref, pot_ref, out_ref, rows, planes, turned
):
    parts, local_g = wave_ref.shape[0], wave_ref.shape[3]
    band_rows = 2 * GROUP
    all_rows = NGRID * band_rows
    piece = min(local_g, PLANE)
    for start in range(0, NGRID * PLANE, piece):
        owner, offset = start // local_g, start % local_g
        x, column = start // PLANE, start % PLANE
        block = wave_ref[owner, :, :, offset : offset + piece]
        rows[x * band_rows : (x + 1) * band_rows, column : column + piece] = block.reshape(
            band_rows, piece
        )

    @pl.loop(0, PLANE // LANES)
    def _(step):
        columns = pl.ds(pl.multiple_of(step * LANES, LANES), LANES)
        planes[:all_rows, columns] = matmul(rows[...], cos_ref[:, columns]).astype(bf16)
        planes[all_rows:, columns] = matmul(rows[...], sin_ref[:, columns]).astype(bf16)

    @pl.loop(0, PLANE // LANES)
    def _(step):
        columns = pl.ds(pl.multiple_of(step * LANES, LANES), LANES)
        space = matmul(back_ref[...], planes[:, columns]).reshape(NGRID, band_rows, LANES)
        space = space * pot_ref[:, columns][:, None, :]
        space = space.reshape(all_rows, LANES).astype(bf16)
        waves = matmul(fore_ref[...], space)
        turned[:, columns] = waves.astype(bf16)
        halves = waves.reshape(NGRID, 2, GROUP, LANES)
        other = jnp.concatenate([halves[:, 1:], -halves[:, :1]], 1).reshape(all_rows, LANES)
        rows[:, columns] = other.astype(bf16)

    @pl.loop(0, PLANE // LANES)
    def _(step):
        columns = pl.ds(pl.multiple_of(step * LANES, LANES), LANES)
        waves = matmul(turned[...], cos_ref[:, columns]) + matmul(rows[...], sin_ref[:, columns])
        planes[:all_rows, columns] = waves.astype(bf16)

    for start in range(0, NGRID * PLANE, piece):
        owner, offset = start // local_g, start % local_g
        x, column = start // PLANE, start % PLANE
        out_ref[owner, 0, :, offset : offset + piece] = planes[
            x * band_rows : (x + 1) * band_rows, column : column + piece
        ]


def apply_potential(waves, tables, grid_potential):
    parts, band_count, _, local_g = waves.shape
    steps = band_count // GROUP
    band_rows = 2 * GROUP
    all_rows = NGRID * band_rows
    whole = lambda step: (0, 0)
    return pl.pallas_call(
        potential_kernel,
        grid=(steps,),
        in_specs=[
            pl.BlockSpec((parts, GROUP, 2, local_g), lambda step: (0, step, 0, 0)),
            pl.BlockSpec((PLANE, PLANE), whole),
            pl.BlockSpec((PLANE, PLANE), whole),
            pl.BlockSpec((all_rows, 2 * all_rows), whole),
            pl.BlockSpec((all_rows, all_rows), whole),
            pl.BlockSpec((NGRID, PLANE), whole),
        ],
        out_specs=pl.BlockSpec((parts, 1, band_rows, local_g), lambda step: (0, step, 0, 0)),
        out_shape=jax.ShapeDtypeStruct((parts, steps, band_rows, local_g), bf16),
        scratch_shapes=[
            pltpu.VMEM((all_rows, PLANE), bf16),
            pltpu.VMEM((2 * all_rows, PLANE), bf16),
            pltpu.VMEM((all_rows, PLANE), bf16),
        ],
        compiler_params=pltpu.CompilerParams(vmem_limit_bytes=VMEM_BYTES),
        cost_estimate=pl.CostEstimate(
            flops=steps * 2 * all_rows * PLANE * (4 * PLANE + 3 * all_rows),
            bytes_accessed=8 * steps * band_rows * parts * local_g + 8 * PLANE * PLANE,
            transcendentals=0,
        ),
    )(waves, *tables, grid_potential)


def trial_kernel(count, base_ref, *refs):
    potentials, (trial_ref, margin_ref, even, odd) = refs[:count], refs[count:]
    step = pl.program_id(0)
    bands = base_ref.shape[1]
    share = bands // count

    for chunk in range(count):
        block = potentials[chunk][...].astype(f32) * step_size
        block = block.reshape(share // GROUP, 2, GROUP, block.shape[1])
        inside = slice(chunk * share, (chunk + 1) * share)
        for half in range(2):
            taken = block[:, half].reshape(share, block.shape[3])
            trial_ref[half, inside, :] = (base_ref[half, inside, :] - taken).astype(bf16)
    real, imag = trial_ref[0], trial_ref[1]

    @pl.when(step == 0)
    def _():
        even[...] = jnp.zeros_like(even)
        odd[...] = jnp.zeros_like(odd)

    even[...] += inner(real, real) + inner(imag, imag)
    odd[...] += inner(imag, real)

    @pl.when(step == pl.num_programs(0) - 1)
    def _():
        across = odd[...]
        row = lax.broadcasted_iota(jnp.int32, even.shape, 0)
        column = lax.broadcasted_iota(jnp.int32, even.shape, 1)
        packed = jnp.where(row <= column, even[...], across - across.T)
        margin_ref[...] = (packed * (1.0 / GVECS)).astype(bf16)


def make_trial(base, potentials):
    _, bands, local_g = base.shape
    count = len(potentials)
    width = min(LANES, local_g)
    return pl.pallas_call(
        functools.partial(trial_kernel, count),
        grid=(local_g // width,),
        in_specs=[pl.BlockSpec((2, bands, width), lambda step: (0, 0, step))]
        + [pl.BlockSpec((2 * bands // count, width), lambda step: (0, step))] * count,
        out_specs=[
            pl.BlockSpec((2, bands, width), lambda step: (0, 0, step)),
            pl.BlockSpec((bands, bands), lambda step: (0, 0)),
        ],
        out_shape=[
            jax.ShapeDtypeStruct((2, bands, local_g), bf16),
            jax.ShapeDtypeStruct((bands, bands), bf16),
        ],
        scratch_shapes=[pltpu.VMEM((bands, bands), f32)] * 2,
        compiler_params=pltpu.CompilerParams(vmem_limit_bytes=VMEM_BYTES),
        cost_estimate=pl.CostEstimate(
            flops=6 * bands * bands * local_g,
            bytes_accessed=16 * bands * local_g,
            transcendentals=0,
        ),
    )(base, *potentials)


def update_kernel(mixer_ref, trial_ref, out_ref, even, odd):
    @pl.when(pl.program_id(0) == 0)
    def _():
        packed = mixer_ref[...].astype(f32)
        flipped = packed.T
        row = lax.broadcasted_iota(jnp.int32, packed.shape, 0)
        column = lax.broadcasted_iota(jnp.int32, packed.shape, 1)
        even[...] = jnp.where(row <= column, packed, flipped).astype(bf16)
        above = jnp.where(row == column, 0.0, -flipped)
        odd[...] = jnp.where(row > column, packed, above).astype(bf16)

    real, imag = trial_ref[0], trial_ref[1]
    out_ref[:, 0, :] = (matmul(even[...], real) - matmul(odd[...], imag)).astype(bf16)
    out_ref[:, 1, :] = (matmul(even[...], imag) + matmul(odd[...], real)).astype(bf16)


def update_waves(mixer, trial):
    _, bands, local_g = trial.shape
    width = min(LANES, local_g)
    return pl.pallas_call(
        update_kernel,
        grid=(local_g // width,),
        in_specs=[
            pl.BlockSpec((bands, bands), lambda step: (0, 0)),
            pl.BlockSpec((2, bands, width), lambda step: (0, 0, step)),
        ],
        out_specs=pl.BlockSpec((bands, 2, width), lambda step: (0, 0, step)),
        out_shape=jax.ShapeDtypeStruct((bands, 2, local_g), bf16),
        scratch_shapes=[pltpu.VMEM((bands, bands), bf16)] * 2,
        compiler_params=pltpu.CompilerParams(vmem_limit_bytes=VMEM_BYTES),
        cost_estimate=pl.CostEstimate(
            flops=8 * bands * bands * local_g,
            bytes_accessed=8 * bands * local_g,
            transcendentals=0,
        ),
    )(mixer, trial)


def per_device(positions, weights, psi, vloc):
    parts = lax.axis_size("ga")
    bands = psi.shape[1]
    local_g = psi.shape[3]

    weight_float = weights.astype(jnp.float32)
    mixing = weight_float / jnp.sum(weight_float, axis=1, keepdims=True)
    own_oxygens = jnp.einsum("cj,jan->can", mixing, positions[:, :, 0::3], precision=highest)[0]
    everyone = exchange(jnp.broadcast_to(own_oxygens[None], (parts,) + own_oxygens.shape))
    oxygens = jnp.swapaxes(everyone, 0, 1).reshape(3, WATERS)

    count = 2 if bands // parts % (2 * GROUP) == 0 else 1
    share = bands // count
    tables = transform_tables()
    grid_potential = vloc[0].reshape(NGRID, PLANE) * (1.0 / GVECS)
    potentials = []
    for chunk in range(count):
        sent = psi[0, chunk * share : (chunk + 1) * share].reshape(
            parts, share // parts, 2, local_g
        )
        moved = apply_potential(exchange(sent), tables, grid_potential)
        potentials.append(exchange(moved).reshape(2 * share, local_g))

    flat_index = lax.axis_index("ga") * local_g + jnp.arange(local_g, dtype=jnp.int32)
    gvectors = jnp.stack(
        [
            frequency(flat_index // (NGRID * NGRID), NGRID),
            frequency(flat_index // NGRID % NGRID, NGRID),
            frequency(flat_index % NGRID, NGRID),
        ]
    )
    square = jnp.sum(gvectors * gvectors, axis=0)
    profile = jnp.exp(-0.5 * width_square * square)
    kinetic = 0.5 * square
    phases = jnp.einsum("ai,ag->ig", oxygens, gvectors, precision=highest)
    wave_cos = profile * jnp.cos(phases)
    wave_sin = profile * jnp.sin(phases)
    table = jnp.concatenate(
        [jnp.concatenate([wave_cos, -wave_sin], 1), jnp.concatenate([wave_sin, wave_cos], 1)], 0
    ).astype(bf16)
    planes = jnp.swapaxes(psi[0], 0, 1)
    real_part, imag_part = planes[0], planes[1]
    partial_proj = (
        inner(table[:, :local_g], real_part) + inner(table[:, local_g:], imag_part)
    ) * (1.0 / GVECS)
    all_proj = lax.psum(partial_proj, "ga").astype(bf16)
    nonlocal_term = lax.dot_general(
        all_proj, table, (((0,), (0,)), ((), ())), preferred_element_type=jnp.float32
    )
    proj_re, proj_im = all_proj[:WATERS], all_proj[WATERS:]
    weighted_re = matmul(proj_re, real_part) + matmul(proj_im, imag_part)
    weighted_im = matmul(proj_re, imag_part) - matmul(proj_im, real_part)
    mixed_wave = wave_cos * weighted_im + wave_sin * weighted_re
    force_part = (
        2.0
        * occupation
        * nonlocal_strength
        / GVECS
        * jnp.einsum("ag,ig->ai", gvectors, mixed_wave, precision=highest)
    )
    force_blocks = jnp.swapaxes(force_part.reshape(3, parts, WATERS // parts), 0, 1)
    oxygen_force = jnp.sum(exchange(force_blocks), axis=0)
    hydrogen_zero = jnp.zeros_like(oxygen_force)
    dft_force = jnp.stack([oxygen_force, hydrogen_zero, hydrogen_zero], axis=2).reshape(1, 3, -1)

    pulled = jnp.stack([nonlocal_term[:, :local_g], nonlocal_term[:, local_g:]])
    wave_float = planes.astype(jnp.float32)
    base = wave_float - step_size * (kinetic * wave_float + nonlocal_strength * pulled)

    trial, margin = make_trial(base, potentials)
    rows = bands // parts
    summed = jnp.sum(exchange(margin.reshape(parts, rows, bands)).astype(jnp.float32), axis=0)
    row = lax.axis_index("ga") * rows + lax.broadcasted_iota(jnp.int32, (rows, bands), 0)
    column = lax.broadcasted_iota(jnp.int32, (rows, bands), 1)
    own_mixer = (jnp.where(row == column, 1.5, 0.0) - 0.5 * summed).astype(bf16)
    mixer = lax.all_gather(own_mixer, "ga", axis=0, tiled=True)
    psi_new = update_waves(mixer, trial)

    near_forces = field_forces(positions)
    contracted_force = jnp.einsum("cj,can->jan", mixing, dft_force, precision=highest)
    bead_forces = near_forces + BEADS / CBEADS * contracted_force
    return (psi_new[None], bead_forces)


def solution(mesh):
    placed = (P("rep", None, "ga"), P(), P("rep", None, None, "ga"), P("rep", None))
    return jax.shard_map(
        per_device,
        mesh=mesh,
        in_specs=placed,
        out_specs=(P("rep", None, None, "ga"), P("rep", None, "ga")),
        check_vma=False,
    )
```

time: 961 us -> 401 us (0.42)
  matrix products: 352 us -> 42.2 us
  other arithmetic: 190 us -> 27.8 us
  local copies, waits for them, and re-layouts: 144 us -> 19.9 us
  waiting for transfers between devices: 136 us -> 38.2 us
  Pallas kernels: 0 us -> 70.3 us
  blocking collectives: 104 us -> 149 us
  starting transfers between devices: 14.2 us -> 45.8 us
  between operations: 14.4 us -> 1.22 us
    dot_general x10 -> x6, matrix products: 329 us -> 27.7 us  [the longest x4 21.7 us: matmul(): return jnp.dot(left_mat, right_mat, preferred_element_type=jnp.float32)]
    psum x1 -> x0, waiting for transfers between devices: 92 us -> none  [per_device(): margin = lax.psum(inner(trial, rotated) * (1.0 / GVECS), 'ga')]
    mul x3 -> x1, other arithmetic: 88.6 us -> 0.36 us  [per_device(): grid_potential = vloc[0].reshape(NGRID, PLANE) * (1.0 / GVECS)]
    all_gather x2 -> x1, blocking collectives: 104 us -> 22.7 us  [per_device(): mixer = lax.all_gather(own_mixer, 'ga', axis=0, tiled=True)]
    psum x0 -> x1, blocking collectives: none -> 74.1 us  [per_device(): all_proj = lax.psum(partial_proj, 'ga').astype(bf16)]
    pallas_call x0 -> x4, Pallas kernels: none -> 70.3 us  [the longest x2 46.4 us: apply_potential(): pl.pallas_call(potential_kernel, grid=(steps,), in_specs=[pl.BlockSpec((p...]
    all_to_all x0 -> x1, blocking collectives: none -> 52.2 us  [exchange(): return lax.all_to_all(blocks, 'ga', split_axis=0, concat_axis=0, tiled=True)]
    another operation x4 -> x1, other arithmetic: 45.8 us -> 0.62 us  [the longest x3 45.1 us: real_form(): jnp.stack([jnp.stack([cosines, sines], 1), jnp.stack([-sines, cosines], 1...]
  transfers between devices with their start and end apart: 5 -> 6, of which waited for: 2 -> 4; matrix products, arithmetic and copies ran while one was open for 37% -> 21% of each run, Pallas kernels for 0% -> 15%
where the time goes in v1:
time: 401 us; the launch traced here: 394 us
  blocking collectives  149 us (37%)
  Pallas kernels  70.3 us (18%)
  starting transfers between devices  45.8 us (11%)
  matrix products  42.2 us (11%)
  waiting for transfers between devices  38.2 us (10%)
  other arithmetic  27.8 us (7%)
  local copies, waits for them, and re-layouts  19.9 us (5%)
    psum x1, blocking collectives, per_device(): all_proj = lax.psum(partial_proj, 'ga').astype(bf16)  74.1 us
    all_to_all x1, blocking collectives, exchange(): return lax.all_to_all(blocks, 'ga', split_axis=0, concat_axis=0, tiled=True)  52.2 us
    pallas_call x2, Pallas kernels, apply_potential(): pl.pallas_call(potential_kernel, grid=(steps,), in_specs=[pl.BlockSpec((p...  46.4 us
    all_to_all x6, starting transfers between devices, exchange(): return lax.all_to_all(blocks, 'ga', split_axis=0, concat_axis=0, tiled=True)  45.8 us
    all_to_all x6, waiting for transfers between devices, exchange(): return lax.all_to_all(blocks, 'ga', split_axis=0, concat_axis=0, tiled=True)  38.2 us
    all_gather x1, blocking collectives, per_device(): mixer = lax.all_gather(own_mixer, 'ga', axis=0, tiled=True)  22.7 us
    dot_general x4, matrix products, matmul(): return jnp.dot(left_mat, right_mat, preferred_element_type=jnp.float32)  21.7 us
    concatenate x1, other arithmetic, per_device(): jnp.concatenate([jnp.concatenate([wave_cos, -wave_sin], 1), jnp.concatena...  19.7 us
  transfers between devices with their start and end apart: 6, of which 4 were waited for; matrix products, arithmetic and copies ran while one was open for 21% of the time, Pallas kernels for 15%

profile of v1, /device:TPU:0, one launch (start us, length us, event | category | flops | bytes accessed | tf_op | source)
XLA Modules:
  0.0 394.4 jit_solution(5975035824900652396)
XLA Ops:
  1.7 1.3 convert_reduce_fusion.1
  3.0 1.4 fusion.39
  5.1 7.4 %all-to-all-start = ((f32[16,3,16]{2,1,0:T(4,128)}), f32[16,3,16]{2,1,0:T(4,128)S(1)}, u32[]{:S(2)}, u32[]{:S(2)}) async-start(f32[16,3,16]{2,1,0:T(4,128)} %broadcast_in_dim.24), calls=%async_computation | async-start | bytes 65536 | tf_op jit(solution)/shard_map/all_to_all | solution.py:68
  12.5 5.7 %fusion.45 = (bf16[1,256,2,2048]{3,2,1,0:T(2,128)(2,1)}, bf16[1,256,2,2048]{3,2,1,0:T(2,128)(2,1)S(1)}) fusion(bf16[1,512,2,2048]{3,2,1,0:T(2,128)(2,1)} %param.10), kind=kLoop, calls=%fused_computation.93 | loop fusion | bytes 8388608 | tf_op jit(solution)/shard_map/slice | solution.py:292
  19.1 52.2 %all_to_all.35.wave_ref = bf16[16,16,2,2048]{3,2,1,0:T(2,128)(2,1)} all-to-all(bf16[16,16,2,2048]{3,2,1,0:T(2,128)(2,1)S(1)} %bitcast.63), channel_id=1, replica_groups=mesh['rep'=2,'ga'=16] {'ga'}, dimensions={0} | all-to-all | bytes 4194304 | tf_op jit(solution)/shard_map/all_to_all | solution.py:68
  71.3 5.1 %all-to-all-start.3 = ((bf16[16,16,2,2048]{3,2,1,0:T(2,128)(2,1)}), bf16[16,16,2,2048]{3,2,1,0:T(2,128)(2,1)S(1)}, u32[]{:S(2)}, u32[]{:S(2)}) async-start(bf16[16,16,2,2048]{3,2,1,0:T(2,128)(2,1)} %bitcast.13), calls=%async_computation.3 | async-start | bytes 4194304 | tf_op jit(solution)/shard_map/all_to_all | solution.py:68
  76.5 6.1 %copy.50 = bf16[1,512,2,2048]{3,1,2,0:T(8,128)(2,1)} copy(bf16[1,512,2,2048]{3,2,1,0:T(2,128)(2,1)} %param.10) | data formatting | bytes 8388608 | tf_op args[2]
  84.9 23.2 %shard_map.95 = bf16[16,2,16,2048]{3,2,1,0:T(8,128)(2,1)} custom-call(bf16[16,16,2,2048]{3,2,1,0:T(2,128)(2,1)} %all_to_all.35.wave_ref, bf16[1024,1024]{1,0:T(8,128)(2,1)} %constant.96.clone.cos_ref, bf16[1024,1024]{1,0:T(8,128)(2,1)} %constant.97.clone.sin_ref, bf16[512,1024]{1,0:T(8,128)(2,1)} %constant.98.clone.back_ref, ...), custom_call_target="tpu_custom_call" | custom-call | flops 11811160064 | bytes 16777216 | tf_op jit(solution)/shard_map/pallas_call | solution.py:151
  108.1 9.4 %all-to-all-done.3.wave_ref = bf16[16,16,2,2048]{3,2,1,0:T(2,128)(2,1)S(1)} async-done(((bf16[16,16,2,2048]{3,2,1,0:T(2,128)(2,1)}), bf16[16,16,2,2048]{3,2,1,0:T(2,128)(2,1)S(1)}, u32[]{:S(2)}, u32[]{:S(2)}) %all-to-all-start.3) | async-done | bytes 2097184 | tf_op jit(solution)/shard_map/all_to_all | solution.py:68
  117.6 11.5 %all-to-all-start.2 = ((bf16[16,2,16,2048]{3,2,1,0:T(8,128)(2,1)}), bf16[16,2,16,2048]{3,2,1,0:T(8,128)(2,1)}, u32[]{:S(2)}, u32[]{:S(2)}) async-start(bf16[16,2,16,2048]{3,2,1,0:T(8,128)(2,1)} %shard_map.95), calls=%async_computation.2 | async-start | bytes 4194304 | tf_op jit(solution)/shard_map/all_to_all | solution.py:68
  129.0 9.2 %negate_convert_fusion = (bf16[256,2048]{1,0:T(8,128)(2,1)S(1)}, bf16[256,2048]{1,0:T(8,128)(2,1)S(1)}, bf16[256,2048]{1,0:T(8,128)(2,1)S(1)}, f32[256,2048]{1,0:T(8,128)S(1)}) fusion(f32[2048]{0:T(1024)S(1)} %get-tuple-element.37, f32[3,256]{1,0:T(4,128)S(1)} %reshape.249, f32[1,2048]{1,0:T(1,128)S(1)} %fusion.33, f32[1,2048]{1,0:T(1,128)S(1)} %get-tuple-element.42, ...), kind=kOutput, calls=%fused_computation.20 | convolution fusion | flops 22032384 | bytes 5278720 | tf_op jit(solution)/shard_map/ai,ag->ig/dot_general | solution.py:309
  138.3 19.7 %maximum_maximum_fusion = bf16[512,4096]{1,0:T(8,128)(2,1)S(1)} fusion(bf16[256,2048]{1,0:T(8,128)(2,1)S(1)} %get-tuple-element.22, bf16[256,2048]{1,0:T(8,128)(2,1)S(1)} %get-tuple-element.21, bf16[256,2048]{1,0:T(8,128)(2,1)S(1)} %get-tuple-element.20), kind=kLoop, calls=%fused_computation.7 | loop fusion | flops 16777216 | bytes 7340032 | tf_op jit(solution)/shard_map/concatenate | solution.py:312
  158.1 1.3 fusion.5
  159.4 2.3 fusion.16
  161.7 74.1 %all-reduce.2 = bf16[512,512]{1,0:T(8,128)(2,1)S(1)} all-reduce(f32[512,512]{1,0:T(8,128)} %fusion.16), channel_id=1, replica_groups=mesh['rep'=2,'ga'=16] {'ga'}, use_global_device_ids=true, to_apply=%region_2.3 | all-reduce | flops 262144 | bytes 1572864 | tf_op jit(solution)/shard_map/psum | solution.py:320
  235.8 2.4 fusion.11
  238.6 8.2 %fusion.2 = f32[256,2048]{1,0:T(8,128)} fusion(f32[256,2048]{1,0:T(8,128)S(1)} %fusion.11, f32[256,2048]{1,0:T(8,128)S(1)} %get-tuple-element.38, bf16[2,512,2048]{2,1,0:T(8,128)(2,1)S(1)} %bitcast.61, f32[2048]{0:T(1024)S(1)} %get-tuple-element.37, bf16[512,512]{1,0:T(8,128)(2,1)S(1)} %all-reduce.2), kind=kOutput, calls=%fused_computation.10 | convolution fusion | flops 538443776 | bytes 8658944 | tf_op jit(solution)/shard_map/dot_general | solution.py:64
  246.8 23.2 %shard_map.96 = bf16[16,2,16,2048]{3,2,1,0:T(8,128)(2,1)} custom-call(bf16[16,16,2,2048]{3,2,1,0:T(2,128)(2,1)} %copy-done.7, bf16[1024,1024]{1,0:T(8,128)(2,1)} %constant.96.clone.cos_ref, bf16[1024,1024]{1,0:T(8,128)(2,1)} %constant.97.clone.sin_ref, bf16[512,1024]{1,0:T(8,128)(2,1)} %constant.98.clone.back_ref, bf16[512,512]{1,0:T(8,128)(2,1)} %constant.99.clone.fore_ref, ...), custom_call_target="tpu_custom_call" | custom-call | flops 11811160064 | bytes 16777216 | tf_op jit(solution)/shard_map/pallas_call | solution.py:151
  270.1 4.6 %all-to-all-start.4 = ((bf16[16,2,16,2048]{3,2,1,0:T(8,128)(2,1)}), bf16[16,2,16,2048]{3,2,1,0:T(8,128)(2,1)}, u32[]{:S(2)}, u32[]{:S(2)}) async-start(bf16[16,2,16,2048]{3,2,1,0:T(8,128)(2,1)} %shard_map.96), calls=%async_computation.4 | async-start | bytes 4194304 | tf_op jit(solution)/shard_map/all_to_all | solution.py:68
  274.7 2.4 fusion.12
  277.5 8.5 %fusion.4 = f32[256,2048]{1,0:T(8,128)S(1)} fusion(f32[256,2048]{1,0:T(8,128)} %fusion.2, f32[256,2048]{1,0:T(8,128)S(1)} %fusion.12, f32[256,2048]{1,0:T(8,128)S(1)} %get-tuple-element.38, bf16[2,512,2048]{2,1,0:T(8,128)(2,1)S(1)} %bitcast.62, f32[2048]{0:T(1024)S(1)} %get-tuple-element.37, bf16[512,512]{1,0:T(8,128)(2,1)S(1)} %all-reduce.2), kind=kOutput, calls=%fused_computation.13 | convolution fusion | flops 538968064 | bytes 10756096 | tf_op jit(solution)/shard_map/dot_general | solution.py:64
  286.1 1.7 convolution_multiply_fusion
  288.5 4.6 %fusion.44 = f32[512,4096]{1,0:T(8,128)S(1)} fusion(bf16[512,512]{1,0:T(8,128)(2,1)S(1)} %all-reduce.2, bf16[256,2048]{1,0:T(8,128)(2,1)} %copy-done.6, bf16[256,2048]{1,0:T(8,128)(2,1)} %copy-done.5, bf16[256,2048]{1,0:T(8,128)(2,1)} %copy-done.4), kind=kOutput, calls=%fused_computation.92 | convolution fusion | flops 2164260864 | bytes 12058624 | tf_op jit(solution)/shard_map/dot_general | solution.py:321
  293.2 1.1 slice_bitcast_fusion.1
  295.3 5.1 %convert_subtract_fusion.base_ref = f32[2,512,2048]{2,1,0:T(8,128)} fusion(f32[1,512,2048]{2,1,0:T(8,128)S(1)} %get-tuple-element.17, f32[1,512,2048]{2,1,0:T(8,128)S(1)} %get-tuple-element.16, f32[2048]{0:T(1024)S(1)} %get-tuple-element.36, bf16[1,512,2,2048]{3,2,1,0:T(2,128)(2,1)S(1)} %copy-done), kind=kLoop, calls=%fused_computation | loop fusion | flops 14680064 | bytes 20979712 | tf_op jit(solution)/shard_map/sub | solution.py:342
  300.4 15.3 %all-to-all-done.4 = bf16[16,2,16,2048]{3,2,1,0:T(8,128)(2,1)} async-done(((bf16[16,2,16,2048]{3,2,1,0:T(8,128)(2,1)}), bf16[16,2,16,2048]{3,2,1,0:T(8,128)(2,1)}, u32[]{:S(2)}, u32[]{:S(2)}) %all-to-all-start.4) | async-done | bytes 2097184 | tf_op jit(solution)/shard_map/all_to_all | solution.py:68
  315.8 11.2 %all-to-all-start.6 = ((f32[16,3,16]{2,1,0:T(4,128)}), f32[16,3,16]{2,1,0:T(4,128)S(1)}, u32[]{:S(2)}, u32[]{:S(2)}) async-start(f32[16,3,16]{2,1,0:T(4,128)} %bitcast.55), calls=%async_computation.6 | async-start | bytes 65536 | tf_op jit(solution)/shard_map/all_to_all | solution.py:68
  327.0 11.8 %shard_map.97 = (bf16[2,512,2048]{2,1,0:T(8,128)(2,1)}, bf16[512,512]{1,0:T(8,128)(2,1)}) custom-call(f32[2,512,2048]{2,1,0:T(8,128)} %convert_subtract_fusion.base_ref, bf16[512,2048]{1,0:T(8,128)(2,1)} %bitcast.12.refs_0_, bf16[512,2048]{1,0:T(8,128)(2,1)} %bitcast.14.refs_1_), custom_call_target="tpu_custom_call" | custom-call | flops 3221225472 | bytes 16777216 | tf_op jit(solution)/shard_map/pallas_call | solution.py:214
  338.8 6.0 %all-to-all-start.5 = ((bf16[16,32,512]{2,1,0:T(8,128)(2,1)}), bf16[16,32,512]{2,1,0:T(8,128)(2,1)S(1)}, u32[]{:S(2)}, u32[]{:S(2)}) async-start(bf16[16,32,512]{2,1,0:T(8,128)(2,1)} %bitcast.64), calls=%async_computation.5 | async-start | bytes 1048576 | tf_op jit(solution)/shard_map/all_to_all | solution.py:68
  346.9 12.4 %all-to-all-done.5 = bf16[16,32,512]{2,1,0:T(8,128)(2,1)S(1)} async-done(((bf16[16,32,512]{2,1,0:T(8,128)(2,1)}), bf16[16,32,512]{2,1,0:T(8,128)(2,1)S(1)}, u32[]{:S(2)}, u32[]{:S(2)}) %all-to-all-start.5) | async-done | bytes 524320 | tf_op jit(solution)/shard_map/all_to_all | solution.py:68
  359.5 22.7 %all_gather.3.mixer_ref = bf16[512,512]{1,0:T(8,128)(2,1)} all-gather(bf16[32,512]{1,0:T(8,128)(2,1)S(1)} %subtract_convert_fusion), channel_id=1, replica_groups=mesh['rep'=2,'ga'=16] {'ga'}, dimensions={0}, use_global_device_ids=true | all-gather | bytes 557056 | tf_op jit(solution)/shard_map/all_gather | solution.py:350
  382.2 12.0 %shard_map.98 = bf16[512,2,2048]{2,1,0:T(2,128)(2,1)} custom-call(bf16[512,512]{1,0:T(8,128)(2,1)} %all_gather.3.mixer_ref, bf16[2,512,2048]{2,1,0:T(8,128)(2,1)} %get-tuple-element.5.trial_ref), custom_call_target="tpu_custom_call" | custom-call | flops 4294967296 | bytes 8388608 | tf_op jit(solution)/shard_map/pallas_call | solution.py:256
  (61 shorter events, 9.6 us)
Async XLA Ops:
  5.1 14.0 %all-to-all-start = ((f32[16,3,16]{2,1,0:T(4,128)}), f32[16,3,16]{2,1,0:T(4,128)S(1)}, u32[]{:S(2)}, u32[]{:S(2)}) async-start(f32[16,3,16]{2,1,0:T(4,128)} %broadcast_in_dim.24), calls=%async_computation | async-start | bytes 65536 | tf_op jit(solution)/shard_map/all_to_all | solution.py:68
  71.3 46.2 %all-to-all-start.3 = ((bf16[16,16,2,2048]{3,2,1,0:T(2,128)(2,1)}), bf16[16,16,2,2048]{3,2,1,0:T(2,128)(2,1)S(1)}, u32[]{:S(2)}, u32[]{:S(2)}) async-start(bf16[16,16,2,2048]{3,2,1,0:T(2,128)(2,1)} %bitcast.13), calls=%async_computation.3 | async-start | bytes 4194304 | tf_op jit(solution)/shard_map/all_to_all | solution.py:68
  76.5 6.1 %copy-start.8 = (f32[32,3,48]{2,0,1:T(8,128)S(1)}, f32[32,3,48]{2,0,1:T(8,128)}, u32[]{:S(2)}) copy-start(f32[32,3,48]{2,0,1:T(8,128)} %param.8) | copy-start | bytes 55300
  76.5 7.0 %copy-start.9 = (f32[1,32768]{1,0:T(1,128)S(1)}, f32[1,32768]{1,0:T(1,128)}, u32[]{:S(2)}) copy-start(f32[1,32768]{1,0:T(1,128)} %param.11) | copy-start | bytes 393220
  117.6 11.5 %copy-start.7 = (bf16[16,16,2,2048]{3,2,1,0:T(2,128)(2,1)}, bf16[16,16,2,2048]{3,2,1,0:T(2,128)(2,1)S(1)}, u32[]{:S(2)}) copy-start(bf16[16,16,2,2048]{3,2,1,0:T(2,128)(2,1)S(1)} %all-to-all-done.3.wave_ref) | copy-start | bytes 6291460
  117.6 152.5 %all-to-all-start.2 = ((bf16[16,2,16,2048]{3,2,1,0:T(8,128)(2,1)}), bf16[16,2,16,2048]{3,2,1,0:T(8,128)(2,1)}, u32[]{:S(2)}, u32[]{:S(2)}) async-start(bf16[16,2,16,2048]{3,2,1,0:T(8,128)(2,1)} %shard_map.95), calls=%async_computation.2 | async-start | bytes 4194304 | tf_op jit(solution)/shard_map/all_to_all | solution.py:68
  138.3 21.1 %copy-start.4 = (bf16[256,2048]{1,0:T(8,128)(2,1)}, bf16[256,2048]{1,0:T(8,128)(2,1)S(1)}, u32[]{:S(2)}) copy-start(bf16[256,2048]{1,0:T(8,128)(2,1)S(1)} %get-tuple-element.20) | copy-start | bytes 3145732
  138.3 21.1 %copy-start.5 = (bf16[256,2048]{1,0:T(8,128)(2,1)}, bf16[256,2048]{1,0:T(8,128)(2,1)S(1)}, u32[]{:S(2)}) copy-start(bf16[256,2048]{1,0:T(8,128)(2,1)S(1)} %get-tuple-element.21) | copy-start | bytes 3145732
  138.3 21.1 %copy-start.6 = (bf16[256,2048]{1,0:T(8,128)(2,1)}, bf16[256,2048]{1,0:T(8,128)(2,1)S(1)}, u32[]{:S(2)}) copy-start(bf16[256,2048]{1,0:T(8,128)(2,1)S(1)} %get-tuple-element.22) | copy-start | bytes 3145732
  138.3 19.7 %copy-start.1 = (bf16[1,512,2,2048]{3,1,2,0:T(8,128)(2,1)S(1)}, bf16[1,512,2,2048]{3,1,2,0:T(8,128)(2,1)}, u32[]{:S(2)}) copy-start(bf16[1,512,2,2048]{3,1,2,0:T(8,128)(2,1)} %copy.50) | copy-start | bytes 12582916
  235.8 2.8 copy-start.2
  270.1 45.7 %all-to-all-start.4 = ((bf16[16,2,16,2048]{3,2,1,0:T(8,128)(2,1)}), bf16[16,2,16,2048]{3,2,1,0:T(8,128)(2,1)}, u32[]{:S(2)}, u32[]{:S(2)}) async-start(bf16[16,2,16,2048]{3,2,1,0:T(8,128)(2,1)} %shard_map.96), calls=%async_computation.4 | async-start | bytes 4194304 | tf_op jit(solution)/shard_map/all_to_all | solution.py:68
  274.7 2.8 copy-start.3
  293.1 2.2 copy-start
  315.8 23.0 %all-to-all-start.6 = ((f32[16,3,16]{2,1,0:T(4,128)}), f32[16,3,16]{2,1,0:T(4,128)S(1)}, u32[]{:S(2)}, u32[]{:S(2)}) async-start(f32[16,3,16]{2,1,0:T(4,128)} %bitcast.55), calls=%async_computation.6 | async-start | bytes 65536 | tf_op jit(solution)/shard_map/all_to_all | solution.py:68
  327.0 18.1 %copy-start.10 = (s32[1,32]{1,0:T(1,128)S(1)}, s32[1,32]{1,0:T(1,128)}, u32[]{:S(2)}) copy-start(s32[1,32]{1,0:T(1,128)} %param.9) | copy-start | bytes 388
  338.8 20.5 %all-to-all-start.5 = ((bf16[16,32,512]{2,1,0:T(8,128)(2,1)}), bf16[16,32,512]{2,1,0:T(8,128)(2,1)S(1)}, u32[]{:S(2)}, u32[]{:S(2)}) async-start(bf16[16,32,512]{2,1,0:T(8,128)(2,1)} %bitcast.64), calls=%async_computation.5 | async-start | bytes 1048576 | tf_op jit(solution)/shard_map/all_to_all | solution.py:68

commit v2 on v1

--- a/solution.py
+++ b/solution.py
@@ -29,6 +29,7 @@
 
 PLANE = NGRID * NGRID
 GROUP = 8
+SLAB = 128
 LANES = 256
 VMEM_BYTES = 56 * 2**20
 
@@ -64,8 +65,14 @@
     return jnp.dot(left_mat, right_mat, preferred_element_type=jnp.float32)
 
 
-def exchange(blocks):
-    return lax.all_to_all(blocks, "ga", split_axis=0, concat_axis=0, tiled=True)
+def exchange(blocks, groups=None):
+    return lax.all_to_all(
+        blocks, "ga", split_axis=0, concat_axis=0, tiled=True, axis_index_groups=groups
+    )
+
+
+def other_core(block, parts):
+    return lax.ppermute(block, "ga", [(device, device ^ 1) for device in range(parts)])
 
 
 def transform_tables():
@@ -95,10 +102,60 @@
     ]
 
 
-def potential_kernel(
-    wave_ref, cos_ref, sin_ref, back_ref, fore_ref, pot_ref, out_ref, rows, planes, turned
+def cosine_and_sine(phases):
+    turns = jnp.round(phases * (0.5 / np.pi))
+    left = (phases - turns * 6.28125) - turns * (2.0 * np.pi - 6.28125)
+    quarter = left * 0.25
+    square = quarter * quarter
+    sine = 1.0 + square * (
+        -1.0 / 6 + square * (1.0 / 120 + square * (-1.0 / 5040 + square * (1.0 / 362880)))
+    )
+    sine = quarter * sine
+    versine = square * (
+        0.5
+        + square
+        * (-1.0 / 24 + square * (1.0 / 720 + square * (-1.0 / 40320 + square * (1.0 / 3628800))))
+    )
+    for _ in range(2):
+        sine, versine = 2.0 * sine * (1.0 - versine), 2.0 * sine * sine
+    return 1.0 - versine, sine
+
+
+def projector_tables(oxygens):
+    line = frequency(jnp.arange(NGRID, dtype=jnp.int32), NGRID)
+    second, third = jnp.repeat(line, NGRID), jnp.tile(line, NGRID)
+    envelope = jnp.exp(-0.5 * width_square * (second * second + third * third))
+    cosine, sine = cosine_and_sine(
+        oxygens[1][:, None] * second[None, :] + oxygens[2][:, None] * third[None, :]
+    )
+    in_plane = jnp.concatenate([envelope * cosine, envelope * sine], 0)
+    in_plane = jnp.concatenate([in_plane, second * in_plane, third * in_plane], 0).astype(bf16)
+    envelope = jnp.exp(-0.5 * width_square * line * line)[:, None]
+    cosine, sine = cosine_and_sine(line[:, None] * oxygens[0][None, :])
+    cosine, sine = envelope * cosine, envelope * sine
+    along = jnp.stack([cosine, sine, line[:, None] * cosine, line[:, None] * sine])
+    return in_plane, along
+
+
+def wave_kernel(
+    wave_ref,
+    cos_ref,
+    sin_ref,
+    back_ref,
+    fore_ref,
+    pot_ref,
+    in_plane_ref,
+    along_ref,
+    out_ref,
+    force_ref,
+    rows,
+    planes,
+    turned,
+    sums,
+    pulls,
 ):
     parts, local_g = wave_ref.shape[0], wave_ref.shape[3]
+    waters = along_ref.shape[2]
     band_rows = 2 * GROUP
     all_rows = NGRID * band_rows
     piece = min(local_g, PLANE)
@@ -109,6 +166,56 @@
         rows[x * band_rows : (x + 1) * band_rows, column : column + piece] = block.reshape(
             band_rows, piece
         )
+
+    @pl.loop(0, sums.shape[0] // 2)
+    def _(step):
+        columns = pl.ds(pl.multiple_of(step * 2 * SLAB, 2 * SLAB), 2 * SLAB)
+        found = inner(rows[...], in_plane_ref[columns, :])
+        sums[2 * step] = found[:, :SLAB]
+        sums[2 * step + 1] = found[:, SLAB:]
+
+    @pl.when(pl.program_id(0) == 0)
+    def _():
+        force_ref[...] = jnp.zeros_like(force_ref)
+
+    slabs = waters // SLAB
+    real, imag = (pl.ds(first, all_rows // 2, stride=2) for first in range(2))
+    shape = (NGRID, GROUP, SLAB)
+    for slab in range(slabs):
+        inside = slice(slab * SLAB, (slab + 1) * SLAB)
+        factors = [along_ref[which, :, inside][:, None, :] for which in range(4)]
+
+        def planewise(factor):
+            first = 2 * factor * slabs + slab
+            second = first + slabs
+            found_re = sums[first, real, :] - sums[second, imag, :]
+            found_im = sums[second, real, :] + sums[first, imag, :]
+            return found_re.reshape(shape), found_im.reshape(shape)
+
+        def over_x(found, cosines, sines):
+            return (
+                jnp.sum(found[0] * cosines - found[1] * sines, axis=0),
+                jnp.sum(found[0] * sines + found[1] * cosines, axis=0),
+            )
+
+        plain = planewise(0)
+        proj_re, proj_im = over_x(plain, *factors[:2])
+        proj_re = (proj_re * (1.0 / GVECS)).astype(bf16).astype(f32)
+        proj_im = (proj_im * (1.0 / GVECS)).astype(bf16).astype(f32)
+        for axis in range(3):
+            if axis == 0:
+                slope_re, slope_im = over_x(plain, *factors[2:])
+            else:
+                slope_re, slope_im = over_x(planewise(axis), *factors[:2])
+            force_ref[axis, :, inside] += proj_re * slope_im - proj_im * slope_re
+
+        cosines, sines = factors[:2]
+        pull_re = nonlocal_strength * (cosines * proj_re[None] + sines * proj_im[None])
+        pull_im = nonlocal_strength * (cosines * proj_im[None] - sines * proj_re[None])
+        for half, pull in enumerate(((pull_re, pull_im), (pull_im, -pull_re))):
+            both = jnp.concatenate(pull, 1).reshape(all_rows, SLAB).astype(bf16)
+            start = half * waters + slab * SLAB
+            pulls[:, start : start + SLAB] = both
 
     @pl.loop(0, PLANE // LANES)
     def _(step):
@@ -132,6 +239,7 @@
     def _(step):
         columns = pl.ds(pl.multiple_of(step * LANES, LANES), LANES)
         waves = matmul(turned[...], cos_ref[:, columns]) + matmul(rows[...], sin_ref[:, columns])
+        waves += matmul(pulls[...], in_plane_ref[: 2 * waters, columns])
         planes[:all_rows, columns] = waves.astype(bf16)
 
     for start in range(0, NGRID * PLANE, piece):
@@ -142,14 +250,15 @@
         ]
 
 
-def apply_potential(waves, tables, grid_potential):
+def apply_hamiltonian(waves, tables, grid_potential, in_plane, along):
     parts, band_count, _, local_g = waves.shape
+    waters = along.shape[2]
     steps = band_count // GROUP
     band_rows = 2 * GROUP
     all_rows = NGRID * band_rows
     whole = lambda step: (0, 0)
     return pl.pallas_call(
-        potential_kernel,
+        wave_kernel,
         grid=(steps,),
         in_specs=[
             pl.BlockSpec((parts, GROUP, 2, local_g), lambda step: (0, step, 0, 0)),
@@ -158,28 +267,39 @@
             pl.BlockSpec((all_rows, 2 * all_rows), whole),
             pl.BlockSpec((all_rows, all_rows), whole),
             pl.BlockSpec((NGRID, PLANE), whole),
-        ],
-        out_specs=pl.BlockSpec((parts, 1, band_rows, local_g), lambda step: (0, step, 0, 0)),
-        out_shape=jax.ShapeDtypeStruct((parts, steps, band_rows, local_g), bf16),
+            pl.BlockSpec((6 * waters, PLANE), whole),
+            pl.BlockSpec((4, NGRID, waters), lambda step: (0, 0, 0)),
+        ],
+        out_specs=[
+            pl.BlockSpec((parts, 1, band_rows, local_g), lambda step: (0, step, 0, 0)),
+            pl.BlockSpec((3, GROUP, waters), lambda step: (0, 0, 0)),
+        ],
+        out_shape=[
+            jax.ShapeDtypeStruct((parts, steps, band_rows, local_g), bf16),
+            jax.ShapeDtypeStruct((3, GROUP, waters), f32),
+        ],
         scratch_shapes=[
             pltpu.VMEM((all_rows, PLANE), bf16),
             pltpu.VMEM((2 * all_rows, PLANE), bf16),
             pltpu.VMEM((all_rows, PLANE), bf16),
+            pltpu.VMEM((6 * waters // SLAB, all_rows, SLAB), f32),
+            pltpu.VMEM((all_rows, 2 * waters), bf16),
         ],
         compiler_params=pltpu.CompilerParams(vmem_limit_bytes=VMEM_BYTES),
         cost_estimate=pl.CostEstimate(
-            flops=steps * 2 * all_rows * PLANE * (4 * PLANE + 3 * all_rows),
+            flops=steps * 2 * all_rows * PLANE * (4 * PLANE + 3 * all_rows + 8 * waters),
             bytes_accessed=8 * steps * band_rows * parts * local_g + 8 * PLANE * PLANE,
             transcendentals=0,
         ),
-    )(waves, *tables, grid_potential)
-
-
-def trial_kernel(count, base_ref, *refs):
-    potentials, (trial_ref, margin_ref, even, odd) = refs[:count], refs[count:]
+    )(waves, *tables, grid_potential, in_plane, along)
+
+
+def trial_kernel(count, core_ref, kinetic_ref, planes_ref, *refs):
+    potentials, (trial_ref, mine_ref, other_ref, even, odd) = refs[:count], refs[count:]
     step = pl.program_id(0)
-    bands = base_ref.shape[1]
+    bands = planes_ref.shape[1]
     share = bands // count
+    kept = 1.0 - step_size * kinetic_ref[...]
 
     for chunk in range(count):
         block = potentials[chunk][...].astype(f32) * step_size
@@ -187,7 +307,8 @@
         inside = slice(chunk * share, (chunk + 1) * share)
         for half in range(2):
             taken = block[:, half].reshape(share, block.shape[3])
-            trial_ref[half, inside, :] = (base_ref[half, inside, :] - taken).astype(bf16)
+            wave = planes_ref[half, inside, :].astype(f32)
+            trial_ref[half, inside, :] = (wave * kept - taken).astype(bf16)
     real, imag = trial_ref[0], trial_ref[1]
 
     @pl.when(step == 0)
@@ -204,40 +325,55 @@
         row = lax.broadcasted_iota(jnp.int32, even.shape, 0)
         column = lax.broadcasted_iota(jnp.int32, even.shape, 1)
         packed = jnp.where(row <= column, even[...], across - across.T)
-        margin_ref[...] = (packed * (1.0 / GVECS)).astype(bf16)
-
-
-def make_trial(base, potentials):
-    _, bands, local_g = base.shape
+        even[...] = packed * (1.0 / GVECS)
+        half = bands // 2
+        core = core_ref[0]
+        mine_ref[...] = even[pl.ds(pl.multiple_of(core * half, half), half), :]
+        others = even[pl.ds(pl.multiple_of((1 - core) * half, half), half), :]
+        other_ref[...] = others.astype(bf16)
+
+
+def make_trial(core, kinetic, planes, potentials):
+    _, bands, local_g = planes.shape
     count = len(potentials)
     width = min(LANES, local_g)
     return pl.pallas_call(
         functools.partial(trial_kernel, count),
         grid=(local_g // width,),
-        in_specs=[pl.BlockSpec((2, bands, width), lambda step: (0, 0, step))]
+        in_specs=[
+            pl.BlockSpec(memory_space=pltpu.SMEM),
+            pl.BlockSpec((1, width), lambda step: (0, step)),
+            pl.BlockSpec((2, bands, width), lambda step: (0, 0, step)),
+        ]
         + [pl.BlockSpec((2 * bands // count, width), lambda step: (0, step))] * count,
         out_specs=[
             pl.BlockSpec((2, bands, width), lambda step: (0, 0, step)),
-            pl.BlockSpec((bands, bands), lambda step: (0, 0)),
+            pl.BlockSpec((bands // 2, bands), lambda step: (0, 0)),
+            pl.BlockSpec((bands // 2, bands), lambda step: (0, 0)),
         ],
         out_shape=[
             jax.ShapeDtypeStruct((2, bands, local_g), bf16),
-            jax.ShapeDtypeStruct((bands, bands), bf16),
+            jax.ShapeDtypeStruct((bands // 2, bands), f32),
+            jax.ShapeDtypeStruct((bands // 2, bands), bf16),
         ],
         scratch_shapes=[pltpu.VMEM((bands, bands), f32)] * 2,
         compiler_params=pltpu.CompilerParams(vmem_limit_bytes=VMEM_BYTES),
         cost_estimate=pl.CostEstimate(
             flops=6 * bands * bands * local_g,
-            bytes_accessed=16 * bands * local_g,
+            bytes_accessed=12 * bands * local_g,
             transcendentals=0,
         ),
-    )(base, *potentials)
-
-
-def update_kernel(mixer_ref, trial_ref, out_ref, even, odd):
+    )(core, kinetic, planes, *potentials)
+
+
+def update_kernel(core_ref, mine_ref, other_ref, trial_ref, out_ref, even, odd):
     @pl.when(pl.program_id(0) == 0)
     def _():
-        packed = mixer_ref[...].astype(f32)
+        mine, others = mine_ref[...].astype(f32), other_ref[...].astype(f32)
+        first = core_ref[0] == 0
+        packed = jnp.concatenate(
+            [jnp.where(first, mine, others), jnp.where(first, others, mine)], 0
+        )
         flipped = packed.T
         row = lax.broadcasted_iota(jnp.int32, packed.shape, 0)
         column = lax.broadcasted_iota(jnp.int32, packed.shape, 1)
@@ -250,14 +386,16 @@
     out_ref[:, 1, :] = (matmul(even[...], imag) + matmul(odd[...], real)).astype(bf16)
 
 
-def update_waves(mixer, trial):
+def update_waves(core, mine, others, trial):
     _, bands, local_g = trial.shape
     width = min(LANES, local_g)
     return pl.pallas_call(
         update_kernel,
         grid=(local_g // width,),
         in_specs=[
-            pl.BlockSpec((bands, bands), lambda step: (0, 0)),
+            pl.BlockSpec(memory_space=pltpu.SMEM),
+            pl.BlockSpec((bands // 2, bands), lambda step: (0, 0)),
+            pl.BlockSpec((bands // 2, bands), lambda step: (0, 0)),
             pl.BlockSpec((2, bands, width), lambda step: (0, 0, step)),
         ],
         out_specs=pl.BlockSpec((bands, 2, width), lambda step: (0, 0, step)),
@@ -269,7 +407,7 @@
             bytes_accessed=8 * bands * local_g,
             transcendentals=0,
         ),
-    )(mixer, trial)
+    )(core, mine, others, trial)
 
 
 def per_device(positions, weights, psi, vloc):
@@ -280,75 +418,70 @@
     weight_float = weights.astype(jnp.float32)
     mixing = weight_float / jnp.sum(weight_float, axis=1, keepdims=True)
     own_oxygens = jnp.einsum("cj,jan->can", mixing, positions[:, :, 0::3], precision=highest)[0]
-    everyone = exchange(jnp.broadcast_to(own_oxygens[None], (parts,) + own_oxygens.shape))
-    oxygens = jnp.swapaxes(everyone, 0, 1).reshape(3, WATERS)
-
     count = 2 if bands // parts % (2 * GROUP) == 0 else 1
     share = bands // count
+
+    def outgoing(whole_psi, chunk):
+        block = whole_psi[0, chunk * share : (chunk + 1) * share]
+        return block.reshape(parts, share // parts, 2, local_g)
+
+    waves = [exchange(outgoing(psi, 0))]
+    later_psi, own_oxygens = lax.optimization_barrier((psi, own_oxygens))
+    later = [outgoing(later_psi, chunk) for chunk in range(1, count)]
+    waves[0], own_oxygens, *later = lax.optimization_barrier((waves[0], own_oxygens, *later))
+    everyone = exchange(jnp.broadcast_to(own_oxygens[None], (parts,) + own_oxygens.shape))
+    everyone, *later = lax.optimization_barrier((everyone, *later))
+    waves += [exchange(block) for block in later]
+    oxygens = jnp.swapaxes(everyone, 0, 1).reshape(3, WATERS)
     tables = transform_tables()
+    in_plane, along = projector_tables(oxygens)
     grid_potential = vloc[0].reshape(NGRID, PLANE) * (1.0 / GVECS)
-    potentials = []
-    for chunk in range(count):
-        sent = psi[0, chunk * share : (chunk + 1) * share].reshape(
-            parts, share // parts, 2, local_g
-        )
-        moved = apply_potential(exchange(sent), tables, grid_potential)
+    potentials, forces = [], []
+    for wave in waves:
+        moved, force = apply_hamiltonian(wave, tables, grid_potential, in_plane, along)
         potentials.append(exchange(moved).reshape(2 * share, local_g))
+        forces.append(force)
+    force_part = jnp.sum(sum(forces), axis=1) * (2.0 * occupation * nonlocal_strength / GVECS)
 
     flat_index = lax.axis_index("ga") * local_g + jnp.arange(local_g, dtype=jnp.int32)
-    gvectors = jnp.stack(
-        [
-            frequency(flat_index // (NGRID * NGRID), NGRID),
-            frequency(flat_index // NGRID % NGRID, NGRID),
-            frequency(flat_index % NGRID, NGRID),
-        ]
-    )
-    square = jnp.sum(gvectors * gvectors, axis=0)
-    profile = jnp.exp(-0.5 * width_square * square)
-    kinetic = 0.5 * square
-    phases = jnp.einsum("ai,ag->ig", oxygens, gvectors, precision=highest)
-    wave_cos = profile * jnp.cos(phases)
-    wave_sin = profile * jnp.sin(phases)
-    table = jnp.concatenate(
-        [jnp.concatenate([wave_cos, -wave_sin], 1), jnp.concatenate([wave_sin, wave_cos], 1)], 0
-    ).astype(bf16)
+    square = (
+        frequency(flat_index // PLANE, NGRID) ** 2
+        + frequency(flat_index // NGRID % NGRID, NGRID) ** 2
+        + frequency(flat_index % NGRID, NGRID) ** 2
+    )
+    kinetic = (0.5 * square)[None]
     planes = jnp.swapaxes(psi[0], 0, 1)
-    real_part, imag_part = planes[0], planes[1]
-    partial_proj = (
-        inner(table[:, :local_g], real_part) + inner(table[:, local_g:], imag_part)
-    ) * (1.0 / GVECS)
-    all_proj = lax.psum(partial_proj, "ga").astype(bf16)
-    nonlocal_term = lax.dot_general(
-        all_proj, table, (((0,), (0,)), ((), ())), preferred_element_type=jnp.float32
-    )
-    proj_re, proj_im = all_proj[:WATERS], all_proj[WATERS:]
-    weighted_re = matmul(proj_re, real_part) + matmul(proj_im, imag_part)
-    weighted_im = matmul(proj_re, imag_part) - matmul(proj_im, real_part)
-    mixed_wave = wave_cos * weighted_im + wave_sin * weighted_re
-    force_part = (
-        2.0
-        * occupation
-        * nonlocal_strength
-        / GVECS
-        * jnp.einsum("ag,ig->ai", gvectors, mixed_wave, precision=highest)
-    )
-    force_blocks = jnp.swapaxes(force_part.reshape(3, parts, WATERS // parts), 0, 1)
-    oxygen_force = jnp.sum(exchange(force_blocks), axis=0)
+
+    chip, core = lax.axis_index("ga") // 2, lax.axis_index("ga") % 2
+    chips = parts // 2
+    same_core = [[2 * number + which for number in range(chips)] for which in range(2)]
+    core_ref = core.reshape(1).astype(jnp.int32)
+    trial, mine, others = make_trial(core_ref, kinetic, planes, potentials)
+    rows = bands // parts
+    pair = (mine + other_core(others, parts).astype(f32)).astype(bf16)
+    near_chip = WATERS // chips
+    pieces, left = [], force_part
+    for _ in range(3):
+        pieces.append(lax.reduce_precision(left, 8, 7))
+        left = left - pieces[-1]
+    pieces = jnp.swapaxes(jnp.stack(pieces).reshape(9, chips, near_chip), 0, 1)
+    pieces = jnp.pad(pieces.reshape(chips, -1), ((0, 0), (0, GROUP * bands - 9 * near_chip)))
+    sent = [pair.reshape(chips, rows, bands), pieces.reshape(chips, GROUP, bands).astype(bf16)]
+    summed = jnp.sum(exchange(jnp.concatenate(sent, 1), same_core).astype(f32), axis=0)
+    summed, found = summed[:rows], summed[rows:].reshape(-1)[: 9 * near_chip]
+    found = jnp.sum(found.reshape(3, 3, near_chip), axis=0)
+    found = (found + other_core(found, parts)).reshape(3, 2, near_chip // 2)
+    oxygen_force = lax.dynamic_index_in_dim(found, core, 1, keepdims=False)
+    row = (core * chips + chip) * rows + lax.broadcasted_iota(jnp.int32, (rows, bands), 0)
+    column = lax.broadcasted_iota(jnp.int32, (rows, bands), 1)
+    own_mixer = (jnp.where(row == column, 1.5, 0.0) - 0.5 * summed).astype(bf16)
+    half_mixer = exchange(
+        jnp.broadcast_to(own_mixer[None], (chips, rows, bands)), same_core
+    ).reshape(bands // 2, bands)
+    psi_new = update_waves(core_ref, half_mixer, other_core(half_mixer, parts), trial)
+
     hydrogen_zero = jnp.zeros_like(oxygen_force)
     dft_force = jnp.stack([oxygen_force, hydrogen_zero, hydrogen_zero], axis=2).reshape(1, 3, -1)
-
-    pulled = jnp.stack([nonlocal_term[:, :local_g], nonlocal_term[:, local_g:]])
-    wave_float = planes.astype(jnp.float32)
-    base = wave_float - step_size * (kinetic * wave_float + nonlocal_strength * pulled)
-
-    trial, margin = make_trial(base, potentials)
-    rows = bands // parts
-    summed = jnp.sum(exchange(margin.reshape(parts, rows, bands)).astype(jnp.float32), axis=0)
-    row = lax.axis_index("ga") * rows + lax.broadcasted_iota(jnp.int32, (rows, bands), 0)
-    column = lax.broadcasted_iota(jnp.int32, (rows, bands), 1)
-    own_mixer = (jnp.where(row == column, 1.5, 0.0) - 0.5 * summed).astype(bf16)
-    mixer = lax.all_gather(own_mixer, "ga", axis=0, tiled=True)
-    psi_new = update_waves(mixer, trial)
 
     near_forces = field_forces(positions)
     contracted_force = jnp.einsum("cj,can->jan", mixing, dft_force, precision=highest)

time: 401 us -> 288 us (0.72); the launches traced: 394 us -> 287 us
  blocking collectives: 149 us -> 17.6 us
  waiting for transfers between devices: 38.2 us -> 99.5 us
  matrix products: 42.2 us -> 0.72 us
  Pallas kernels: 70.3 us -> 88.9 us
  other arithmetic: 27.8 us -> 9.2 us
    psum x1 -> x0, blocking collectives: 74.1 us -> none  [per_device(): all_proj = lax.psum(partial_proj, 'ga').astype(bf16)]
    all_to_all x6, waiting for transfers between devices: 38.2 us -> 97.1 us  [exchange(): lax.all_to_all(blocks, 'ga', split_axis=0, concat_axis=0, tiled=True, axi...]
    dot_general x9 -> x0, matrix products: 40.8 us -> none  [the longest x4 21.7 us: matmul(): return jnp.dot(left_mat, right_mat, preferred_element_type=jnp.float32)]
    all_to_all x1, blocking collectives: 52.2 us -> 17.6 us  [exchange(): lax.all_to_all(blocks, 'ga', split_axis=0, concat_axis=0, tiled=True, axi...]
    all_gather x1 -> x0, blocking collectives: 22.7 us -> none  [per_device(): mixer = lax.all_gather(own_mixer, 'ga', axis=0, tiled=True)]
    pallas_call x2, Pallas kernels: 46.4 us -> 65.1 us  [apply_hamiltonian(): pl.pallas_call(wave_kernel, grid=(steps,), in_specs=[pl.BlockSpec((parts,...]
    concatenate x1 -> x2, other arithmetic: 19.7 us -> 2.6 us  [the longest x1 1.86 us: projector_tables(): jnp.concatenate([in_plane, second * in_plane, third * in_plane], 0)]
    sub x1 -> x0, other arithmetic: 5.11 us -> none  [per_device(): wave_float - step_size * (kinetic * wave_float + nonlocal_strength * pulled)]
  transfers between devices with their start and end apart: 6 -> 9, of which waited for: 4 -> 9; matrix products, arithmetic and copies ran while one was open for 21% -> 8% of each run, Pallas kernels for 15% -> 23%
where the time goes in v2:
time: 288 us; the launch traced here: 287 us
  waiting for transfers between devices  99.5 us (35%)
  Pallas kernels  88.9 us (31%)
  starting transfers between devices  49.6 us (17%)
  local copies, waits for them, and re-layouts  20.2 us (7%)
  blocking collectives  17.6 us (6%)
  other arithmetic  9.2 us (3%)
    all_to_all x6, waiting for transfers between devices, exchange(): lax.all_to_all(blocks, 'ga', split_axis=0, concat_axis=0, tiled=True, axi...  97.1 us
    pallas_call x2, Pallas kernels, apply_hamiltonian(): pl.pallas_call(wave_kernel, grid=(steps,), in_specs=[pl.BlockSpec((parts,...  65.1 us
    all_to_all x6, starting transfers between devices, exchange(): lax.all_to_all(blocks, 'ga', split_axis=0, concat_axis=0, tiled=True, axi...  48.8 us
    all_to_all x1, blocking collectives, exchange(): lax.all_to_all(blocks, 'ga', split_axis=0, concat_axis=0, tiled=True, axi...  17.6 us
    pallas_call x1, Pallas kernels, update_waves(): pl.pallas_call(update_kernel, grid=(local_g // width,), in_specs=[pl.Bloc...  12.1 us
    pallas_call x1, Pallas kernels, make_trial(): pl.pallas_call(functools.partial(trial_kernel, count), grid=(local_g // w...  11.7 us
    slice x2, local copies, waits for them, and re-layouts, outgoing(): block = whole_psi[0, chunk * share:(chunk + 1) * share]  8.74 us
    unnamed x24, local copies, waits for them, and re-layouts  7.73 us
  transfers between devices with their start and end apart: 9, of which 9 were waited for; matrix products, arithmetic and copies ran while one was open for 8% of the time, Pallas kernels for 23%

profile of v2, /device:TPU:0, one launch (start us, length us, event | category | flops | bytes accessed | tf_op | source)
XLA Modules:
  0.0 286.7 jit_solution(17655740103797243704)
XLA Ops:
  0.6 4.4 %slice.53 = bf16[1,256,2,2048]{3,2,1,0:T(2,128)(2,1)} slice(bf16[1,512,2,2048]{3,2,1,0:T(2,128)(2,1)} %param.10), slice={[0:1], [0:256], [0:2], [0:2048]} | slice | bytes 4194304 | tf_op jit(solution)/shard_map/slice | solution.py:425
  5.0 7.5 %all-to-all-start = ((bf16[16,16,2,2048]{3,2,1,0:T(2,128)(2,1)}), bf16[16,16,2,2048]{3,2,1,0:T(2,128)(2,1)S(1)}, u32[]{:S(2)}, u32[]{:S(2)}) async-start(bf16[16,16,2,2048]{3,2,1,0:T(2,128)(2,1)} %bitcast.3), calls=%async_computation | async-start | bytes 4194304 | tf_op jit(solution)/shard_map/all_to_all | solution.py:69
  13.4 0.7 fusion.43
  14.1 4.4 %slice.55 = bf16[1,256,2,2048]{3,2,1,0:T(2,128)(2,1)} slice(bf16[1,512,2,2048]{3,2,1,0:T(2,128)(2,1)} %param.10), slice={[0:1], [256:512], [0:2], [0:2048]} | slice | bytes 4194304 | tf_op jit(solution)/shard_map/slice | solution.py:425
  18.5 35.1 %all-to-all-done.wave_ref = bf16[16,16,2,2048]{3,2,1,0:T(2,128)(2,1)S(1)} async-done(((bf16[16,16,2,2048]{3,2,1,0:T(2,128)(2,1)}), bf16[16,16,2,2048]{3,2,1,0:T(2,128)(2,1)S(1)}, u32[]{:S(2)}, u32[]{:S(2)}) %all-to-all-start) | async-done | bytes 2097184 | tf_op jit(solution)/shard_map/all_to_all | solution.py:69
  53.6 17.6 %all_to_all.35 = f32[16,3,16]{2,1,0:T(4,128)S(1)} all-to-all(f32[16,3,16]{2,1,0:T(4,128)S(1)} %broadcast_in_dim.45), channel_id=1, replica_groups=mesh['rep'=2,'ga'=16] {'ga'}, dimensions={0} | all-to-all | bytes 6144 | tf_op jit(solution)/shard_map/all_to_all | solution.py:69
  71.3 4.4 %all-to-all-start.3 = ((bf16[16,16,2,2048]{3,2,1,0:T(2,128)(2,1)}), bf16[16,16,2,2048]{3,2,1,0:T(2,128)(2,1)}, u32[]{:S(2)}, u32[]{:S(2)}) async-start(bf16[16,16,2,2048]{3,2,1,0:T(2,128)(2,1)} %bitcast.7), calls=%async_computation.3 | async-start | bytes 4194304 | tf_op jit(solution)/shard_map/all_to_all | solution.py:69
  78.1 1.5 fusion.7
  80.1 1.9 pad_maximum_fusion.in_plane_ref
  82.0 32.5 %shard_map.95 = (bf16[16,2,16,2048]{3,2,1,0:T(8,128)(2,1)}, f32[3,8,256]{2,1,0:T(8,128)}) custom-call(bf16[16,16,2,2048]{3,2,1,0:T(2,128)(2,1)} %copy-done, bf16[1024,1024]{1,0:T(8,128)(2,1)} %constant.172.clone.cos_ref, bf16[1024,1024]{1,0:T(8,128)(2,1)} %constant.173.clone.sin_ref, bf16[512,1024]{1,0:T(8,128)(2,1)} %constant.174.clone.back_ref, ...), custom_call_target="tpu_custom_call" | custom-call | flops 16106127360 | bytes 16777216 | tf_op jit(solution)/shard_map/pallas_call | solution.py:260
  114.5 2.3 all-to-all-done.3.wave_ref
  116.8 11.2 %all-to-all-start.2 = ((bf16[16,2,16,2048]{3,2,1,0:T(8,128)(2,1)}), bf16[16,2,16,2048]{3,2,1,0:T(8,128)(2,1)S(1)}, u32[]{:S(2)}, u32[]{:S(2)}) async-start(bf16[16,2,16,2048]{3,2,1,0:T(8,128)(2,1)} %get-tuple-element.22), calls=%async_computation.2 | async-start | bytes 4194304 | tf_op jit(solution)/shard_map/all_to_all | solution.py:69
  128.0 32.6 %shard_map.96 = (bf16[16,2,16,2048]{3,2,1,0:T(8,128)(2,1)}, f32[3,8,256]{2,1,0:T(8,128)}) custom-call(bf16[16,16,2,2048]{3,2,1,0:T(2,128)(2,1)} %all-to-all-done.3.wave_ref, bf16[1024,1024]{1,0:T(8,128)(2,1)} %constant.172.clone.cos_ref, bf16[1024,1024]{1,0:T(8,128)(2,1)} %constant.173.clone.sin_ref, bf16[512,1024]{1,0:T(8,128)(2,1)} %constant.174.clone.back_ref, ...), custom_call_target="tpu_custom_call" | custom-call | flops 16106127360 | bytes 16777216 | tf_op jit(solution)/shard_map/pallas_call | solution.py:260
  160.6 8.5 %all-to-all-done.2 = bf16[16,2,16,2048]{3,2,1,0:T(8,128)(2,1)S(1)} async-done(((bf16[16,2,16,2048]{3,2,1,0:T(8,128)(2,1)}), bf16[16,2,16,2048]{3,2,1,0:T(8,128)(2,1)S(1)}, u32[]{:S(2)}, u32[]{:S(2)}) %all-to-all-start.2) | async-done | bytes 2097184 | tf_op jit(solution)/shard_map/all_to_all | solution.py:69
  169.1 11.3 %all-to-all-start.4 = ((bf16[16,2,16,2048]{3,2,1,0:T(8,128)(2,1)}), bf16[16,2,16,2048]{3,2,1,0:T(8,128)(2,1)}, u32[]{:S(2)}, u32[]{:S(2)}) async-start(bf16[16,2,16,2048]{3,2,1,0:T(8,128)(2,1)} %get-tuple-element.24), calls=%async_computation.4 | async-start | bytes 4194304 | tf_op jit(solution)/shard_map/all_to_all | solution.py:69
  180.4 6.1 %copy.39 = bf16[1,512,2,2048]{3,1,2,0:T(8,128)(2,1)} copy(bf16[1,512,2,2048]{3,2,1,0:T(2,128)(2,1)} %param.10) | data formatting | bytes 8388608 | tf_op args[2]
  187.1 0.8 fusion.37.kinetic_ref
  187.9 33.6 %all-to-all-done.4 = bf16[16,2,16,2048]{3,2,1,0:T(8,128)(2,1)} async-done(((bf16[16,2,16,2048]{3,2,1,0:T(8,128)(2,1)}), bf16[16,2,16,2048]{3,2,1,0:T(8,128)(2,1)}, u32[]{:S(2)}, u32[]{:S(2)}) %all-to-all-start.4) | async-done | bytes 2097184 | tf_op jit(solution)/shard_map/all_to_all | solution.py:69
  221.5 11.7 %shard_map.97 = (bf16[2,512,2048]{2,1,0:T(8,128)(2,1)}, f32[256,512]{1,0:T(8,128)}, bf16[256,512]{1,0:T(8,128)(2,1)}) custom-call(s32[1]{0:T(128)} %bitcast.core_ref, f32[1,2048]{1,0:T(1,128)} %fusion.37.kinetic_ref, bf16[2,512,2048]{2,1,0:T(8,128)(2,1)} %bitcast.46, bf16[512,2048]{1,0:T(8,128)(2,1)} %bitcast.47, bf16[512,2048]{1,0:T(8,128)(2,1)} %bitcast.10.refs_1_), custom_call_target="tpu_custom_call" | custom-call | flops 3221225472 | bytes 12582912 | tf_op jit(solution)/shard_map/pallas_call | solution.py:340
  233.3 0.8 collective-permute-start
  234.3 1.1 collective-permute-done
  235.4 1.1 add_convert_fusion
  236.5 0.7 pad_maximum_fusion.2
  237.3 10.7 %all-to-all-start.5 = ((bf16[8,40,512]{2,1,0:T(8,128)(2,1)}), bf16[8,40,512]{2,1,0:T(8,128)(2,1)S(1)}, u32[]{:S(2)}, u32[]{:S(2)}) async-start(bf16[8,40,512]{2,1,0:T(8,128)(2,1)} %pad_maximum_fusion.2), calls=%async_computation.5 | async-start | bytes 655360 | tf_op jit(solution)/shard_map/all_to_all | solution.py:69
  248.7 10.1 %all-to-all-done.5 = bf16[8,40,512]{2,1,0:T(8,128)(2,1)S(1)} async-done(((bf16[8,40,512]{2,1,0:T(8,128)(2,1)}), bf16[8,40,512]{2,1,0:T(8,128)(2,1)S(1)}, u32[]{:S(2)}, u32[]{:S(2)}) %all-to-all-start.5) | async-done | bytes 327712 | tf_op jit(solution)/shard_map/all_to_all | solution.py:69
  258.9 0.7 broadcast_in_dim.46
  259.6 3.6 %all-to-all-start.6 = ((bf16[8,32,512]{2,1,0:T(8,128)(2,1)}), bf16[8,32,512]{2,1,0:T(8,128)(2,1)S(1)}, u32[]{:S(2)}, u32[]{:S(2)}) async-start(bf16[8,32,512]{2,1,0:T(8,128)(2,1)} %broadcast_in_dim.46), calls=%async_computation.6 | async-start | bytes 524288 | tf_op jit(solution)/shard_map/all_to_all | solution.py:69
  264.0 0.8 collective-permute-done.2
  264.9 7.5 %all-to-all-done.6 = bf16[8,32,512]{2,1,0:T(8,128)(2,1)S(1)} async-done(((bf16[8,32,512]{2,1,0:T(8,128)(2,1)}), bf16[8,32,512]{2,1,0:T(8,128)(2,1)S(1)}, u32[]{:S(2)}, u32[]{:S(2)}) %all-to-all-start.6) | async-done | bytes 262176 | tf_op jit(solution)/shard_map/all_to_all | solution.py:69
  272.7 0.7 copy.33
  273.9 0.7 copy-done.8
  274.6 12.1 %shard_map.98 = bf16[512,2,2048]{2,1,0:T(2,128)(2,1)} custom-call(s32[1]{0:T(128)} %bitcast.core_ref, bf16[256,512]{1,0:T(8,128)(2,1)} %bitcast.50, bf16[256,512]{1,0:T(8,128)(2,1)} %copy-done.8, bf16[2,512,2048]{2,1,0:T(8,128)(2,1)} %get-tuple-element.29.trial_ref), custom_call_target="tpu_custom_call" | custom-call | flops 4294967296 | bytes 8388608 | tf_op jit(solution)/shard_map/pallas_call | solution.py:392
  (76 shorter events, 7.0 us)
Async XLA Ops:
  5.0 7.5 %copy-start.2 = (f32[32,3,48]{2,0,1:T(8,128)S(1)}, f32[32,3,48]{2,0,1:T(8,128)}, u32[]{:S(2)}) copy-start(f32[32,3,48]{2,0,1:T(8,128)} %param.8) | copy-start | bytes 55300
  5.0 7.8 %copy-start.7 = (s32[1,32]{1,0:T(1,128)S(1)}, s32[1,32]{1,0:T(1,128)}, u32[]{:S(2)}) copy-start(s32[1,32]{1,0:T(1,128)} %param.9) | copy-start | bytes 388
  5.0 48.6 %all-to-all-start = ((bf16[16,16,2,2048]{3,2,1,0:T(2,128)(2,1)}), bf16[16,16,2,2048]{3,2,1,0:T(2,128)(2,1)S(1)}, u32[]{:S(2)}, u32[]{:S(2)}) async-start(bf16[16,16,2,2048]{3,2,1,0:T(2,128)(2,1)} %bitcast.3), calls=%async_computation | async-start | bytes 4194304 | tf_op jit(solution)/shard_map/all_to_all | solution.py:69
  18.5 57.5 %copy-start.4 = (f32[1,32768]{1,0:T(1,128)S(1)}, f32[1,32768]{1,0:T(1,128)}, u32[]{:S(2)}) copy-start(f32[1,32768]{1,0:T(1,128)} %param.11) | copy-start | bytes 393220
  53.6 26.1 %copy-start = (bf16[16,16,2,2048]{3,2,1,0:T(2,128)(2,1)}, bf16[16,16,2,2048]{3,2,1,0:T(2,128)(2,1)S(1)}, u32[]{:S(2)}) copy-start(bf16[16,16,2,2048]{3,2,1,0:T(2,128)(2,1)S(1)} %all-to-all-done.wave_ref) | copy-start | bytes 6291460
  71.3 45.5 %all-to-all-start.3 = ((bf16[16,16,2,2048]{3,2,1,0:T(2,128)(2,1)}), bf16[16,16,2,2048]{3,2,1,0:T(2,128)(2,1)}, u32[]{:S(2)}, u32[]{:S(2)}) async-start(bf16[16,16,2,2048]{3,2,1,0:T(2,128)(2,1)} %bitcast.7), calls=%async_computation.3 | async-start | bytes 4194304 | tf_op jit(solution)/shard_map/all_to_all | solution.py:69
  116.8 52.3 %all-to-all-start.2 = ((bf16[16,2,16,2048]{3,2,1,0:T(8,128)(2,1)}), bf16[16,2,16,2048]{3,2,1,0:T(8,128)(2,1)S(1)}, u32[]{:S(2)}, u32[]{:S(2)}) async-start(bf16[16,2,16,2048]{3,2,1,0:T(8,128)(2,1)} %get-tuple-element.22), calls=%async_computation.2 | async-start | bytes 4194304 | tf_op jit(solution)/shard_map/all_to_all | solution.py:69
  169.1 17.4 %copy-start.1 = (bf16[16,2,16,2048]{3,2,1,0:T(8,128)(2,1)}, bf16[16,2,16,2048]{3,2,1,0:T(8,128)(2,1)S(1)}, u32[]{:S(2)}) copy-start(bf16[16,2,16,2048]{3,2,1,0:T(8,128)(2,1)S(1)} %all-to-all-done.2) | copy-start | bytes 6291460
  169.1 52.4 %all-to-all-start.4 = ((bf16[16,2,16,2048]{3,2,1,0:T(8,128)(2,1)}), bf16[16,2,16,2048]{3,2,1,0:T(8,128)(2,1)}, u32[]{:S(2)}, u32[]{:S(2)}) async-start(bf16[16,2,16,2048]{3,2,1,0:T(8,128)(2,1)} %get-tuple-element.24), calls=%async_computation.4 | async-start | bytes 4194304 | tf_op jit(solution)/shard_map/all_to_all | solution.py:69
  180.4 7.5 %copy-start.5 = (f32[3,8,256]{2,1,0:T(8,128)S(1)}, f32[3,8,256]{2,1,0:T(8,128)}, u32[]{:S(2)}) copy-start(f32[3,8,256]{2,1,0:T(8,128)} %get-tuple-element.27) | copy-start | bytes 73732
  180.4 7.5 %copy-start.6 = (f32[3,8,256]{2,1,0:T(8,128)S(1)}, f32[3,8,256]{2,1,0:T(8,128)}, u32[]{:S(2)}) copy-start(f32[3,8,256]{2,1,0:T(8,128)} %get-tuple-element.28) | copy-start | bytes 73732
  233.3 2.2 collective-permute-start
  237.3 21.5 %all-to-all-start.5 = ((bf16[8,40,512]{2,1,0:T(8,128)(2,1)}), bf16[8,40,512]{2,1,0:T(8,128)(2,1)S(1)}, u32[]{:S(2)}, u32[]{:S(2)}) async-start(bf16[8,40,512]{2,1,0:T(8,128)(2,1)} %pad_maximum_fusion.2), calls=%async_computation.5 | async-start | bytes 655360 | tf_op jit(solution)/shard_map/all_to_all | solution.py:69
  259.6 12.7 %all-to-all-start.6 = ((bf16[8,32,512]{2,1,0:T(8,128)(2,1)}), bf16[8,32,512]{2,1,0:T(8,128)(2,1)S(1)}, u32[]{:S(2)}, u32[]{:S(2)}) async-start(bf16[8,32,512]{2,1,0:T(8,128)(2,1)} %broadcast_in_dim.46), calls=%async_computation.6 | async-start | bytes 524288 | tf_op jit(solution)/shard_map/all_to_all | solution.py:69
  263.6 1.2 collective-permute-start.2
  272.3 1.5 copy-start.3
  272.3 1.5 collective-permute-start.1
  273.9 0.7 copy-start.8

commit v3 on v2

--- a/solution.py
+++ b/solution.py
@@ -31,7 +31,9 @@
 GROUP = 8
 SLAB = 128
 LANES = 256
+WIDE = 512
 VMEM_BYTES = 56 * 2**20
+TAIL_VMEM_BYTES = 60 * 2**20
 
 
 def frequency(index, count):
@@ -119,6 +121,82 @@
     for _ in range(2):
         sine, versine = 2.0 * sine * (1.0 - versine), 2.0 * sine * sine
     return 1.0 - versine, sine
+
+
+def pack_kernel(positions_ref, weights_ref, psi_ref, out_ref, lanes, stage, in_sems, out_sems):
+    parts, total, _, local_g = out_ref.shape
+    extra = lanes.shape[0] // 2
+    own = total - extra
+    arrivals = [
+        pltpu.make_async_copy(
+            psi_ref.at[0, pl.ds(owner * own, own)],
+            stage.at[owner, pl.ds(0, own)],
+            in_sems.at[owner],
+        )
+        for owner in range(parts)
+    ]
+    for copy in arrivals:
+        copy.start()
+    weights = weights_ref[...].astype(f32)
+    mixing = weights / jnp.sum(weights, axis=1, keepdims=True)
+    lanes[...] = jnp.zeros_like(lanes)
+    atoms = positions_ref.shape[2]
+    for axis in range(3):
+        left = jnp.dot(
+            mixing, positions_ref[axis], precision=highest, preferred_element_type=jnp.float32
+        )
+        for piece in range(3):
+            sent = left.astype(bf16).astype(f32)
+            left = left - sent
+            place = (3 * piece + axis) * SLAB
+            row, column = 2 * (place // local_g), place % local_g
+            lanes[row : row + 1, column : column + atoms] = sent
+    for row in range(extra):
+        ending = lanes[2 * row : 2 * row + 2, :].astype(bf16)
+        for owner in range(parts):
+            stage[owner, own + row] = ending
+    departures = [
+        pltpu.make_async_copy(stage.at[owner], out_ref.at[owner], out_sems.at[owner])
+        for owner in range(parts)
+    ]
+    for arrival, departure in zip(arrivals, departures):
+        arrival.wait()
+        departure.start()
+    for copy in departures:
+        copy.wait()
+
+
+def pack_first(positions, weights, psi, parts, share):
+    local_g = psi.shape[3]
+    beads, _, atoms = positions.shape
+    extra = -(-9 * SLAB // local_g)
+    return pl.pallas_call(
+        pack_kernel,
+        in_specs=[
+            pl.BlockSpec(memory_space=pltpu.VMEM),
+            pl.BlockSpec(memory_space=pltpu.VMEM),
+            pl.BlockSpec(memory_space=pl.ANY),
+        ],
+        out_specs=pl.BlockSpec(memory_space=pl.ANY),
+        out_shape=jax.ShapeDtypeStruct((parts, share // parts + extra, 2, local_g), bf16),
+        scratch_shapes=[
+            pltpu.VMEM((2 * extra, local_g), f32),
+            pltpu.VMEM((parts, share // parts + extra, 2, local_g), bf16),
+            pltpu.SemaphoreType.DMA((parts,)),
+            pltpu.SemaphoreType.DMA((parts,)),
+        ],
+        compiler_params=pltpu.CompilerParams(vmem_limit_bytes=TAIL_VMEM_BYTES),
+        cost_estimate=pl.CostEstimate(
+            flops=0, bytes_accessed=8 * share * local_g, transcendentals=0
+        ),
+    )(jnp.swapaxes(positions, 0, 1), weights, psi)
+
+
+def unpack_oxygens(rows, atoms):
+    parts = rows.shape[0]
+    pieces = rows.reshape(parts, -1)[:, : 9 * SLAB].reshape(parts, 3, 3, SLAB)
+    found = jnp.sum(pieces[..., 0:atoms:3].astype(f32), axis=1)
+    return jnp.swapaxes(found, 0, 1).reshape(3, -1)
 
 
 def projector_tables(oxygens):
@@ -250,8 +328,8 @@
         ]
 
 
-def apply_hamiltonian(waves, tables, grid_potential, in_plane, along):
-    parts, band_count, _, local_g = waves.shape
+def apply_hamiltonian(waves, band_count, tables, grid_potential, in_plane, along):
+    parts, _, _, local_g = waves.shape
     waters = along.shape[2]
     steps = band_count // GROUP
     band_rows = 2 * GROUP
@@ -294,79 +372,127 @@
     )(waves, *tables, grid_potential, in_plane, along)
 
 
-def trial_kernel(count, core_ref, kinetic_ref, planes_ref, *refs):
-    potentials, (trial_ref, mine_ref, other_ref, even, odd) = refs[:count], refs[count:]
+def trial_kernel(
+    first, last, core_ref, kinetic_ref, wave_ref, potential_ref, pieces_ref, before_ref,
+    margin_ref, trial_ref, mine_ref, other_ref, even, odd, packed,
+):
     step = pl.program_id(0)
-    bands = planes_ref.shape[1]
-    share = bands // count
+    share, width = wave_ref.shape[1:]
     kept = 1.0 - step_size * kinetic_ref[...]
-
-    for chunk in range(count):
-        block = potentials[chunk][...].astype(f32) * step_size
-        block = block.reshape(share // GROUP, 2, GROUP, block.shape[1])
-        inside = slice(chunk * share, (chunk + 1) * share)
-        for half in range(2):
-            taken = block[:, half].reshape(share, block.shape[3])
-            wave = planes_ref[half, inside, :].astype(f32)
-            trial_ref[half, inside, :] = (wave * kept - taken).astype(bf16)
+    block = potential_ref[...].astype(f32) * step_size
+    block = block.reshape(share // GROUP, 2, GROUP, width)
+    for half in range(2):
+        taken = block[:, half].reshape(share, width)
+        trial_ref[half] = (wave_ref[half].astype(f32) * kept - taken).astype(bf16)
     real, imag = trial_ref[0], trial_ref[1]
+    if first:
+        all_real, all_imag = real, imag
+    else:
+        all_real = jnp.concatenate([before_ref[0], real], 0)
+        all_imag = jnp.concatenate([before_ref[1], imag], 0)
 
     @pl.when(step == 0)
     def _():
         even[...] = jnp.zeros_like(even)
         odd[...] = jnp.zeros_like(odd)
 
-    even[...] += inner(real, real) + inner(imag, imag)
-    odd[...] += inner(imag, real)
+    even[...] += inner(real, all_real) + inner(imag, all_imag)
+    odd[...] += inner(imag, all_real) - inner(real, all_imag)
 
     @pl.when(step == pl.num_programs(0) - 1)
     def _():
-        across = odd[...]
-        row = lax.broadcasted_iota(jnp.int32, even.shape, 0)
-        column = lax.broadcasted_iota(jnp.int32, even.shape, 1)
-        packed = jnp.where(row <= column, even[...], across - across.T)
-        even[...] = packed * (1.0 / GVECS)
-        half = bands // 2
-        core = core_ref[0]
-        mine_ref[...] = even[pl.ds(pl.multiple_of(core * half, half), half), :]
-        others = even[pl.ds(pl.multiple_of((1 - core) * half, half), half), :]
-        other_ref[...] = others.astype(bf16)
-
-
-def make_trial(core, kinetic, planes, potentials):
+        start = even.shape[1] - share
+        row = lax.broadcasted_iota(jnp.int32, (share, share), 0)
+        column = lax.broadcasted_iota(jnp.int32, (share, share), 1)
+        own = jnp.where(row <= column, even[:, start:], odd[:, start:]) * (1.0 / GVECS)
+        if not last:
+            mine_ref[...] = own
+        else:
+            packed[start:, start:] = own
+            if not first:
+                packed[:start, :start] = margin_ref[...]
+                packed[start:, :start] = odd[:, :start] * (1.0 / GVECS)
+                packed[:start, start:] = even[:, :start] * (1.0 / GVECS)
+            chips, rows, bands = mine_ref.shape
+            rows -= GROUP
+            half = chips * rows
+            core = core_ref[0]
+            mine = packed[pl.ds(pl.multiple_of(core * half, half), half), :]
+            others = packed[pl.ds(pl.multiple_of((1 - core) * half, half), half), :]
+            mine_ref[:, :rows, :] = mine.reshape(chips, rows, bands)
+            mine_ref[:, rows:, :] = pieces_ref[...]
+            other_ref[:, :rows, :] = others.reshape(chips, rows, bands).astype(bf16)
+            other_ref[:, rows:, :] = jnp.zeros((chips, GROUP, bands), bf16)
+
+
+def make_trial(chunk, count, core, kinetic, planes, potential, pieces, before, margin):
     _, bands, local_g = planes.shape
-    count = len(potentials)
-    width = min(LANES, local_g)
+    chips = pieces.shape[0]
+    share = bands // count
+    first, last = chunk == 0, chunk == count - 1
+    width = min(WIDE, local_g)
+    deep = lambda step: (0, 0, step)
+    if last:
+        rows = bands // (2 * chips) + GROUP
+        out_specs = [pl.BlockSpec((chips, rows, bands), lambda step: (0, 0, 0))] * 2
+        out_shape = [
+            jax.ShapeDtypeStruct((chips, rows, bands), f32),
+            jax.ShapeDtypeStruct((chips, rows, bands), bf16),
+        ]
+    else:
+        out_specs = [pl.BlockSpec((share, share), lambda step: (0, 0))]
+        out_shape = [jax.ShapeDtypeStruct((share, share), f32)]
+    operands = [core, kinetic, planes, potential]
+    in_specs = [
+        pl.BlockSpec(memory_space=pltpu.SMEM),
+        pl.BlockSpec((1, width), lambda step: (0, step)),
+        pl.BlockSpec((2, share, width), lambda step: (0, chunk, step)),
+        pl.BlockSpec((2 * share, width), lambda step: (0, step)),
+    ]
+    if last:
+        operands.append(pieces)
+        in_specs.append(pl.BlockSpec(pieces.shape, lambda step: (0, 0, 0)))
+    if not first:
+        operands += [before, margin]
+        in_specs.append(pl.BlockSpec((2, share, width), deep))
+        in_specs.append(pl.BlockSpec((share, share), lambda step: (0, 0)))
+
+    def body(core_ref, kinetic_ref, wave_ref, potential_ref, *refs):
+        refs = list(refs)
+        pieces_ref = refs.pop(0) if last else None
+        before_ref = None if first else refs.pop(0)
+        margin_ref = None if first else refs.pop(0)
+        trial_ref, mine_ref = refs.pop(0), refs.pop(0)
+        other_ref = refs.pop(0) if last else None
+        trial_kernel(
+            first, last, core_ref, kinetic_ref, wave_ref, potential_ref, pieces_ref, before_ref,
+            margin_ref, trial_ref, mine_ref, other_ref, *refs,
+        )
+
+    seen = (chunk + 1) * share
     return pl.pallas_call(
-        functools.partial(trial_kernel, count),
+        body,
         grid=(local_g // width,),
-        in_specs=[
-            pl.BlockSpec(memory_space=pltpu.SMEM),
-            pl.BlockSpec((1, width), lambda step: (0, step)),
-            pl.BlockSpec((2, bands, width), lambda step: (0, 0, step)),
-        ]
-        + [pl.BlockSpec((2 * bands // count, width), lambda step: (0, step))] * count,
-        out_specs=[
-            pl.BlockSpec((2, bands, width), lambda step: (0, 0, step)),
-            pl.BlockSpec((bands // 2, bands), lambda step: (0, 0)),
-            pl.BlockSpec((bands // 2, bands), lambda step: (0, 0)),
+        in_specs=in_specs,
+        out_specs=[pl.BlockSpec((2, share, width), deep)] + out_specs,
+        out_shape=[jax.ShapeDtypeStruct((2, share, local_g), bf16)] + out_shape,
+        scratch_shapes=[
+            pltpu.VMEM((share, seen), f32),
+            pltpu.VMEM((share, seen), f32),
+            pltpu.VMEM((bands, bands), f32),
         ],
-        out_shape=[
-            jax.ShapeDtypeStruct((2, bands, local_g), bf16),
-            jax.ShapeDtypeStruct((bands // 2, bands), f32),
-            jax.ShapeDtypeStruct((bands // 2, bands), bf16),
-        ],
-        scratch_shapes=[pltpu.VMEM((bands, bands), f32)] * 2,
-        compiler_params=pltpu.CompilerParams(vmem_limit_bytes=VMEM_BYTES),
+        compiler_params=pltpu.CompilerParams(vmem_limit_bytes=TAIL_VMEM_BYTES),
         cost_estimate=pl.CostEstimate(
-            flops=6 * bands * bands * local_g,
-            bytes_accessed=12 * bands * local_g,
+            flops=8 * share * seen * local_g,
+            bytes_accessed=12 * seen * local_g,
             transcendentals=0,
         ),
-    )(core, kinetic, planes, *potentials)
-
-
-def update_kernel(core_ref, mine_ref, other_ref, trial_ref, out_ref, even, odd):
+    )(*operands)
+
+
+def update_kernel(count, core_ref, mine_ref, other_ref, *refs):
+    trials, (out_ref, even, odd) = refs[:count], refs[count:]
+
     @pl.when(pl.program_id(0) == 0)
     def _():
         mine, others = mine_ref[...].astype(f32), other_ref[...].astype(f32)
@@ -374,40 +500,53 @@
         packed = jnp.concatenate(
             [jnp.where(first, mine, others), jnp.where(first, others, mine)], 0
         )
-        flipped = packed.T
-        row = lax.broadcasted_iota(jnp.int32, packed.shape, 0)
-        column = lax.broadcasted_iota(jnp.int32, packed.shape, 1)
-        even[...] = jnp.where(row <= column, packed, flipped).astype(bf16)
-        above = jnp.where(row == column, 0.0, -flipped)
-        odd[...] = jnp.where(row > column, packed, above).astype(bf16)
-
-    real, imag = trial_ref[0], trial_ref[1]
+        share = packed.shape[0] // count
+        row = lax.broadcasted_iota(jnp.int32, (share, share), 0)
+        column = lax.broadcasted_iota(jnp.int32, (share, share), 1)
+        spans = [slice(chunk * share, (chunk + 1) * share) for chunk in range(count)]
+        for lower, down in enumerate(spans):
+            own = packed[down, down]
+            flipped = own.T
+            even[down, down] = jnp.where(row <= column, own, flipped).astype(bf16)
+            above = jnp.where(row == column, 0.0, -flipped)
+            odd[down, down] = jnp.where(row > column, own, above).astype(bf16)
+            for over in spans[:lower]:
+                both, opposite = packed[over, down], packed[down, over]
+                even[down, over] = both.astype(bf16)
+                even[over, down] = both.T.astype(bf16)
+                odd[down, over] = opposite.astype(bf16)
+                odd[over, down] = -opposite.T.astype(bf16)
+
+    real = jnp.concatenate([trial[0] for trial in trials], 0)
+    imag = jnp.concatenate([trial[1] for trial in trials], 0)
     out_ref[:, 0, :] = (matmul(even[...], real) - matmul(odd[...], imag)).astype(bf16)
     out_ref[:, 1, :] = (matmul(even[...], imag) + matmul(odd[...], real)).astype(bf16)
 
 
-def update_waves(core, mine, others, trial):
-    _, bands, local_g = trial.shape
-    width = min(LANES, local_g)
+def update_waves(core, mine, others, trials):
+    _, share, local_g = trials[0].shape
+    count = len(trials)
+    bands = share * count
+    width = min(WIDE, local_g)
     return pl.pallas_call(
-        update_kernel,
+        functools.partial(update_kernel, count),
         grid=(local_g // width,),
         in_specs=[
             pl.BlockSpec(memory_space=pltpu.SMEM),
             pl.BlockSpec((bands // 2, bands), lambda step: (0, 0)),
             pl.BlockSpec((bands // 2, bands), lambda step: (0, 0)),
-            pl.BlockSpec((2, bands, width), lambda step: (0, 0, step)),
-        ],
+        ]
+        + [pl.BlockSpec((2, share, width), lambda step: (0, 0, step))] * count,
         out_specs=pl.BlockSpec((bands, 2, width), lambda step: (0, 0, step)),
         out_shape=jax.ShapeDtypeStruct((bands, 2, local_g), bf16),
         scratch_shapes=[pltpu.VMEM((bands, bands), bf16)] * 2,
-        compiler_params=pltpu.CompilerParams(vmem_limit_bytes=VMEM_BYTES),
+        compiler_params=pltpu.CompilerParams(vmem_limit_bytes=TAIL_VMEM_BYTES),
         cost_estimate=pl.CostEstimate(
             flops=8 * bands * bands * local_g,
             bytes_accessed=8 * bands * local_g,
             transcendentals=0,
         ),
-    )(core, mine, others, trial)
+    )(core, mine, others, *trials)
 
 
 def per_device(positions, weights, psi, vloc):
@@ -417,28 +556,23 @@
 
     weight_float = weights.astype(jnp.float32)
     mixing = weight_float / jnp.sum(weight_float, axis=1, keepdims=True)
-    own_oxygens = jnp.einsum("cj,jan->can", mixing, positions[:, :, 0::3], precision=highest)[0]
     count = 2 if bands // parts % (2 * GROUP) == 0 else 1
     share = bands // count
 
-    def outgoing(whole_psi, chunk):
-        block = whole_psi[0, chunk * share : (chunk + 1) * share]
-        return block.reshape(parts, share // parts, 2, local_g)
-
-    waves = [exchange(outgoing(psi, 0))]
-    later_psi, own_oxygens = lax.optimization_barrier((psi, own_oxygens))
-    later = [outgoing(later_psi, chunk) for chunk in range(1, count)]
-    waves[0], own_oxygens, *later = lax.optimization_barrier((waves[0], own_oxygens, *later))
-    everyone = exchange(jnp.broadcast_to(own_oxygens[None], (parts,) + own_oxygens.shape))
-    everyone, *later = lax.optimization_barrier((everyone, *later))
-    waves += [exchange(block) for block in later]
-    oxygens = jnp.swapaxes(everyone, 0, 1).reshape(3, WATERS)
+    sent = pack_first(positions, weights, psi, parts, share)
+    waves = [exchange(sent)]
+    for chunk in range(1, count):
+        block = psi[0, chunk * share : (chunk + 1) * share]
+        waves.append(exchange(block.reshape(parts, share // parts, 2, local_g)))
+    oxygens = unpack_oxygens(waves[0][:, share // parts :, 0, :], positions.shape[2])
     tables = transform_tables()
     in_plane, along = projector_tables(oxygens)
     grid_potential = vloc[0].reshape(NGRID, PLANE) * (1.0 / GVECS)
     potentials, forces = [], []
     for wave in waves:
-        moved, force = apply_hamiltonian(wave, tables, grid_potential, in_plane, along)
+        moved, force = apply_hamiltonian(
+            wave, share // parts, tables, grid_potential, in_plane, along
+        )
         potentials.append(exchange(moved).reshape(2 * share, local_g))
         forces.append(force)
     force_part = jnp.sum(sum(forces), axis=1) * (2.0 * occupation * nonlocal_strength / GVECS)
@@ -454,11 +588,9 @@
 
     chip, core = lax.axis_index("ga") // 2, lax.axis_index("ga") % 2
     chips = parts // 2
+    rows = bands // parts
     same_core = [[2 * number + which for number in range(chips)] for which in range(2)]
     core_ref = core.reshape(1).astype(jnp.int32)
-    trial, mine, others = make_trial(core_ref, kinetic, planes, potentials)
-    rows = bands // parts
-    pair = (mine + other_core(others, parts).astype(f32)).astype(bf16)
     near_chip = WATERS // chips
     pieces, left = [], force_part
     for _ in range(3):
@@ -466,8 +598,16 @@
         left = left - pieces[-1]
     pieces = jnp.swapaxes(jnp.stack(pieces).reshape(9, chips, near_chip), 0, 1)
     pieces = jnp.pad(pieces.reshape(chips, -1), ((0, 0), (0, GROUP * bands - 9 * near_chip)))
-    sent = [pair.reshape(chips, rows, bands), pieces.reshape(chips, GROUP, bands).astype(bf16)]
-    summed = jnp.sum(exchange(jnp.concatenate(sent, 1), same_core).astype(f32), axis=0)
+    pieces = pieces.reshape(chips, GROUP, bands)
+    trials, margin = [], None
+    for chunk, potential in enumerate(potentials):
+        before = trials[-1] if trials else None
+        trial, margin, *others = make_trial(
+            chunk, count, core_ref, kinetic, planes, potential, pieces, before, margin
+        )
+        trials.append(trial)
+    pair = (margin + other_core(others[0], parts).astype(f32)).astype(bf16)
+    summed = jnp.sum(exchange(pair, same_core).astype(f32), axis=0)
     summed, found = summed[:rows], summed[rows:].reshape(-1)[: 9 * near_chip]
     found = jnp.sum(found.reshape(3, 3, near_chip), axis=0)
     found = (found + other_core(found, parts)).reshape(3, 2, near_chip // 2)
@@ -478,7 +618,7 @@
     half_mixer = exchange(
         jnp.broadcast_to(own_mixer[None], (chips, rows, bands)), same_core
     ).reshape(bands // 2, bands)
-    psi_new = update_waves(core_ref, half_mixer, other_core(half_mixer, parts), trial)
+    psi_new = update_waves(core_ref, half_mixer, other_core(half_mixer, parts), trials)
 
     hydrogen_zero = jnp.zeros_like(oxygen_force)
     dft_force = jnp.stack([oxygen_force, hydrogen_zero, hydrogen_zero], axis=2).reshape(1, 3, -1)

time: 288 us -> 275 us (0.955)
  blocking collectives: 17.6 us -> 0 us
  starting transfers between devices: 49.6 us -> 56.9 us
  waiting for transfers between devices: 99.5 us -> 93.7 us
    all_to_all x1 -> x0, blocking collectives: 17.6 us -> none  [exchange(): lax.all_to_all(blocks, 'ga', split_axis=0, concat_axis=0, tiled=True, axi...]
    all_to_all x6, starting transfers between devices: 48.8 us -> 56 us  [exchange(): lax.all_to_all(blocks, 'ga', split_axis=0, concat_axis=0, tiled=True, axi...]
    all_to_all x6, waiting for transfers between devices: 97.1 us -> 91.7 us  [exchange(): lax.all_to_all(blocks, 'ga', split_axis=0, concat_axis=0, tiled=True, axi...]
    unnamed x24 -> x28, local copies, waits for them, and re-layouts: 7.73 us -> 11.1 us
    pallas_call x2 -> x4, Pallas kernels: 23.8 us -> 26.5 us  [the longest x2 14.2 us: make_trial(): pl.pallas_call(body, grid=(local_g // width,), in_specs=in_specs, out_spe...]
    slice x3 -> x5, local copies, waits for them, and re-layouts: 9 us -> 6.55 us  [the longest x1 4.39 us: per_device(): block = psi[0, chunk * share:(chunk + 1) * share]]
  transfers between devices with their start and end apart: 9 -> 9, of which waited for: 9 -> 9; matrix products, arithmetic and copies ran while one was open for 8% -> 9% of each run, Pallas kernels for 23% -> 26%
where the time goes in v3:
time: 275 us; the launch traced here: 274 us
  waiting for transfers between devices  93.7 us (34%)
  Pallas kernels  91.5 us (33%)
  starting transfers between devices  56.9 us (21%)
  local copies, waits for them, and re-layouts  21.1 us (8%)
  other arithmetic  9.34 us (3%)
    all_to_all x6, waiting for transfers between devices, exchange(): lax.all_to_all(blocks, 'ga', split_axis=0, concat_axis=0, tiled=True, axi...  91.7 us
    pallas_call x2, Pallas kernels, apply_hamiltonian(): pl.pallas_call(wave_kernel, grid=(steps,), in_specs=[pl.BlockSpec((parts,...  65 us
    all_to_all x6, starting transfers between devices, exchange(): lax.all_to_all(blocks, 'ga', split_axis=0, concat_axis=0, tiled=True, axi...  56 us
    pallas_call x2, Pallas kernels, make_trial(): pl.pallas_call(body, grid=(local_g // width,), in_specs=in_specs, out_spe...  14.2 us
    unnamed x28, local copies, waits for them, and re-layouts  11.1 us
    pallas_call x1, Pallas kernels, update_waves(): pl.pallas_call(functools.partial(update_kernel, count), grid=(local_g //...  8.91 us
  transfers between devices with their start and end apart: 9, of which 9 were waited for; matrix products, arithmetic and copies ran while one was open for 9% of the time, Pallas kernels for 26%

profile of v3, /device:TPU:0, one launch (start us, length us, event | category | flops | bytes accessed | tf_op | source)
XLA Modules:
  0.0 273.5 jit_solution(8016086965876000417)
XLA Ops:
  0.6 3.4 %shard_map.95 = bf16[16,17,2,2048]{3,2,1,0:T(2,128)(2,1)} custom-call(f32[3,32,48]{2,1,0:T(8,128)} %bitcast.49, s32[1,32]{1,0:T(1,128)} %weights_ref.1, bf16[1,512,2,2048]{3,2,1,0:T(2,128)(2,1)} %psi_ref.1), custom_call_target="tpu_custom_call" | custom-call | bytes 4194304 | tf_op jit(solution)/shard_map/pallas_call | solution.py:173
  4.0 7.4 %all-to-all-start.1 = ((bf16[16,17,2,2048]{3,2,1,0:T(2,128)(2,1)}), bf16[16,17,2,2048]{3,2,1,0:T(2,128)(2,1)S(1)}, u32[]{:S(2)}, u32[]{:S(2)}) async-start(bf16[16,17,2,2048]{3,2,1,0:T(2,128)(2,1)} %shard_map.95), calls=%async_computation.1 | async-start | bytes 4456448 | tf_op jit(solution)/shard_map/all_to_all | solution.py:71
  11.5 4.4 %slice.58 = bf16[1,256,2,2048]{3,2,1,0:T(2,128)(2,1)} slice(bf16[1,512,2,2048]{3,2,1,0:T(2,128)(2,1)} %psi_ref.1), slice={[0:1], [256:512], [0:2], [0:2048]} | slice | bytes 4194304 | tf_op jit(solution)/shard_map/slice | solution.py:565
  15.9 39.0 %all-to-all-done.1.wave_ref = bf16[16,17,2,2048]{3,2,1,0:T(2,128)(2,1)S(1)} async-done(((bf16[16,17,2,2048]{3,2,1,0:T(2,128)(2,1)}), bf16[16,17,2,2048]{3,2,1,0:T(2,128)(2,1)S(1)}, u32[]{:S(2)}, u32[]{:S(2)}) %all-to-all-start.1) | async-done | bytes 2228256 | tf_op jit(solution)/shard_map/all_to_all | solution.py:71
  54.8 11.8 %all-to-all-start = ((bf16[16,16,2,2048]{3,2,1,0:T(2,128)(2,1)}), bf16[16,16,2,2048]{3,2,1,0:T(2,128)(2,1)}, u32[]{:S(2)}, u32[]{:S(2)}) async-start(bf16[16,16,2,2048]{3,2,1,0:T(2,128)(2,1)} %bitcast.3), calls=%async_computation | async-start | bytes 4194304 | tf_op jit(solution)/shard_map/all_to_all | solution.py:71
  68.1 1.8 slice.61
  71.1 1.5 fusion.7
  73.1 1.9 pad_maximum_fusion.in_plane_ref
  74.9 32.5 %shard_map.97 = (bf16[16,2,16,2048]{3,2,1,0:T(8,128)(2,1)}, f32[3,8,256]{2,1,0:T(8,128)}) custom-call(bf16[16,17,2,2048]{3,2,1,0:T(2,128)(2,1)} %copy-done.2, bf16[1024,1024]{1,0:T(8,128)(2,1)} %constant.170.clone.cos_ref, bf16[1024,1024]{1,0:T(8,128)(2,1)} %constant.171.clone.sin_ref, bf16[512,1024]{1,0:T(8,128)(2,1)} %constant.172.clone.back_ref, ...), custom_call_target="tpu_custom_call" | custom-call | flops 16106127360 | bytes 16777216 | tf_op jit(solution)/shard_map/pallas_call | solution.py:338
  107.8 11.2 %all-to-all-start.3 = ((bf16[16,2,16,2048]{3,2,1,0:T(8,128)(2,1)}), bf16[16,2,16,2048]{3,2,1,0:T(8,128)(2,1)S(1)}, u32[]{:S(2)}, u32[]{:S(2)}) async-start(bf16[16,2,16,2048]{3,2,1,0:T(8,128)(2,1)} %get-tuple-element.14), calls=%async_computation.3 | async-start | bytes 4194304 | tf_op jit(solution)/shard_map/all_to_all | solution.py:71
  119.0 32.5 %shard_map.96 = (bf16[16,2,16,2048]{3,2,1,0:T(8,128)(2,1)}, f32[3,8,256]{2,1,0:T(8,128)}) custom-call(bf16[16,16,2,2048]{3,2,1,0:T(2,128)(2,1)} %all-to-all-done.wave_ref, bf16[1024,1024]{1,0:T(8,128)(2,1)} %constant.170.clone.cos_ref, bf16[1024,1024]{1,0:T(8,128)(2,1)} %constant.171.clone.sin_ref, bf16[512,1024]{1,0:T(8,128)(2,1)} %constant.172.clone.back_ref, ...), custom_call_target="tpu_custom_call" | custom-call | flops 16106127360 | bytes 16777216 | tf_op jit(solution)/shard_map/pallas_call | solution.py:338
  151.5 8.6 %all-to-all-done.3 = bf16[16,2,16,2048]{3,2,1,0:T(8,128)(2,1)S(1)} async-done(((bf16[16,2,16,2048]{3,2,1,0:T(8,128)(2,1)}), bf16[16,2,16,2048]{3,2,1,0:T(8,128)(2,1)S(1)}, u32[]{:S(2)}, u32[]{:S(2)}) %all-to-all-start.3) | async-done | bytes 2097184 | tf_op jit(solution)/shard_map/all_to_all | solution.py:71
  160.1 1.3 copy-done.1
  161.5 11.2 %all-to-all-start.2 = ((bf16[16,2,16,2048]{3,2,1,0:T(8,128)(2,1)}), bf16[16,2,16,2048]{3,2,1,0:T(8,128)(2,1)S(1)}, u32[]{:S(2)}, u32[]{:S(2)}) async-start(bf16[16,2,16,2048]{3,2,1,0:T(8,128)(2,1)} %get-tuple-element.11), calls=%async_computation.2 | async-start | bytes 4194304 | tf_op jit(solution)/shard_map/all_to_all | solution.py:71
  173.5 6.1 %copy.39 = bf16[1,512,2,2048]{3,1,2,0:T(8,128)(2,1)} copy(bf16[1,512,2,2048]{3,2,1,0:T(2,128)(2,1)} %psi_ref.1) | data formatting | bytes 8388608 | tf_op args[2]
  179.6 0.8 fusion.37.kinetic_ref
  180.6 0.7 copy.40
  181.4 6.2 %shard_map.98 = (bf16[2,256,2048]{2,1,0:T(8,128)(2,1)}, f32[256,256]{1,0:T(8,128)}) custom-call(s32[1]{0:T(128)} %bitcast.core_ref, f32[1,2048]{1,0:T(1,128)} %fusion.37.kinetic_ref, bf16[2,512,2048]{2,1,0:T(8,128)(2,1)} %bitcast.45, bf16[512,2048]{1,0:T(8,128)(2,1)} %bitcast.48), custom_call_target="tpu_custom_call" | custom-call | flops 1073741824 | bytes 6291456 | tf_op jit(solution)/shard_map/pallas_call | solution.py:473
  187.5 26.2 %all-to-all-done.2 = bf16[16,2,16,2048]{3,2,1,0:T(8,128)(2,1)S(1)} async-done(((bf16[16,2,16,2048]{3,2,1,0:T(8,128)(2,1)}), bf16[16,2,16,2048]{3,2,1,0:T(8,128)(2,1)S(1)}, u32[]{:S(2)}, u32[]{:S(2)}) %all-to-all-start.2) | async-done | bytes 2097184 | tf_op jit(solution)/shard_map/all_to_all | solution.py:71
  213.8 1.3 copy-done
  215.1 8.0 %shard_map.99 = (bf16[2,256,2048]{2,1,0:T(8,128)(2,1)}, f32[8,40,512]{2,1,0:T(8,128)}, bf16[8,40,512]{2,1,0:T(8,128)(2,1)}) custom-call(s32[1]{0:T(128)} %bitcast.core_ref, f32[1,2048]{1,0:T(1,128)} %fusion.37.kinetic_ref, bf16[2,512,2048]{2,1,0:T(8,128)(2,1)} %bitcast.46, bf16[512,2048]{1,0:T(8,128)(2,1)} %bitcast.47, f32[8,8,512]{2,1,0:T(8,128)} %bitcast.50, ...), custom_call_target="tpu_custom_call" | custom-call | flops 2147483648 | bytes 12582912 | tf_op jit(solution)/shard_map/pallas_call | solution.py:473
  223.1 0.8 collective-permute-start
  224.6 0.8 collective-permute-done
  225.4 1.9 add_convert_fusion
  227.3 10.7 %all-to-all-start.4 = ((bf16[8,40,512]{2,1,0:T(8,128)(2,1)}), bf16[8,40,512]{2,1,0:T(8,128)(2,1)S(1)}, u32[]{:S(2)}, u32[]{:S(2)}) async-start(bf16[8,40,512]{2,1,0:T(8,128)(2,1)} %add_convert_fusion), calls=%async_computation.4 | async-start | bytes 655360 | tf_op jit(solution)/shard_map/all_to_all | solution.py:71
  238.8 10.0 %all-to-all-done.4 = bf16[8,40,512]{2,1,0:T(8,128)(2,1)S(1)} async-done(((bf16[8,40,512]{2,1,0:T(8,128)(2,1)}), bf16[8,40,512]{2,1,0:T(8,128)(2,1)S(1)}, u32[]{:S(2)}, u32[]{:S(2)}) %all-to-all-start.4) | async-done | bytes 327712 | tf_op jit(solution)/shard_map/all_to_all | solution.py:71
  248.9 0.7 broadcast_in_dim.39
  249.6 3.6 %all-to-all-start.5 = ((bf16[8,32,512]{2,1,0:T(8,128)(2,1)}), bf16[8,32,512]{2,1,0:T(8,128)(2,1)S(1)}, u32[]{:S(2)}, u32[]{:S(2)}) async-start(bf16[8,32,512]{2,1,0:T(8,128)(2,1)} %broadcast_in_dim.39), calls=%async_computation.5 | async-start | bytes 524288 | tf_op jit(solution)/shard_map/all_to_all | solution.py:71
  254.0 0.8 collective-permute-done.2
  254.9 7.5 %all-to-all-done.5 = bf16[8,32,512]{2,1,0:T(8,128)(2,1)S(1)} async-done(((bf16[8,32,512]{2,1,0:T(8,128)(2,1)}), bf16[8,32,512]{2,1,0:T(8,128)(2,1)S(1)}, u32[]{:S(2)}, u32[]{:S(2)}) %all-to-all-start.5) | async-done | bytes 262176 | tf_op jit(solution)/shard_map/all_to_all | solution.py:71
  262.7 0.7 copy.31
  264.6 8.9 %shard_map.100 = bf16[512,2,2048]{2,1,0:T(2,128)(2,1)} custom-call(s32[1]{0:T(128)} %bitcast.core_ref, bf16[256,512]{1,0:T(8,128)(2,1)} %bitcast.53, bf16[256,512]{1,0:T(8,128)(2,1)} %copy-done.9, bf16[2,256,2048]{2,1,0:T(8,128)(2,1)} %get-tuple-element.15.refs_1_.refs_0_, bf16[2,256,2048]{2,1,0:T(8,128)(2,1)} %get-tuple-element.19.refs_1_), custom_call_target="tpu_custom_call" | custom-call | flops 4294967296 | bytes 8388608 | tf_op jit(solution)/shard_map/pallas_call | solution.py:531
  (80 shorter events, 8.2 us)
Async XLA Ops:
  4.0 50.8 %all-to-all-start.1 = ((bf16[16,17,2,2048]{3,2,1,0:T(2,128)(2,1)}), bf16[16,17,2,2048]{3,2,1,0:T(2,128)(2,1)S(1)}, u32[]{:S(2)}, u32[]{:S(2)}) async-start(bf16[16,17,2,2048]{3,2,1,0:T(2,128)(2,1)} %shard_map.95), calls=%async_computation.1 | async-start | bytes 4456448 | tf_op jit(solution)/shard_map/all_to_all | solution.py:71
  15.8 51.0 %copy-start.5 = (f32[1,32768]{1,0:T(1,128)S(1)}, f32[1,32768]{1,0:T(1,128)}, u32[]{:S(2)}) copy-start(f32[1,32768]{1,0:T(1,128)} %param.11) | copy-start | bytes 393220
  54.8 13.1 %copy-start.2 = (bf16[16,17,2,2048]{3,2,1,0:T(2,128)(2,1)}, bf16[16,17,2,2048]{3,2,1,0:T(2,128)(2,1)S(1)}, u32[]{:S(2)}) copy-start(bf16[16,17,2,2048]{3,2,1,0:T(2,128)(2,1)S(1)} %all-to-all-done.1.wave_ref) | copy-start | bytes 6684676
  54.8 53.0 %all-to-all-start = ((bf16[16,16,2,2048]{3,2,1,0:T(2,128)(2,1)}), bf16[16,16,2,2048]{3,2,1,0:T(2,128)(2,1)}, u32[]{:S(2)}, u32[]{:S(2)}) async-start(bf16[16,16,2,2048]{3,2,1,0:T(2,128)(2,1)} %bitcast.3), calls=%async_computation | async-start | bytes 4194304 | tf_op jit(solution)/shard_map/all_to_all | solution.py:71
  107.8 52.3 %all-to-all-start.3 = ((bf16[16,2,16,2048]{3,2,1,0:T(8,128)(2,1)}), bf16[16,2,16,2048]{3,2,1,0:T(8,128)(2,1)S(1)}, u32[]{:S(2)}, u32[]{:S(2)}) async-start(bf16[16,2,16,2048]{3,2,1,0:T(8,128)(2,1)} %get-tuple-element.14), calls=%async_computation.3 | async-start | bytes 4194304 | tf_op jit(solution)/shard_map/all_to_all | solution.py:71
  151.5 21.2 %copy-start.3 = (f32[32,3,48]{2,0,1:T(8,128)S(1)}, f32[32,3,48]{2,0,1:T(8,128)}, u32[]{:S(2)}) copy-start(f32[32,3,48]{2,0,1:T(8,128)} %param.8) | copy-start | bytes 55300
  160.1 1.3 copy-start.1
  161.5 52.3 %all-to-all-start.2 = ((bf16[16,2,16,2048]{3,2,1,0:T(8,128)(2,1)}), bf16[16,2,16,2048]{3,2,1,0:T(8,128)(2,1)S(1)}, u32[]{:S(2)}, u32[]{:S(2)}) async-start(bf16[16,2,16,2048]{3,2,1,0:T(8,128)(2,1)} %get-tuple-element.11), calls=%async_computation.2 | async-start | bytes 4194304 | tf_op jit(solution)/shard_map/all_to_all | solution.py:71
  173.5 6.9 %copy-start.6 = (f32[3,8,256]{2,1,0:T(8,128)S(1)}, f32[3,8,256]{2,1,0:T(8,128)}, u32[]{:S(2)}) copy-start(f32[3,8,256]{2,1,0:T(8,128)} %get-tuple-element.12) | copy-start | bytes 73732
  173.5 6.9 %copy-start.7 = (f32[3,8,256]{2,1,0:T(8,128)S(1)}, f32[3,8,256]{2,1,0:T(8,128)}, u32[]{:S(2)}) copy-start(f32[3,8,256]{2,1,0:T(8,128)} %get-tuple-element.13) | copy-start | bytes 73732
  213.8 1.3 copy-start
  215.1 8.8 %copy-start.8 = (s32[1,32]{1,0:T(1,128)S(1)}, s32[1,32]{1,0:T(1,128)}, u32[]{:S(2)}) copy-start(s32[1,32]{1,0:T(1,128)} %weights_ref.1) | copy-start | bytes 388
  223.1 2.3 collective-permute-start
  227.3 21.5 %all-to-all-start.4 = ((bf16[8,40,512]{2,1,0:T(8,128)(2,1)}), bf16[8,40,512]{2,1,0:T(8,128)(2,1)S(1)}, u32[]{:S(2)}, u32[]{:S(2)}) async-start(bf16[8,40,512]{2,1,0:T(8,128)(2,1)} %add_convert_fusion), calls=%async_computation.4 | async-start | bytes 655360 | tf_op jit(solution)/shard_map/all_to_all | solution.py:71
  249.6 12.7 %all-to-all-start.5 = ((bf16[8,32,512]{2,1,0:T(8,128)(2,1)}), bf16[8,32,512]{2,1,0:T(8,128)(2,1)S(1)}, u32[]{:S(2)}, u32[]{:S(2)}) async-start(bf16[8,32,512]{2,1,0:T(8,128)(2,1)} %broadcast_in_dim.39), calls=%async_computation.5 | async-start | bytes 524288 | tf_op jit(solution)/shard_map/all_to_all | solution.py:71
  253.6 1.2 collective-permute-start.2
  262.4 1.5 copy-start.4
  262.4 1.5 collective-permute-start.1
  263.9 0.7 copy-start.9

commit v4 on v3

--- a/solution.py
+++ b/solution.py
@@ -32,8 +32,10 @@
 SLAB = 128
 LANES = 256
 WIDE = 512
+TRIAL_WIDE = 2048
 VMEM_BYTES = 56 * 2**20
 TAIL_VMEM_BYTES = 60 * 2**20
+LAST_VMEM_BYTES = 28 * 2**20
 
 
 def frequency(index, count):
@@ -426,11 +428,11 @@
 
 
 def make_trial(chunk, count, core, kinetic, planes, potential, pieces, before, margin):
-    _, bands, local_g = planes.shape
+    _, share, local_g = planes.shape
     chips = pieces.shape[0]
-    share = bands // count
+    bands = share * count
     first, last = chunk == 0, chunk == count - 1
-    width = min(WIDE, local_g)
+    width = min(TRIAL_WIDE, local_g)
     deep = lambda step: (0, 0, step)
     if last:
         rows = bands // (2 * chips) + GROUP
@@ -446,7 +448,7 @@
     in_specs = [
         pl.BlockSpec(memory_space=pltpu.SMEM),
         pl.BlockSpec((1, width), lambda step: (0, step)),
-        pl.BlockSpec((2, share, width), lambda step: (0, chunk, step)),
+        pl.BlockSpec((2, share, width), deep),
         pl.BlockSpec((2 * share, width), lambda step: (0, step)),
     ]
     if last:
@@ -481,7 +483,7 @@
             pltpu.VMEM((share, seen), f32),
             pltpu.VMEM((bands, bands), f32),
         ],
-        compiler_params=pltpu.CompilerParams(vmem_limit_bytes=TAIL_VMEM_BYTES),
+        compiler_params=pltpu.CompilerParams(vmem_limit_bytes=LAST_VMEM_BYTES),
         cost_estimate=pl.CostEstimate(
             flops=8 * share * seen * local_g,
             bytes_accessed=12 * seen * local_g,
@@ -540,7 +542,7 @@
         out_specs=pl.BlockSpec((bands, 2, width), lambda step: (0, 0, step)),
         out_shape=jax.ShapeDtypeStruct((bands, 2, local_g), bf16),
         scratch_shapes=[pltpu.VMEM((bands, bands), bf16)] * 2,
-        compiler_params=pltpu.CompilerParams(vmem_limit_bytes=TAIL_VMEM_BYTES),
+        compiler_params=pltpu.CompilerParams(vmem_limit_bytes=LAST_VMEM_BYTES),
         cost_estimate=pl.CostEstimate(
             flops=8 * bands * bands * local_g,
             bytes_accessed=8 * bands * local_g,
@@ -584,7 +586,9 @@
         + frequency(flat_index % NGRID, NGRID) ** 2
     )
     kinetic = (0.5 * square)[None]
-    planes = jnp.swapaxes(psi[0], 0, 1)
+    planes = [
+        jnp.swapaxes(psi[0, chunk * share : (chunk + 1) * share], 0, 1) for chunk in range(count)
+    ]
 
     chip, core = lax.axis_index("ga") // 2, lax.axis_index("ga") % 2
     chips = parts // 2
@@ -603,7 +607,7 @@
     for chunk, potential in enumerate(potentials):
         before = trials[-1] if trials else None
         trial, margin, *others = make_trial(
-            chunk, count, core_ref, kinetic, planes, potential, pieces, before, margin
+            chunk, count, core_ref, kinetic, planes[chunk], potential, pieces, before, margin
         )
         trials.append(trial)
     pair = (margin + other_core(others[0], parts).astype(f32)).astype(bf16)

time: 275 us -> 270 us (0.982)
  Pallas kernels: 91.5 us -> 83.7 us
  local copies, waits for them, and re-layouts: 21.1 us -> 28.8 us
  waiting for transfers between devices: 93.7 us -> 90.9 us
    pallas_call x2, Pallas kernels: 14.2 us -> 7.4 us  [make_trial(): pl.pallas_call(body, grid=(local_g // width,), in_specs=in_specs, out_spe...]
    another operation x1 -> x2, local copies, waits for them, and re-layouts: 0.09 us -> 3.62 us  [the longest x1 3.53 us: per_device(): waves.append(exchange(block.reshape(parts, share // parts, 2, local_g)))]
    unnamed x28 -> x31, local copies, waits for them, and re-layouts: 11.1 us -> 13.1 us
  transfers between devices with their start and end apart: 9 -> 9, of which waited for: 9 -> 8; matrix products, arithmetic and copies ran while one was open for 9% -> 10% of each run, Pallas kernels for 26% -> 25%
where the time goes in v4:
time: 270 us; the launch traced here: 269 us
  waiting for transfers between devices  90.9 us (34%)
  Pallas kernels  83.7 us (31%)
  starting transfers between devices  56.5 us (21%)
  local copies, waits for them, and re-layouts  28.8 us (11%)
  other arithmetic  7.81 us (3%)
    all_to_all x6, waiting for transfers between devices, exchange(): lax.all_to_all(blocks, 'ga', split_axis=0, concat_axis=0, tiled=True, axi...  89 us
    pallas_call x2, Pallas kernels, apply_hamiltonian(): pl.pallas_call(wave_kernel, grid=(steps,), in_specs=[pl.BlockSpec((parts,...  65.1 us
    all_to_all x6, starting transfers between devices, exchange(): lax.all_to_all(blocks, 'ga', split_axis=0, concat_axis=0, tiled=True, axi...  55.7 us
    unnamed x31, local copies, waits for them, and re-layouts  13.1 us
    pallas_call x1, Pallas kernels, update_waves(): pl.pallas_call(functools.partial(update_kernel, count), grid=(local_g //...  7.83 us
    pallas_call x2, Pallas kernels, make_trial(): pl.pallas_call(body, grid=(local_g // width,), in_specs=in_specs, out_spe...  7.4 us
    slice x1, local copies, waits for them, and re-layouts, per_device(): psi[0, chunk * share:(chunk + 1) * share]  5.67 us
  transfers between devices with their start and end apart: 9, of which 8 were waited for; matrix products, arithmetic and copies ran while one was open for 10% of the time, Pallas kernels for 25%

profile of v4, /device:TPU:0, one launch (start us, length us, event | category | flops | bytes accessed | tf_op | source)
XLA Modules:
  0.0 268.8 jit_solution(18137644410371051459)
XLA Ops:
  0.6 3.4 %shard_map.95 = bf16[16,17,2,2048]{3,2,1,0:T(2,128)(2,1)} custom-call(f32[3,32,48]{2,1,0:T(8,128)} %bitcast.55, s32[1,32]{1,0:T(1,128)} %weights_ref.1, bf16[1,512,2,2048]{3,2,1,0:T(2,128)(2,1)} %psi_ref.1), custom_call_target="tpu_custom_call" | custom-call | bytes 4194304 | tf_op jit(solution)/shard_map/pallas_call | solution.py:175
  4.0 7.4 %all-to-all-start.1 = ((bf16[16,17,2,2048]{3,2,1,0:T(2,128)(2,1)}), bf16[16,17,2,2048]{3,2,1,0:T(2,128)(2,1)}, u32[]{:S(2)}, u32[]{:S(2)}) async-start(bf16[16,17,2,2048]{3,2,1,0:T(2,128)(2,1)} %shard_map.95), calls=%async_computation.1 | async-start | bytes 4456448 | tf_op jit(solution)/shard_map/all_to_all | solution.py:73
  11.5 5.7 %fusion.42 = (bf16[1,256,2,2048]{3,2,1,0:T(2,128)(2,1)}, bf16[1,256,2,2048]{3,2,1,0:T(2,128)(2,1)S(1)}) fusion(bf16[1,512,2,2048]{3,2,1,0:T(2,128)(2,1)} %psi_ref.1), kind=kLoop, calls=%fused_computation.116 | loop fusion | bytes 8388608 | tf_op jit(solution)/shard_map/slice | solution.py:590
  17.2 0.9 copy.52
  18.1 3.5 %copy.27 = bf16[16,16,2,2048]{3,2,1,0:T(2,128)(2,1)} copy(bf16[16,16,2,2048]{3,1,0,2:T(8,128)(2,1)S(1)} %bitcast.49) | data formatting | bytes 4194304 | tf_op jit(solution)/shard_map/reshape;squeeze | solution.py:568
  21.6 33.4 %all-to-all-done.1.wave_ref = bf16[16,17,2,2048]{3,2,1,0:T(2,128)(2,1)} async-done(((bf16[16,17,2,2048]{3,2,1,0:T(2,128)(2,1)}), bf16[16,17,2,2048]{3,2,1,0:T(2,128)(2,1)}, u32[]{:S(2)}, u32[]{:S(2)}) %all-to-all-start.1) | async-done | bytes 2228256 | tf_op jit(solution)/shard_map/all_to_all | solution.py:73
  54.9 11.8 %all-to-all-start = ((bf16[16,16,2,2048]{3,2,1,0:T(2,128)(2,1)}), bf16[16,16,2,2048]{3,2,1,0:T(2,128)(2,1)}, u32[]{:S(2)}, u32[]{:S(2)}) async-start(bf16[16,16,2,2048]{3,2,1,0:T(2,128)(2,1)} %copy.27), calls=%async_computation | async-start | bytes 4194304 | tf_op jit(solution)/shard_map/all_to_all | solution.py:73
  68.0 1.0 slice.80
  69.1 1.8 slice.65
  72.1 1.5 fusion.7
  74.1 1.9 pad_maximum_fusion.in_plane_ref
  76.0 32.5 %shard_map.97 = (bf16[16,2,16,2048]{3,2,1,0:T(8,128)(2,1)}, f32[3,8,256]{2,1,0:T(8,128)}) custom-call(bf16[16,17,2,2048]{3,2,1,0:T(2,128)(2,1)} %all-to-all-done.1.wave_ref, bf16[1024,1024]{1,0:T(8,128)(2,1)} %constant.170.clone.cos_ref, bf16[1024,1024]{1,0:T(8,128)(2,1)} %constant.171.clone.sin_ref, bf16[512,1024]{1,0:T(8,128)(2,1)} %constant.172.clone.back_ref, ...), custom_call_target="tpu_custom_call" | custom-call | flops 16106127360 | bytes 16777216 | tf_op jit(solution)/shard_map/pallas_call | solution.py:340
  108.5 10.7 %all-to-all-start.3 = ((bf16[16,2,16,2048]{3,2,1,0:T(8,128)(2,1)}), bf16[16,2,16,2048]{3,2,1,0:T(8,128)(2,1)}, u32[]{:S(2)}, u32[]{:S(2)}) async-start(bf16[16,2,16,2048]{3,2,1,0:T(8,128)(2,1)} %get-tuple-element.14), calls=%async_computation.3 | async-start | bytes 4194304 | tf_op jit(solution)/shard_map/all_to_all | solution.py:73
  119.2 32.5 %shard_map.96 = (bf16[16,2,16,2048]{3,2,1,0:T(8,128)(2,1)}, f32[3,8,256]{2,1,0:T(8,128)}) custom-call(bf16[16,16,2,2048]{3,2,1,0:T(2,128)(2,1)} %all-to-all-done.wave_ref, bf16[1024,1024]{1,0:T(8,128)(2,1)} %constant.170.clone.cos_ref, bf16[1024,1024]{1,0:T(8,128)(2,1)} %constant.171.clone.sin_ref, bf16[512,1024]{1,0:T(8,128)(2,1)} %constant.172.clone.back_ref, ...), custom_call_target="tpu_custom_call" | custom-call | flops 16106127360 | bytes 16777216 | tf_op jit(solution)/shard_map/pallas_call | solution.py:340
  151.7 8.6 %all-to-all-done.3 = bf16[16,2,16,2048]{3,2,1,0:T(8,128)(2,1)} async-done(((bf16[16,2,16,2048]{3,2,1,0:T(8,128)(2,1)}), bf16[16,2,16,2048]{3,2,1,0:T(8,128)(2,1)}, u32[]{:S(2)}, u32[]{:S(2)}) %all-to-all-start.3) | async-done | bytes 2097184 | tf_op jit(solution)/shard_map/all_to_all | solution.py:73
  160.3 11.4 %all-to-all-start.2 = ((bf16[16,2,16,2048]{3,2,1,0:T(8,128)(2,1)}), bf16[16,2,16,2048]{3,2,1,0:T(8,128)(2,1)}, u32[]{:S(2)}, u32[]{:S(2)}) async-start(bf16[16,2,16,2048]{3,2,1,0:T(8,128)(2,1)} %get-tuple-element.11), calls=%async_computation.2 | async-start | bytes 4194304 | tf_op jit(solution)/shard_map/all_to_all | solution.py:73
  172.6 3.8 %copy.49 = bf16[1,256,2,2048]{3,1,2,0:T(8,128)(2,1)} copy(bf16[1,256,2,2048]{3,2,1,0:T(2,128)(2,1)} %get-tuple-element.31) | data formatting | bytes 4194304
  177.0 1.6 copy-done
  178.5 3.3 %shard_map.98 = (bf16[2,256,2048]{2,1,0:T(8,128)(2,1)S(1)}, f32[256,256]{1,0:T(8,128)S(1)}) custom-call(s32[1]{0:T(128)} %bitcast.core_ref, f32[1,2048]{1,0:T(1,128)S(1)} %fusion.37.kinetic_ref, bf16[2,256,2048]{2,1,0:T(8,128)(2,1)S(1)} %bitcast.51, bf16[512,2048]{1,0:T(8,128)(2,1)} %bitcast.11.potential_ref), custom_call_target="tpu_custom_call" | custom-call | flops 1073741824 | bytes 6291456 | tf_op jit(solution)/shard_map/pallas_call | solution.py:475
  181.9 1.3 copy-done.1
  183.2 29.7 %all-to-all-done.2 = bf16[16,2,16,2048]{3,2,1,0:T(8,128)(2,1)} async-done(((bf16[16,2,16,2048]{3,2,1,0:T(8,128)(2,1)}), bf16[16,2,16,2048]{3,2,1,0:T(8,128)(2,1)}, u32[]{:S(2)}, u32[]{:S(2)}) %all-to-all-start.2) | async-done | bytes 2097184 | tf_op jit(solution)/shard_map/all_to_all | solution.py:73
  212.9 1.6 copy-done.2
  214.5 4.1 %shard_map.99 = (bf16[2,256,2048]{2,1,0:T(8,128)(2,1)S(1)}, f32[8,40,512]{2,1,0:T(8,128)S(1)}, bf16[8,40,512]{2,1,0:T(8,128)(2,1)S(1)}) custom-call(s32[1]{0:T(128)} %bitcast.core_ref, f32[1,2048]{1,0:T(1,128)S(1)} %fusion.37.kinetic_ref, bf16[2,256,2048]{2,1,0:T(8,128)(2,1)S(1)} %bitcast.50, bf16[512,2048]{1,0:T(8,128)(2,1)} %bitcast.6.potential_ref, ...), custom_call_target="tpu_custom_call" | custom-call | flops 2147483648 | bytes 12582912 | tf_op jit(solution)/shard_map/pallas_call | solution.py:475
  218.6 1.3 copy-done.4
  222.0 0.8 add_convert_fusion
  222.8 10.7 %all-to-all-start.4 = ((bf16[8,40,512]{2,1,0:T(8,128)(2,1)}), bf16[8,40,512]{2,1,0:T(8,128)(2,1)S(1)}, u32[]{:S(2)}, u32[]{:S(2)}) async-start(bf16[8,40,512]{2,1,0:T(8,128)(2,1)} %add_convert_fusion), calls=%async_computation.4 | async-start | bytes 655360 | tf_op jit(solution)/shard_map/all_to_all | solution.py:73
  233.5 0.8 divide_bitcast_fusion
  234.4 9.8 %all-to-all-done.4 = bf16[8,40,512]{2,1,0:T(8,128)(2,1)S(1)} async-done(((bf16[8,40,512]{2,1,0:T(8,128)(2,1)}), bf16[8,40,512]{2,1,0:T(8,128)(2,1)S(1)}, u32[]{:S(2)}, u32[]{:S(2)}) %all-to-all-start.4) | async-done | bytes 327712 | tf_op jit(solution)/shard_map/all_to_all | solution.py:73
  245.1 3.6 %all-to-all-start.5 = ((bf16[8,32,512]{2,1,0:T(8,128)(2,1)}), bf16[8,32,512]{2,1,0:T(8,128)(2,1)S(1)}, u32[]{:S(2)}, u32[]{:S(2)}) async-start(bf16[8,32,512]{2,1,0:T(8,128)(2,1)} %broadcast_in_dim.39), calls=%async_computation.5 | async-start | bytes 524288 | tf_op jit(solution)/shard_map/all_to_all | solution.py:73
  250.3 7.5 %all-to-all-done.5 = bf16[8,32,512]{2,1,0:T(8,128)(2,1)S(1)} async-done(((bf16[8,32,512]{2,1,0:T(8,128)(2,1)}), bf16[8,32,512]{2,1,0:T(8,128)(2,1)S(1)}, u32[]{:S(2)}, u32[]{:S(2)}) %all-to-all-start.5) | async-done | bytes 262176 | tf_op jit(solution)/shard_map/all_to_all | solution.py:73
  259.3 1.6 copy-done.5
  260.9 7.8 %shard_map.100 = bf16[512,2,2048]{2,1,0:T(2,128)(2,1)} custom-call(s32[1]{0:T(128)} %bitcast.core_ref, bf16[256,512]{1,0:T(8,128)(2,1)S(1)} %bitcast.53, bf16[256,512]{1,0:T(8,128)(2,1)S(1)} %collective-permute-done.1.other_ref, bf16[2,256,2048]{2,1,0:T(8,128)(2,1)S(1)} %copy-done.3, bf16[2,256,2048]{2,1,0:T(8,128)(2,1)S(1)} %copy-done.5), custom_call_target="tpu_custom_call" | custom-call | flops 4294967296 | bytes 8388608 | tf_op jit(solution)/shard_map/pallas_call | solution.py:533
  (84 shorter events, 10.3 us)
Async XLA Ops:
  4.0 50.9 %all-to-all-start.1 = ((bf16[16,17,2,2048]{3,2,1,0:T(2,128)(2,1)}), bf16[16,17,2,2048]{3,2,1,0:T(2,128)(2,1)}, u32[]{:S(2)}, u32[]{:S(2)}) async-start(bf16[16,17,2,2048]{3,2,1,0:T(2,128)(2,1)} %shard_map.95), calls=%async_computation.1 | async-start | bytes 4456448 | tf_op jit(solution)/shard_map/all_to_all | solution.py:73
  21.6 45.4 %copy-start.7 = (f32[1,32768]{1,0:T(1,128)S(1)}, f32[1,32768]{1,0:T(1,128)}, u32[]{:S(2)}) copy-start(f32[1,32768]{1,0:T(1,128)} %param.11) | copy-start | bytes 393220
  54.9 53.5 %all-to-all-start = ((bf16[16,16,2,2048]{3,2,1,0:T(2,128)(2,1)}), bf16[16,16,2,2048]{3,2,1,0:T(2,128)(2,1)}, u32[]{:S(2)}, u32[]{:S(2)}) async-start(bf16[16,16,2,2048]{3,2,1,0:T(2,128)(2,1)} %copy.27), calls=%async_computation | async-start | bytes 4194304 | tf_op jit(solution)/shard_map/all_to_all | solution.py:73
  108.5 51.9 %all-to-all-start.3 = ((bf16[16,2,16,2048]{3,2,1,0:T(8,128)(2,1)}), bf16[16,2,16,2048]{3,2,1,0:T(8,128)(2,1)}, u32[]{:S(2)}, u32[]{:S(2)}) async-start(bf16[16,2,16,2048]{3,2,1,0:T(8,128)(2,1)} %get-tuple-element.14), calls=%async_computation.3 | async-start | bytes 4194304 | tf_op jit(solution)/shard_map/all_to_all | solution.py:73
  160.3 11.4 %copy-start.6 = (f32[32,3,48]{2,0,1:T(8,128)S(1)}, f32[32,3,48]{2,0,1:T(8,128)}, u32[]{:S(2)}) copy-start(f32[32,3,48]{2,0,1:T(8,128)} %param.8) | copy-start | bytes 55300
  160.3 52.6 %all-to-all-start.2 = ((bf16[16,2,16,2048]{3,2,1,0:T(8,128)(2,1)}), bf16[16,2,16,2048]{3,2,1,0:T(8,128)(2,1)}, u32[]{:S(2)}, u32[]{:S(2)}) async-start(bf16[16,2,16,2048]{3,2,1,0:T(8,128)(2,1)} %get-tuple-element.11), calls=%async_computation.2 | async-start | bytes 4194304 | tf_op jit(solution)/shard_map/all_to_all | solution.py:73
  172.6 4.0 %copy-start.8 = (f32[3,8,256]{2,1,0:T(8,128)S(1)}, f32[3,8,256]{2,1,0:T(8,128)}, u32[]{:S(2)}) copy-start(f32[3,8,256]{2,1,0:T(8,128)} %get-tuple-element.12) | copy-start | bytes 73732
  172.6 4.0 %copy-start.9 = (f32[3,8,256]{2,1,0:T(8,128)S(1)}, f32[3,8,256]{2,1,0:T(8,128)}, u32[]{:S(2)}) copy-start(f32[3,8,256]{2,1,0:T(8,128)} %get-tuple-element.13) | copy-start | bytes 73732
  176.9 1.6 copy-start
  181.9 1.3 copy-start.1
  212.9 1.6 copy-start.2
  214.5 6.2 %copy-start.10 = (s32[1,32]{1,0:T(1,128)S(1)}, s32[1,32]{1,0:T(1,128)}, u32[]{:S(2)}) copy-start(s32[1,32]{1,0:T(1,128)} %weights_ref.1) | copy-start | bytes 388
  218.6 1.3 copy-start.4
  219.9 2.0 collective-permute-start
  222.8 21.4 %all-to-all-start.4 = ((bf16[8,40,512]{2,1,0:T(8,128)(2,1)}), bf16[8,40,512]{2,1,0:T(8,128)(2,1)S(1)}, u32[]{:S(2)}, u32[]{:S(2)}) async-start(bf16[8,40,512]{2,1,0:T(8,128)(2,1)} %add_convert_fusion), calls=%async_computation.4 | async-start | bytes 655360 | tf_op jit(solution)/shard_map/all_to_all | solution.py:73
  233.5 25.9 %copy-start.3 = (bf16[2,256,2048]{2,1,0:T(8,128)(2,1)S(1)}, bf16[2,256,2048]{2,1,0:T(8,128)(2,1)}, u32[]{:S(2)}) copy-start(bf16[2,256,2048]{2,1,0:T(8,128)(2,1)} %copy-done.1) | copy-start | bytes 6291460
  245.1 12.7 %all-to-all-start.5 = ((bf16[8,32,512]{2,1,0:T(8,128)(2,1)}), bf16[8,32,512]{2,1,0:T(8,128)(2,1)S(1)}, u32[]{:S(2)}, u32[]{:S(2)}) async-start(bf16[8,32,512]{2,1,0:T(8,128)(2,1)} %broadcast_in_dim.39), calls=%async_computation.5 | async-start | bytes 524288 | tf_op jit(solution)/shard_map/all_to_all | solution.py:73
  249.0 1.2 collective-permute-start.2
  257.8 1.5 collective-permute-start.1
  259.3 1.6 copy-start.5

commit v5 on v4

--- a/solution.py
+++ b/solution.py
@@ -32,7 +32,6 @@
 SLAB = 128
 LANES = 256
 WIDE = 512
-TRIAL_WIDE = 2048
 VMEM_BYTES = 56 * 2**20
 TAIL_VMEM_BYTES = 60 * 2**20
 LAST_VMEM_BYTES = 28 * 2**20
@@ -100,9 +99,11 @@
     on_sine = spread(mixed(-sine, -cosine, cosine, -sine), "xcbymd")
     backward = np.concatenate([on_cosine, on_sine], 1)
     forward = spread(mixed(cosine, sine, -sine, cosine), "xcbydm")
+    still, none = np.eye(NGRID), np.zeros((NGRID, NGRID))
+    order = spread(mixed(still, none, none, still), "xcbymd")
     return [
         jnp.asarray(table.astype(np.float32), dtype=bf16)
-        for table in (np.cos(angle), np.sin(angle), backward, forward)
+        for table in (np.cos(angle), np.sin(angle), backward, forward, order)
     ]
 
 
@@ -223,7 +224,9 @@
     sin_ref,
     back_ref,
     fore_ref,
+    order_ref,
     pot_ref,
+    kept_ref,
     in_plane_ref,
     along_ref,
     out_ref,
@@ -233,6 +236,7 @@
     turned,
     sums,
     pulls,
+    kinetic,
 ):
     parts, local_g = wave_ref.shape[0], wave_ref.shape[3]
     waters = along_ref.shape[2]
@@ -290,8 +294,9 @@
             force_ref[axis, :, inside] += proj_re * slope_im - proj_im * slope_re
 
         cosines, sines = factors[:2]
-        pull_re = nonlocal_strength * (cosines * proj_re[None] + sines * proj_im[None])
-        pull_im = nonlocal_strength * (cosines * proj_im[None] - sines * proj_re[None])
+        strength = step_size * nonlocal_strength
+        pull_re = strength * (cosines * proj_re[None] + sines * proj_im[None])
+        pull_im = strength * (cosines * proj_im[None] - sines * proj_re[None])
         for half, pull in enumerate(((pull_re, pull_im), (pull_im, -pull_re))):
             both = jnp.concatenate(pull, 1).reshape(all_rows, SLAB).astype(bf16)
             start = half * waters + slab * SLAB
@@ -302,6 +307,8 @@
         columns = pl.ds(pl.multiple_of(step * LANES, LANES), LANES)
         planes[:all_rows, columns] = matmul(rows[...], cos_ref[:, columns]).astype(bf16)
         planes[all_rows:, columns] = matmul(rows[...], sin_ref[:, columns]).astype(bf16)
+        moved = matmul(order_ref[...], rows[:, columns]).reshape(NGRID, band_rows, LANES)
+        kinetic[:, columns] = (moved * kept_ref[:, columns][:, None, :]).reshape(all_rows, LANES)
 
     @pl.loop(0, PLANE // LANES)
     def _(step):
@@ -320,7 +327,7 @@
         columns = pl.ds(pl.multiple_of(step * LANES, LANES), LANES)
         waves = matmul(turned[...], cos_ref[:, columns]) + matmul(rows[...], sin_ref[:, columns])
         waves += matmul(pulls[...], in_plane_ref[: 2 * waters, columns])
-        planes[:all_rows, columns] = waves.astype(bf16)
+        planes[:all_rows, columns] = (kinetic[:, columns] - waves).astype(bf16)
 
     for start in range(0, NGRID * PLANE, piece):
         owner, offset = start // local_g, start % local_g
@@ -330,7 +337,7 @@
         ]
 
 
-def apply_hamiltonian(waves, band_count, tables, grid_potential, in_plane, along):
+def make_trial(waves, band_count, tables, grid_potential, kept, in_plane, along):
     parts, _, _, local_g = waves.shape
     waters = along.shape[2]
     steps = band_count // GROUP
@@ -346,6 +353,8 @@
             pl.BlockSpec((PLANE, PLANE), whole),
             pl.BlockSpec((all_rows, 2 * all_rows), whole),
             pl.BlockSpec((all_rows, all_rows), whole),
+            pl.BlockSpec((all_rows, all_rows), whole),
+            pl.BlockSpec((NGRID, PLANE), whole),
             pl.BlockSpec((NGRID, PLANE), whole),
             pl.BlockSpec((6 * waters, PLANE), whole),
             pl.BlockSpec((4, NGRID, waters), lambda step: (0, 0, 0)),
@@ -364,129 +373,86 @@
             pltpu.VMEM((all_rows, PLANE), bf16),
             pltpu.VMEM((6 * waters // SLAB, all_rows, SLAB), f32),
             pltpu.VMEM((all_rows, 2 * waters), bf16),
+            pltpu.VMEM((all_rows, PLANE), f32),
         ],
         compiler_params=pltpu.CompilerParams(vmem_limit_bytes=VMEM_BYTES),
         cost_estimate=pl.CostEstimate(
-            flops=steps * 2 * all_rows * PLANE * (4 * PLANE + 3 * all_rows + 8 * waters),
+            flops=steps * 2 * all_rows * PLANE * (4 * PLANE + 4 * all_rows + 8 * waters),
             bytes_accessed=8 * steps * band_rows * parts * local_g + 8 * PLANE * PLANE,
             transcendentals=0,
         ),
-    )(waves, *tables, grid_potential, in_plane, along)
-
-
-def trial_kernel(
-    first, last, core_ref, kinetic_ref, wave_ref, potential_ref, pieces_ref, before_ref,
-    margin_ref, trial_ref, mine_ref, other_ref, even, odd, packed,
-):
-    step = pl.program_id(0)
-    share, width = wave_ref.shape[1:]
-    kept = 1.0 - step_size * kinetic_ref[...]
-    block = potential_ref[...].astype(f32) * step_size
-    block = block.reshape(share // GROUP, 2, GROUP, width)
-    for half in range(2):
-        taken = block[:, half].reshape(share, width)
-        trial_ref[half] = (wave_ref[half].astype(f32) * kept - taken).astype(bf16)
-    real, imag = trial_ref[0], trial_ref[1]
-    if first:
-        all_real, all_imag = real, imag
-    else:
-        all_real = jnp.concatenate([before_ref[0], real], 0)
-        all_imag = jnp.concatenate([before_ref[1], imag], 0)
-
-    @pl.when(step == 0)
-    def _():
-        even[...] = jnp.zeros_like(even)
-        odd[...] = jnp.zeros_like(odd)
-
-    even[...] += inner(real, all_real) + inner(imag, all_imag)
-    odd[...] += inner(imag, all_real) - inner(real, all_imag)
-
-    @pl.when(step == pl.num_programs(0) - 1)
-    def _():
-        start = even.shape[1] - share
-        row = lax.broadcasted_iota(jnp.int32, (share, share), 0)
-        column = lax.broadcasted_iota(jnp.int32, (share, share), 1)
-        own = jnp.where(row <= column, even[:, start:], odd[:, start:]) * (1.0 / GVECS)
-        if not last:
-            mine_ref[...] = own
-        else:
-            packed[start:, start:] = own
-            if not first:
-                packed[:start, :start] = margin_ref[...]
-                packed[start:, :start] = odd[:, :start] * (1.0 / GVECS)
-                packed[:start, start:] = even[:, :start] * (1.0 / GVECS)
-            chips, rows, bands = mine_ref.shape
-            rows -= GROUP
-            half = chips * rows
-            core = core_ref[0]
-            mine = packed[pl.ds(pl.multiple_of(core * half, half), half), :]
-            others = packed[pl.ds(pl.multiple_of((1 - core) * half, half), half), :]
-            mine_ref[:, :rows, :] = mine.reshape(chips, rows, bands)
-            mine_ref[:, rows:, :] = pieces_ref[...]
-            other_ref[:, :rows, :] = others.reshape(chips, rows, bands).astype(bf16)
-            other_ref[:, rows:, :] = jnp.zeros((chips, GROUP, bands), bf16)
-
-
-def make_trial(chunk, count, core, kinetic, planes, potential, pieces, before, margin):
-    _, share, local_g = planes.shape
+    )(waves, *tables, grid_potential, kept, in_plane, along)
+
+
+def split_rows(block):
+    count, width = block.shape
+    block = block.astype(f32).reshape(count // (2 * GROUP), 2, GROUP, width)
+    return [block[:, half].reshape(count // 2, width).astype(bf16) for half in range(2)]
+
+
+def margin_kernel(first, last, core_ref, trial_ref, *refs):
+    refs = list(refs)
+    pieces_ref = refs.pop(0) if last else None
+    before_ref, margin_ref = (None, None) if first else (refs.pop(0), refs.pop(0))
+    mine_ref = refs.pop(0)
+    real, imag = split_rows(trial_ref[...])
+    share = real.shape[0]
+
+    def margins(other_real, other_imag):
+        even = inner(real, other_real) + inner(imag, other_imag)
+        odd = inner(imag, other_real) - inner(real, other_imag)
+        return even * (1.0 / GVECS), odd * (1.0 / GVECS)
+
+    even, odd = margins(real, imag)
+    row = lax.broadcasted_iota(jnp.int32, (share, share), 0)
+    column = lax.broadcasted_iota(jnp.int32, (share, share), 1)
+    own = jnp.where(row <= column, even, odd)
+    if not last:
+        mine_ref[...] = own
+        return
+    other_ref, packed = refs
+    start = packed.shape[0] - share
+    packed[start:, start:] = own
+    if not first:
+        even, odd = margins(*split_rows(before_ref[...]))
+        packed[:start, :start] = margin_ref[...]
+        packed[start:, :start] = odd
+        packed[:start, start:] = even
+    chips, rows, bands = mine_ref.shape
+    rows -= GROUP
+    half = chips * rows
+    core = core_ref[0]
+    mine = packed[pl.ds(pl.multiple_of(core * half, half), half), :]
+    others = packed[pl.ds(pl.multiple_of((1 - core) * half, half), half), :]
+    mine_ref[:, :rows, :] = mine.reshape(chips, rows, bands)
+    mine_ref[:, rows:, :] = pieces_ref[...]
+    other_ref[:, :rows, :] = others.reshape(chips, rows, bands).astype(bf16)
+    other_ref[:, rows:, :] = jnp.zeros((chips, GROUP, bands), bf16)
+
+
+def make_margin(first, last, bands, core, trial, pieces, before, margin):
+    share, local_g = trial.shape[0] // 2, trial.shape[1]
     chips = pieces.shape[0]
-    bands = share * count
-    first, last = chunk == 0, chunk == count - 1
-    width = min(TRIAL_WIDE, local_g)
-    deep = lambda step: (0, 0, step)
     if last:
         rows = bands // (2 * chips) + GROUP
-        out_specs = [pl.BlockSpec((chips, rows, bands), lambda step: (0, 0, 0))] * 2
         out_shape = [
             jax.ShapeDtypeStruct((chips, rows, bands), f32),
             jax.ShapeDtypeStruct((chips, rows, bands), bf16),
         ]
     else:
-        out_specs = [pl.BlockSpec((share, share), lambda step: (0, 0))]
         out_shape = [jax.ShapeDtypeStruct((share, share), f32)]
-    operands = [core, kinetic, planes, potential]
-    in_specs = [
-        pl.BlockSpec(memory_space=pltpu.SMEM),
-        pl.BlockSpec((1, width), lambda step: (0, step)),
-        pl.BlockSpec((2, share, width), deep),
-        pl.BlockSpec((2 * share, width), lambda step: (0, step)),
-    ]
-    if last:
-        operands.append(pieces)
-        in_specs.append(pl.BlockSpec(pieces.shape, lambda step: (0, 0, 0)))
-    if not first:
-        operands += [before, margin]
-        in_specs.append(pl.BlockSpec((2, share, width), deep))
-        in_specs.append(pl.BlockSpec((share, share), lambda step: (0, 0)))
-
-    def body(core_ref, kinetic_ref, wave_ref, potential_ref, *refs):
-        refs = list(refs)
-        pieces_ref = refs.pop(0) if last else None
-        before_ref = None if first else refs.pop(0)
-        margin_ref = None if first else refs.pop(0)
-        trial_ref, mine_ref = refs.pop(0), refs.pop(0)
-        other_ref = refs.pop(0) if last else None
-        trial_kernel(
-            first, last, core_ref, kinetic_ref, wave_ref, potential_ref, pieces_ref, before_ref,
-            margin_ref, trial_ref, mine_ref, other_ref, *refs,
-        )
-
-    seen = (chunk + 1) * share
+    operands = [core, trial] + ([pieces] if last else []) + ([] if first else [before, margin])
+    inside = pl.BlockSpec(memory_space=pltpu.VMEM)
     return pl.pallas_call(
-        body,
-        grid=(local_g // width,),
-        in_specs=in_specs,
-        out_specs=[pl.BlockSpec((2, share, width), deep)] + out_specs,
-        out_shape=[jax.ShapeDtypeStruct((2, share, local_g), bf16)] + out_shape,
-        scratch_shapes=[
-            pltpu.VMEM((share, seen), f32),
-            pltpu.VMEM((share, seen), f32),
-            pltpu.VMEM((bands, bands), f32),
-        ],
+        functools.partial(margin_kernel, first, last),
+        in_specs=[pl.BlockSpec(memory_space=pltpu.SMEM)] + [inside] * (len(operands) - 1),
+        out_specs=[inside] * len(out_shape),
+        out_shape=out_shape,
+        scratch_shapes=[pltpu.VMEM((bands, bands), f32)] if last else [],
         compiler_params=pltpu.CompilerParams(vmem_limit_bytes=LAST_VMEM_BYTES),
         cost_estimate=pl.CostEstimate(
-            flops=8 * share * seen * local_g,
-            bytes_accessed=12 * seen * local_g,
+            flops=8 * share * (share if first else 2 * share) * local_g,
+            bytes_accessed=8 * share * local_g,
             transcendentals=0,
         ),
     )(*operands)
@@ -519,16 +485,17 @@
                 odd[down, over] = opposite.astype(bf16)
                 odd[over, down] = -opposite.T.astype(bf16)
 
-    real = jnp.concatenate([trial[0] for trial in trials], 0)
-    imag = jnp.concatenate([trial[1] for trial in trials], 0)
+    parted = [split_rows(trial[...]) for trial in trials]
+    real = jnp.concatenate([part[0] for part in parted], 0)
+    imag = jnp.concatenate([part[1] for part in parted], 0)
     out_ref[:, 0, :] = (matmul(even[...], real) - matmul(odd[...], imag)).astype(bf16)
     out_ref[:, 1, :] = (matmul(even[...], imag) + matmul(odd[...], real)).astype(bf16)
 
 
 def update_waves(core, mine, others, trials):
-    _, share, local_g = trials[0].shape
+    rows, local_g = trials[0].shape
     count = len(trials)
-    bands = share * count
+    bands = rows // 2 * count
     width = min(WIDE, local_g)
     return pl.pallas_call(
         functools.partial(update_kernel, count),
@@ -538,7 +505,7 @@
             pl.BlockSpec((bands // 2, bands), lambda step: (0, 0)),
             pl.BlockSpec((bands // 2, bands), lambda step: (0, 0)),
         ]
-        + [pl.BlockSpec((2, share, width), lambda step: (0, 0, step))] * count,
+        + [pl.BlockSpec((rows, width), lambda step: (0, step))] * count,
         out_specs=pl.BlockSpec((bands, 2, width), lambda step: (0, 0, step)),
         out_shape=jax.ShapeDtypeStruct((bands, 2, local_g), bf16),
         scratch_shapes=[pltpu.VMEM((bands, bands), bf16)] * 2,
@@ -569,26 +536,18 @@
     oxygens = unpack_oxygens(waves[0][:, share // parts :, 0, :], positions.shape[2])
     tables = transform_tables()
     in_plane, along = projector_tables(oxygens)
-    grid_potential = vloc[0].reshape(NGRID, PLANE) * (1.0 / GVECS)
-    potentials, forces = [], []
+    grid_potential = vloc[0].reshape(NGRID, PLANE) * (step_size / GVECS)
+    line = frequency(jnp.arange(NGRID, dtype=jnp.int32), NGRID) ** 2
+    square = line[:, None, None] + line[None, :, None] + line[None, None, :]
+    kept = (1.0 - step_size * 0.5 * square).reshape(NGRID, PLANE)
+    trials, forces = [], []
     for wave in waves:
-        moved, force = apply_hamiltonian(
-            wave, share // parts, tables, grid_potential, in_plane, along
+        moved, force = make_trial(
+            wave, share // parts, tables, grid_potential, kept, in_plane, along
         )
-        potentials.append(exchange(moved).reshape(2 * share, local_g))
+        trials.append(exchange(moved).reshape(2 * share, local_g))
         forces.append(force)
     force_part = jnp.sum(sum(forces), axis=1) * (2.0 * occupation * nonlocal_strength / GVECS)
-
-    flat_index = lax.axis_index("ga") * local_g + jnp.arange(local_g, dtype=jnp.int32)
-    square = (
-        frequency(flat_index // PLANE, NGRID) ** 2
-        + frequency(flat_index // NGRID % NGRID, NGRID) ** 2
-        + frequency(flat_index % NGRID, NGRID) ** 2
-    )
-    kinetic = (0.5 * square)[None]
-    planes = [
-        jnp.swapaxes(psi[0, chunk * share : (chunk + 1) * share], 0, 1) for chunk in range(count)
-    ]
 
     chip, core = lax.axis_index("ga") // 2, lax.axis_index("ga") % 2
     chips = parts // 2
@@ -603,13 +562,12 @@
     pieces = jnp.swapaxes(jnp.stack(pieces).reshape(9, chips, near_chip), 0, 1)
     pieces = jnp.pad(pieces.reshape(chips, -1), ((0, 0), (0, GROUP * bands - 9 * near_chip)))
     pieces = pieces.reshape(chips, GROUP, bands)
-    trials, margin = [], None
-    for chunk, potential in enumerate(potentials):
-        before = trials[-1] if trials else None
-        trial, margin, *others = make_trial(
-            chunk, count, core_ref, kinetic, planes[chunk], potential, pieces, before, margin
+    before, margin = None, None
+    for chunk, trial in enumerate(trials):
+        margin, *others = make_margin(
+            chunk == 0, chunk == count - 1, bands, core_ref, trial, pieces, before, margin
         )
-        trials.append(trial)
+        before = trial
     pair = (margin + other_core(others[0], parts).astype(f32)).astype(bf16)
     summed = jnp.sum(exchange(pair, same_core).astype(f32), axis=0)
     summed, found = summed[:rows], summed[rows:].reshape(-1)[: 9 * near_chip]

time: 270 us -> 266 us (0.985)
  local copies, waits for them, and re-layouts: 28.8 us -> 12.4 us
  waiting for transfers between devices: 90.9 us -> 104 us
    all_to_all x6, waiting for transfers between devices: 89 us -> 102 us  [exchange(): lax.all_to_all(blocks, 'ga', split_axis=0, concat_axis=0, tiled=True, axi...]
    unnamed x31 -> x17, local copies, waits for them, and re-layouts: 13.1 us -> 1.04 us
    another operation x2 -> x1, local copies, waits for them, and re-layouts: 3.62 us -> 0.09 us  [the longest x1 3.53 us: per_device(): waves.append(exchange(block.reshape(parts, share // parts, 2, local_g)))]
  transfers between devices with their start and end apart: 9 -> 9, of which waited for: 8 -> 8; matrix products, arithmetic and copies ran while one was open for 10% -> 7% of each run, Pallas kernels for 25% -> 26%
where the time goes in v5:
time: 266 us; the launch traced here: 265 us
  waiting for transfers between devices  104 us (39%)
  Pallas kernels  85 us (32%)
  starting transfers between devices  54.2 us (20%)
  local copies, waits for them, and re-layouts  12.4 us (5%)
  other arithmetic  8.27 us (3%)
    all_to_all x6, waiting for transfers between devices, exchange(): lax.all_to_all(blocks, 'ga', split_axis=0, concat_axis=0, tiled=True, axi...  102 us
    pallas_call x2, Pallas kernels, make_trial(): pl.pallas_call(wave_kernel, grid=(steps,), in_specs=[pl.BlockSpec((parts,...  67.6 us
    all_to_all x6, starting transfers between devices, exchange(): lax.all_to_all(blocks, 'ga', split_axis=0, concat_axis=0, tiled=True, axi...  53.3 us
    pallas_call x1, Pallas kernels, update_waves(): pl.pallas_call(functools.partial(update_kernel, count), grid=(local_g //...  8.66 us
    pallas_call x2, Pallas kernels, make_margin(): pl.pallas_call(functools.partial(margin_kernel, first, last), in_specs=[p...  5.34 us
  transfers between devices with their start and end apart: 9, of which 8 were waited for; matrix products, arithmetic and copies ran while one was open for 7% of the time, Pallas kernels for 26%

profile of v5, /device:TPU:0, one launch (start us, length us, event | category | flops | bytes accessed | tf_op | source)
XLA Modules:
  0.0 265.2 jit_solution(11237278438189387093)
XLA Ops:
  0.6 3.4 %shard_map.104 = bf16[16,17,2,2048]{3,2,1,0:T(2,128)(2,1)} custom-call(f32[3,32,48]{2,1,0:T(8,128)} %bitcast.46, s32[1,32]{1,0:T(1,128)} %weights_ref.1, bf16[1,512,2,2048]{3,2,1,0:T(2,128)(2,1)} %psi_ref.1), custom_call_target="tpu_custom_call" | custom-call | bytes 4194304 | tf_op jit(solution)/shard_map/pallas_call | solution.py:176
  4.0 7.4 %all-to-all-start.1 = ((bf16[16,17,2,2048]{3,2,1,0:T(2,128)(2,1)}), bf16[16,17,2,2048]{3,2,1,0:T(2,128)(2,1)}, u32[]{:S(2)}, u32[]{:S(2)}) async-start(bf16[16,17,2,2048]{3,2,1,0:T(2,128)(2,1)} %shard_map.104), calls=%async_computation.1 | async-start | bytes 4456448 | tf_op jit(solution)/shard_map/all_to_all | solution.py:72
  11.5 4.4 %slice.58 = bf16[1,256,2,2048]{3,2,1,0:T(2,128)(2,1)} slice(bf16[1,512,2,2048]{3,2,1,0:T(2,128)(2,1)} %psi_ref.1), slice={[0:1], [256:512], [0:2], [0:2048]} | slice | bytes 4194304 | tf_op jit(solution)/shard_map/slice | solution.py:534
  16.0 39.0 %all-to-all-done.1.wave_ref = bf16[16,17,2,2048]{3,2,1,0:T(2,128)(2,1)} async-done(((bf16[16,17,2,2048]{3,2,1,0:T(2,128)(2,1)}), bf16[16,17,2,2048]{3,2,1,0:T(2,128)(2,1)}, u32[]{:S(2)}, u32[]{:S(2)}) %all-to-all-start.1) | async-done | bytes 2228256 | tf_op jit(solution)/shard_map/all_to_all | solution.py:72
  55.0 11.9 %all-to-all-start = ((bf16[16,16,2,2048]{3,2,1,0:T(2,128)(2,1)}), bf16[16,16,2,2048]{3,2,1,0:T(2,128)(2,1)}, u32[]{:S(2)}, u32[]{:S(2)}) async-start(bf16[16,16,2,2048]{3,2,1,0:T(2,128)(2,1)} %bitcast.1), calls=%async_computation | async-start | bytes 4194304 | tf_op jit(solution)/shard_map/all_to_all | solution.py:72
  68.0 0.7 mul.914.pot_ref
  68.7 0.7 multiply_subtract_fusion.kept_ref
  69.4 1.0 slice.75
  70.5 1.8 slice.61
  72.8 0.7 pad_maximum_fusion.3.along_ref
  73.4 1.5 fusion.7
  75.4 1.9 pad_maximum_fusion.in_plane_ref
  77.3 33.8 %shard_map.106 = (bf16[16,2,16,2048]{3,2,1,0:T(8,128)(2,1)}, f32[3,8,256]{2,1,0:T(8,128)}) custom-call(bf16[16,17,2,2048]{3,2,1,0:T(2,128)(2,1)} %all-to-all-done.1.wave_ref, bf16[1024,1024]{1,0:T(8,128)(2,1)} %constant.39.clone.cos_ref, bf16[1024,1024]{1,0:T(8,128)(2,1)} %constant.128.clone.sin_ref, bf16[512,1024]{1,0:T(8,128)(2,1)} %constant.129.clone.back_ref, ...), custom_call_target="tpu_custom_call" | custom-call | flops 17179869184 | bytes 16777216 | tf_op jit(solution)/shard_map/pallas_call | solution.py:347
  111.1 8.2 %all-to-all-start.3 = ((bf16[16,2,16,2048]{3,2,1,0:T(8,128)(2,1)}), bf16[16,2,16,2048]{3,2,1,0:T(8,128)(2,1)S(1)}, u32[]{:S(2)}, u32[]{:S(2)}) async-start(bf16[16,2,16,2048]{3,2,1,0:T(8,128)(2,1)} %get-tuple-element.11), calls=%async_computation.3 | async-start | bytes 4194304 | tf_op jit(solution)/shard_map/all_to_all | solution.py:72
  119.3 33.8 %shard_map.105 = (bf16[16,2,16,2048]{3,2,1,0:T(8,128)(2,1)}, f32[3,8,256]{2,1,0:T(8,128)}) custom-call(bf16[16,16,2,2048]{3,2,1,0:T(2,128)(2,1)} %all-to-all-done.wave_ref, bf16[1024,1024]{1,0:T(8,128)(2,1)} %constant.39.clone.cos_ref, bf16[1024,1024]{1,0:T(8,128)(2,1)} %constant.128.clone.sin_ref, bf16[512,1024]{1,0:T(8,128)(2,1)} %constant.129.clone.back_ref, ...), custom_call_target="tpu_custom_call" | custom-call | flops 17179869184 | bytes 16777216 | tf_op jit(solution)/shard_map/pallas_call | solution.py:347
  153.1 7.3 %all-to-all-done.3 = bf16[16,2,16,2048]{3,2,1,0:T(8,128)(2,1)S(1)} async-done(((bf16[16,2,16,2048]{3,2,1,0:T(8,128)(2,1)}), bf16[16,2,16,2048]{3,2,1,0:T(8,128)(2,1)S(1)}, u32[]{:S(2)}, u32[]{:S(2)}) %all-to-all-start.3) | async-done | bytes 2097184 | tf_op jit(solution)/shard_map/all_to_all | solution.py:72
  160.4 11.4 %all-to-all-start.2 = ((bf16[16,2,16,2048]{3,2,1,0:T(8,128)(2,1)}), bf16[16,2,16,2048]{3,2,1,0:T(8,128)(2,1)}, u32[]{:S(2)}, u32[]{:S(2)}) async-start(bf16[16,2,16,2048]{3,2,1,0:T(8,128)(2,1)} %get-tuple-element.8), calls=%async_computation.2 | async-start | bytes 4194304 | tf_op jit(solution)/shard_map/all_to_all | solution.py:72
  173.0 1.3 shard_map.107.refs_2_
  174.3 38.6 %all-to-all-done.2 = bf16[16,2,16,2048]{3,2,1,0:T(8,128)(2,1)} async-done(((bf16[16,2,16,2048]{3,2,1,0:T(8,128)(2,1)}), bf16[16,2,16,2048]{3,2,1,0:T(8,128)(2,1)}, u32[]{:S(2)}, u32[]{:S(2)}) %all-to-all-start.2) | async-done | bytes 2097184 | tf_op jit(solution)/shard_map/all_to_all | solution.py:72
  212.9 4.1 %shard_map.108 = (f32[8,40,512]{2,1,0:T(8,128)S(1)}, bf16[8,40,512]{2,1,0:T(8,128)(2,1)S(1)}) custom-call(s32[1]{0:T(128)} %bitcast.core_ref, bf16[512,2048]{1,0:T(8,128)(2,1)} %bitcast.4.trial_ref.refs_1_, f32[8,8,512]{2,1,0:T(8,128)S(1)} %bitcast.45, bf16[512,2048]{1,0:T(8,128)(2,1)S(1)} %bitcast.41, f32[256,256]{1,0:T(8,128)S(1)} %shard_map.107.refs_2_), custom_call_target="tpu_custom_call" | custom-call | flops 2147483648 | bytes 4194304 | tf_op jit(solution)/shard_map/pallas_call | solution.py:446
  217.0 0.8 collective-permute-start
  218.5 0.6 collective-permute-done
  219.1 0.8 add_convert_fusion
  219.9 10.7 %all-to-all-start.4 = ((bf16[8,40,512]{2,1,0:T(8,128)(2,1)}), bf16[8,40,512]{2,1,0:T(8,128)(2,1)S(1)}, u32[]{:S(2)}, u32[]{:S(2)}) async-start(bf16[8,40,512]{2,1,0:T(8,128)(2,1)} %add_convert_fusion), calls=%async_computation.4 | async-start | bytes 655360 | tf_op jit(solution)/shard_map/all_to_all | solution.py:72
  230.6 0.6 divide_bitcast_fusion
  231.4 10.0 %all-to-all-done.4 = bf16[8,40,512]{2,1,0:T(8,128)(2,1)S(1)} async-done(((bf16[8,40,512]{2,1,0:T(8,128)(2,1)}), bf16[8,40,512]{2,1,0:T(8,128)(2,1)S(1)}, u32[]{:S(2)}, u32[]{:S(2)}) %all-to-all-start.4) | async-done | bytes 327712 | tf_op jit(solution)/shard_map/all_to_all | solution.py:72
  241.5 0.7 broadcast_in_dim.41
  242.2 3.6 %all-to-all-start.5 = ((bf16[8,32,512]{2,1,0:T(8,128)(2,1)}), bf16[8,32,512]{2,1,0:T(8,128)(2,1)S(1)}, u32[]{:S(2)}, u32[]{:S(2)}) async-start(bf16[8,32,512]{2,1,0:T(8,128)(2,1)} %broadcast_in_dim.41), calls=%async_computation.5 | async-start | bytes 524288 | tf_op jit(solution)/shard_map/all_to_all | solution.py:72
  246.6 0.8 collective-permute-done.2
  247.5 7.5 %all-to-all-done.5 = bf16[8,32,512]{2,1,0:T(8,128)(2,1)S(1)} async-done(((bf16[8,32,512]{2,1,0:T(8,128)(2,1)}), bf16[8,32,512]{2,1,0:T(8,128)(2,1)S(1)}, u32[]{:S(2)}, u32[]{:S(2)}) %all-to-all-start.5) | async-done | bytes 262176 | tf_op jit(solution)/shard_map/all_to_all | solution.py:72
  255.3 0.7 copy.29
  256.5 8.7 %shard_map.109 = bf16[512,2,2048]{2,1,0:T(2,128)(2,1)} custom-call(s32[1]{0:T(128)} %bitcast.core_ref, bf16[256,512]{1,0:T(8,128)(2,1)S(1)} %bitcast.44, bf16[256,512]{1,0:T(8,128)(2,1)S(1)} %collective-permute-done.1.other_ref, bf16[512,2048]{1,0:T(8,128)(2,1)S(1)} %bitcast.42, bf16[512,2048]{1,0:T(8,128)(2,1)} %bitcast.4.trial_ref.refs_1_), custom_call_target="tpu_custom_call" | custom-call | flops 4294967296 | bytes 8388608 | tf_op jit(solution)/shard_map/pallas_call | solution.py:500
  (75 shorter events, 5.7 us)
Async XLA Ops:
  4.0 50.9 %all-to-all-start.1 = ((bf16[16,17,2,2048]{3,2,1,0:T(2,128)(2,1)}), bf16[16,17,2,2048]{3,2,1,0:T(2,128)(2,1)}, u32[]{:S(2)}, u32[]{:S(2)}) async-start(bf16[16,17,2,2048]{3,2,1,0:T(2,128)(2,1)} %shard_map.104), calls=%async_computation.1 | async-start | bytes 4456448 | tf_op jit(solution)/shard_map/all_to_all | solution.py:72
  54.9 12.7 %copy-start.1 = (f32[1,32768]{1,0:T(1,128)S(1)}, f32[1,32768]{1,0:T(1,128)}, u32[]{:S(2)}) copy-start(f32[1,32768]{1,0:T(1,128)} %param.12) | copy-start | bytes 393220
  55.0 56.1 %all-to-all-start = ((bf16[16,16,2,2048]{3,2,1,0:T(2,128)(2,1)}), bf16[16,16,2,2048]{3,2,1,0:T(2,128)(2,1)}, u32[]{:S(2)}, u32[]{:S(2)}) async-start(bf16[16,16,2,2048]{3,2,1,0:T(2,128)(2,1)} %bitcast.1), calls=%async_computation | async-start | bytes 4194304 | tf_op jit(solution)/shard_map/all_to_all | solution.py:72
  111.1 49.3 %all-to-all-start.3 = ((bf16[16,2,16,2048]{3,2,1,0:T(8,128)(2,1)}), bf16[16,2,16,2048]{3,2,1,0:T(8,128)(2,1)S(1)}, u32[]{:S(2)}, u32[]{:S(2)}) async-start(bf16[16,2,16,2048]{3,2,1,0:T(8,128)(2,1)} %get-tuple-element.11), calls=%async_computation.3 | async-start | bytes 4194304 | tf_op jit(solution)/shard_map/all_to_all | solution.py:72
  153.1 18.7 %copy-start = (f32[32,3,48]{2,0,1:T(8,128)S(1)}, f32[32,3,48]{2,0,1:T(8,128)}, u32[]{:S(2)}) copy-start(f32[32,3,48]{2,0,1:T(8,128)} %param.9) | copy-start | bytes 55300
  160.4 12.3 %copy-start.2 = (f32[3,8,256]{2,1,0:T(8,128)S(1)}, f32[3,8,256]{2,1,0:T(8,128)}, u32[]{:S(2)}) copy-start(f32[3,8,256]{2,1,0:T(8,128)} %get-tuple-element.9) | copy-start | bytes 73732
  160.4 12.3 %copy-start.3 = (f32[3,8,256]{2,1,0:T(8,128)S(1)}, f32[3,8,256]{2,1,0:T(8,128)}, u32[]{:S(2)}) copy-start(f32[3,8,256]{2,1,0:T(8,128)} %get-tuple-element.10) | copy-start | bytes 73732
  160.4 52.6 %all-to-all-start.2 = ((bf16[16,2,16,2048]{3,2,1,0:T(8,128)(2,1)}), bf16[16,2,16,2048]{3,2,1,0:T(8,128)(2,1)}, u32[]{:S(2)}, u32[]{:S(2)}) async-start(bf16[16,2,16,2048]{3,2,1,0:T(8,128)(2,1)} %get-tuple-element.8), calls=%async_computation.2 | async-start | bytes 4194304 | tf_op jit(solution)/shard_map/all_to_all | solution.py:72
  212.9 4.9 %copy-start.4 = (s32[1,32]{1,0:T(1,128)S(1)}, s32[1,32]{1,0:T(1,128)}, u32[]{:S(2)}) copy-start(s32[1,32]{1,0:T(1,128)} %weights_ref.1) | copy-start | bytes 388
  217.0 2.1 collective-permute-start
  219.9 21.5 %all-to-all-start.4 = ((bf16[8,40,512]{2,1,0:T(8,128)(2,1)}), bf16[8,40,512]{2,1,0:T(8,128)(2,1)S(1)}, u32[]{:S(2)}, u32[]{:S(2)}) async-start(bf16[8,40,512]{2,1,0:T(8,128)(2,1)} %add_convert_fusion), calls=%async_computation.4 | async-start | bytes 655360 | tf_op jit(solution)/shard_map/all_to_all | solution.py:72
  242.2 12.7 %all-to-all-start.5 = ((bf16[8,32,512]{2,1,0:T(8,128)(2,1)}), bf16[8,32,512]{2,1,0:T(8,128)(2,1)S(1)}, u32[]{:S(2)}, u32[]{:S(2)}) async-start(bf16[8,32,512]{2,1,0:T(8,128)(2,1)} %broadcast_in_dim.41), calls=%async_computation.5 | async-start | bytes 524288 | tf_op jit(solution)/shard_map/all_to_all | solution.py:72
  246.2 1.2 collective-permute-start.2
  255.0 1.5 collective-permute-start.1

commit v6 on v5

--- a/solution.py
+++ b/solution.py
@@ -31,7 +31,8 @@
 GROUP = 8
 SLAB = 128
 LANES = 256
-WIDE = 512
+WIDE = 1024
+PIECE = 512
 VMEM_BYTES = 56 * 2**20
 TAIL_VMEM_BYTES = 60 * 2**20
 LAST_VMEM_BYTES = 28 * 2**20
@@ -127,19 +128,24 @@
 
 
 def pack_kernel(positions_ref, weights_ref, psi_ref, out_ref, lanes, stage, in_sems, out_sems):
-    parts, total, _, local_g = out_ref.shape
+    parts, total, _, width = out_ref.shape
     extra = lanes.shape[0] // 2
-    own = total - extra
+    pieces = psi_ref.shape[3] // width
+    own = (total - extra) // pieces
     arrivals = [
-        pltpu.make_async_copy(
-            psi_ref.at[0, pl.ds(owner * own, own)],
-            stage.at[owner, pl.ds(0, own)],
-            in_sems.at[owner],
-        )
+        [
+            pltpu.make_async_copy(
+                psi_ref.at[0, pl.ds(owner * own, own), :, pl.ds(piece * width, width)],
+                stage.at[owner, pl.ds(piece * own, own)],
+                in_sems.at[owner, piece],
+            )
+            for piece in range(pieces)
+        ]
         for owner in range(parts)
     ]
-    for copy in arrivals:
-        copy.start()
+    for copies in arrivals:
+        for copy in copies:
+            copy.start()
     weights = weights_ref[...].astype(f32)
     mixing = weights / jnp.sum(weights, axis=1, keepdims=True)
     lanes[...] = jnp.zeros_like(lanes)
@@ -151,28 +157,36 @@
         for piece in range(3):
             sent = left.astype(bf16).astype(f32)
             left = left - sent
-            place = (3 * piece + axis) * SLAB
-            row, column = 2 * (place // local_g), place % local_g
+            place = (3 * piece + axis) * segment(atoms)
+            row, column = place // width, place % width
             lanes[row : row + 1, column : column + atoms] = sent
     for row in range(extra):
         ending = lanes[2 * row : 2 * row + 2, :].astype(bf16)
         for owner in range(parts):
-            stage[owner, own + row] = ending
+            stage[owner, own * pieces + row] = ending
     departures = [
         pltpu.make_async_copy(stage.at[owner], out_ref.at[owner], out_sems.at[owner])
         for owner in range(parts)
     ]
-    for arrival, departure in zip(arrivals, departures):
-        arrival.wait()
+    for copies, departure in zip(arrivals, departures):
+        for copy in copies:
+            copy.wait()
         departure.start()
     for copy in departures:
         copy.wait()
 
 
+def segment(atoms):
+    return -(-atoms // 64) * 64
+
+
 def pack_first(positions, weights, psi, parts, share):
     local_g = psi.shape[3]
-    beads, _, atoms = positions.shape
-    extra = -(-9 * SLAB // local_g)
+    atoms = positions.shape[2]
+    width = min(PIECE, local_g)
+    pieces = local_g // width
+    extra = -(-9 * segment(atoms) // (2 * width))
+    block = (parts, pieces * share // parts + extra, 2, width)
     return pl.pallas_call(
         pack_kernel,
         in_specs=[
@@ -181,11 +195,11 @@
             pl.BlockSpec(memory_space=pl.ANY),
         ],
         out_specs=pl.BlockSpec(memory_space=pl.ANY),
-        out_shape=jax.ShapeDtypeStruct((parts, share // parts + extra, 2, local_g), bf16),
+        out_shape=jax.ShapeDtypeStruct(block, bf16),
         scratch_shapes=[
-            pltpu.VMEM((2 * extra, local_g), f32),
-            pltpu.VMEM((parts, share // parts + extra, 2, local_g), bf16),
-            pltpu.SemaphoreType.DMA((parts,)),
+            pltpu.VMEM((2 * extra, width), f32),
+            pltpu.VMEM(block, bf16),
+            pltpu.SemaphoreType.DMA((parts, pieces)),
             pltpu.SemaphoreType.DMA((parts,)),
         ],
         compiler_params=pltpu.CompilerParams(vmem_limit_bytes=TAIL_VMEM_BYTES),
@@ -196,8 +210,8 @@
 
 
 def unpack_oxygens(rows, atoms):
-    parts = rows.shape[0]
-    pieces = rows.reshape(parts, -1)[:, : 9 * SLAB].reshape(parts, 3, 3, SLAB)
+    parts, each = rows.shape[0], segment(atoms)
+    pieces = rows.reshape(parts, -1)[:, : 9 * each].reshape(parts, 3, 3, each)
     found = jnp.sum(pieces[..., 0:atoms:3].astype(f32), axis=1)
     return jnp.swapaxes(found, 0, 1).reshape(3, -1)
 
@@ -219,6 +233,7 @@
 
 
 def wave_kernel(
+    band_count,
     wave_ref,
     cos_ref,
     sin_ref,
@@ -238,15 +253,18 @@
     pulls,
     kinetic,
 ):
-    parts, local_g = wave_ref.shape[0], wave_ref.shape[3]
+    parts, _, _, local_g = out_ref.shape
+    width = wave_ref.shape[3]
     waters = along_ref.shape[2]
     band_rows = 2 * GROUP
     all_rows = NGRID * band_rows
-    piece = min(local_g, PLANE)
+    piece = min(width, PLANE)
+    first = pl.program_id(0) * GROUP if width < local_g else 0
     for start in range(0, NGRID * PLANE, piece):
         owner, offset = start // local_g, start % local_g
         x, column = start // PLANE, start % PLANE
-        block = wave_ref[owner, :, :, offset : offset + piece]
+        bands = pl.ds(first + offset // width * band_count, GROUP)
+        block = wave_ref[owner, bands, :, offset % width : offset % width + piece]
         rows[x * band_rows : (x + 1) * band_rows, column : column + piece] = block.reshape(
             band_rows, piece
         )
@@ -329,6 +347,7 @@
         waves += matmul(pulls[...], in_plane_ref[: 2 * waters, columns])
         planes[:all_rows, columns] = (kinetic[:, columns] - waves).astype(bf16)
 
+    piece = min(local_g, PLANE)
     for start in range(0, NGRID * PLANE, piece):
         owner, offset = start // local_g, start % local_g
         x, column = start // PLANE, start % PLANE
@@ -337,18 +356,22 @@
         ]
 
 
-def make_trial(waves, band_count, tables, grid_potential, kept, in_plane, along):
-    parts, _, _, local_g = waves.shape
+def make_trial(waves, band_count, local_g, tables, grid_potential, kept, in_plane, along):
+    parts, total, _, width = waves.shape
+    if width < local_g:
+        taken = pl.BlockSpec((parts, total, 2, width), lambda step: (0, 0, 0, 0))
+    else:
+        taken = pl.BlockSpec((parts, GROUP, 2, width), lambda step: (0, step, 0, 0))
     waters = along.shape[2]
     steps = band_count // GROUP
     band_rows = 2 * GROUP
     all_rows = NGRID * band_rows
     whole = lambda step: (0, 0)
     return pl.pallas_call(
-        wave_kernel,
+        functools.partial(wave_kernel, band_count),
         grid=(steps,),
         in_specs=[
-            pl.BlockSpec((parts, GROUP, 2, local_g), lambda step: (0, step, 0, 0)),
+            taken,
             pl.BlockSpec((PLANE, PLANE), whole),
             pl.BlockSpec((PLANE, PLANE), whole),
             pl.BlockSpec((all_rows, 2 * all_rows), whole),
@@ -533,7 +556,8 @@
     for chunk in range(1, count):
         block = psi[0, chunk * share : (chunk + 1) * share]
         waves.append(exchange(block.reshape(parts, share // parts, 2, local_g)))
-    oxygens = unpack_oxygens(waves[0][:, share // parts :, 0, :], positions.shape[2])
+    psi_rows = local_g // sent.shape[3] * share // parts
+    oxygens = unpack_oxygens(waves[0][:, psi_rows:], positions.shape[2])
     tables = transform_tables()
     in_plane, along = projector_tables(oxygens)
     grid_potential = vloc[0].reshape(NGRID, PLANE) * (step_size / GVECS)
@@ -543,7 +567,7 @@
     trials, forces = [], []
     for wave in waves:
         moved, force = make_trial(
-            wave, share // parts, tables, grid_potential, kept, in_plane, along
+            wave, share // parts, local_g, tables, grid_potential, kept, in_plane, along
         )
         trials.append(exchange(moved).reshape(2 * share, local_g))
         forces.append(force)

time: 266 us -> 264 us (level)
  no operation moved by 1% of the time
where the time goes in v6:
time: 264 us; the launch traced here: 263 us
  waiting for transfers between devices  103 us (39%)
  Pallas kernels  85.5 us (32%)
  starting transfers between devices  53.5 us (20%)
  local copies, waits for them, and re-layouts  12.2 us (5%)
  other arithmetic  8.26 us (3%)
    all_to_all x6, waiting for transfers between devices, exchange(): lax.all_to_all(blocks, 'ga', split_axis=0, concat_axis=0, tiled=True, axi...  101 us
    pallas_call x2, Pallas kernels, make_trial(): pl.pallas_call(functools.partial(wave_kernel, band_count), grid=(steps,),...  68 us
    all_to_all x6, starting transfers between devices, exchange(): lax.all_to_all(blocks, 'ga', split_axis=0, concat_axis=0, tiled=True, axi...  52.6 us
    pallas_call x1, Pallas kernels, update_waves(): pl.pallas_call(functools.partial(update_kernel, count), grid=(local_g //...  8.42 us
    pallas_call x2, Pallas kernels, make_margin(): pl.pallas_call(functools.partial(margin_kernel, first, last), in_specs=[p...  5.35 us
  transfers between devices with their start and end apart: 9, of which 8 were waited for; matrix products, arithmetic and copies ran while one was open for 7% of the time, Pallas kernels for 26%

profile of v6, /device:TPU:0, one launch (start us, length us, event | category | flops | bytes accessed | tf_op | source)
XLA Modules:
  0.0 263.1 jit_solution(17969095168249207304)
XLA Ops:
  0.6 3.7 %shard_map.104 = bf16[16,65,2,512]{3,2,1,0:T(2,128)(2,1)} custom-call(f32[3,32,48]{2,1,0:T(8,128)} %bitcast.46, s32[1,32]{1,0:T(1,128)} %weights_ref.1, bf16[1,512,2,2048]{3,2,1,0:T(2,128)(2,1)} %psi_ref.1), custom_call_target="tpu_custom_call" | custom-call | bytes 4194304 | tf_op jit(solution)/shard_map/pallas_call | solution.py:190
  4.3 7.4 %all-to-all-start.1 = ((bf16[16,65,2,512]{3,2,1,0:T(2,128)(2,1)}), bf16[16,65,2,512]{3,2,1,0:T(2,128)(2,1)}, u32[]{:S(2)}, u32[]{:S(2)}) async-start(bf16[16,65,2,512]{3,2,1,0:T(2,128)(2,1)} %shard_map.104), calls=%async_computation.1 | async-start | bytes 4259840 | tf_op jit(solution)/shard_map/all_to_all | solution.py:73
  11.8 4.4 %slice.58 = bf16[1,256,2,2048]{3,2,1,0:T(2,128)(2,1)} slice(bf16[1,512,2,2048]{3,2,1,0:T(2,128)(2,1)} %psi_ref.1), slice={[0:1], [256:512], [0:2], [0:2048]} | slice | bytes 4194304 | tf_op jit(solution)/shard_map/slice | solution.py:557
  16.3 37.3 %all-to-all-done.1.wave_ref = bf16[16,65,2,512]{3,2,1,0:T(2,128)(2,1)} async-done(((bf16[16,65,2,512]{3,2,1,0:T(2,128)(2,1)}), bf16[16,65,2,512]{3,2,1,0:T(2,128)(2,1)}, u32[]{:S(2)}, u32[]{:S(2)}) %all-to-all-start.1) | async-done | bytes 2129952 | tf_op jit(solution)/shard_map/all_to_all | solution.py:73
  53.5 11.5 %all-to-all-start = ((bf16[16,16,2,2048]{3,2,1,0:T(2,128)(2,1)}), bf16[16,16,2,2048]{3,2,1,0:T(2,128)(2,1)}, u32[]{:S(2)}, u32[]{:S(2)}) async-start(bf16[16,16,2,2048]{3,2,1,0:T(2,128)(2,1)} %bitcast.1), calls=%async_computation | async-start | bytes 4194304 | tf_op jit(solution)/shard_map/all_to_all | solution.py:73
  66.2 0.7 mul.914.pot_ref
  66.9 0.7 multiply_subtract_fusion.kept_ref
  67.6 0.8 slice.75
  68.5 1.8 slice.61
  70.8 0.7 pad_maximum_fusion.3.along_ref
  71.5 1.5 fusion.7
  73.4 1.9 pad_maximum_fusion.in_plane_ref
  75.3 34.2 %shard_map.106 = (bf16[16,2,16,2048]{3,2,1,0:T(8,128)(2,1)}, f32[3,8,256]{2,1,0:T(8,128)}) custom-call(bf16[16,65,2,512]{3,2,1,0:T(2,128)(2,1)} %all-to-all-done.1.wave_ref, bf16[1024,1024]{1,0:T(8,128)(2,1)} %constant.39.clone.cos_ref, bf16[1024,1024]{1,0:T(8,128)(2,1)} %constant.128.clone.sin_ref, bf16[512,1024]{1,0:T(8,128)(2,1)} %constant.129.clone.back_ref, ...), custom_call_target="tpu_custom_call" | custom-call | flops 17179869184 | bytes 16777216 | tf_op jit(solution)/shard_map/pallas_call | solution.py:370
  109.5 7.9 %all-to-all-start.3 = ((bf16[16,2,16,2048]{3,2,1,0:T(8,128)(2,1)}), bf16[16,2,16,2048]{3,2,1,0:T(8,128)(2,1)S(1)}, u32[]{:S(2)}, u32[]{:S(2)}) async-start(bf16[16,2,16,2048]{3,2,1,0:T(8,128)(2,1)} %get-tuple-element.11), calls=%async_computation.3 | async-start | bytes 4194304 | tf_op jit(solution)/shard_map/all_to_all | solution.py:73
  117.5 33.8 %shard_map.105 = (bf16[16,2,16,2048]{3,2,1,0:T(8,128)(2,1)}, f32[3,8,256]{2,1,0:T(8,128)}) custom-call(bf16[16,16,2,2048]{3,2,1,0:T(2,128)(2,1)} %all-to-all-done.wave_ref, bf16[1024,1024]{1,0:T(8,128)(2,1)} %constant.39.clone.cos_ref, bf16[1024,1024]{1,0:T(8,128)(2,1)} %constant.128.clone.sin_ref, bf16[512,1024]{1,0:T(8,128)(2,1)} %constant.129.clone.back_ref, ...), custom_call_target="tpu_custom_call" | custom-call | flops 17179869184 | bytes 16777216 | tf_op jit(solution)/shard_map/pallas_call | solution.py:370
  151.3 7.3 %all-to-all-done.3 = bf16[16,2,16,2048]{3,2,1,0:T(8,128)(2,1)S(1)} async-done(((bf16[16,2,16,2048]{3,2,1,0:T(8,128)(2,1)}), bf16[16,2,16,2048]{3,2,1,0:T(8,128)(2,1)S(1)}, u32[]{:S(2)}, u32[]{:S(2)}) %all-to-all-start.3) | async-done | bytes 2097184 | tf_op jit(solution)/shard_map/all_to_all | solution.py:73
  158.6 11.4 %all-to-all-start.2 = ((bf16[16,2,16,2048]{3,2,1,0:T(8,128)(2,1)}), bf16[16,2,16,2048]{3,2,1,0:T(8,128)(2,1)}, u32[]{:S(2)}, u32[]{:S(2)}) async-start(bf16[16,2,16,2048]{3,2,1,0:T(8,128)(2,1)} %get-tuple-element.8), calls=%async_computation.2 | async-start | bytes 4194304 | tf_op jit(solution)/shard_map/all_to_all | solution.py:73
  171.2 1.3 shard_map.107.refs_2_
  172.5 38.6 %all-to-all-done.2 = bf16[16,2,16,2048]{3,2,1,0:T(8,128)(2,1)} async-done(((bf16[16,2,16,2048]{3,2,1,0:T(8,128)(2,1)}), bf16[16,2,16,2048]{3,2,1,0:T(8,128)(2,1)}, u32[]{:S(2)}, u32[]{:S(2)}) %all-to-all-start.2) | async-done | bytes 2097184 | tf_op jit(solution)/shard_map/all_to_all | solution.py:73
  211.1 4.1 %shard_map.108 = (f32[8,40,512]{2,1,0:T(8,128)S(1)}, bf16[8,40,512]{2,1,0:T(8,128)(2,1)S(1)}) custom-call(s32[1]{0:T(128)} %bitcast.core_ref, bf16[512,2048]{1,0:T(8,128)(2,1)} %bitcast.4.trial_ref.refs_1_, f32[8,8,512]{2,1,0:T(8,128)S(1)} %bitcast.45, bf16[512,2048]{1,0:T(8,128)(2,1)S(1)} %bitcast.41, f32[256,256]{1,0:T(8,128)S(1)} %shard_map.107.refs_2_), custom_call_target="tpu_custom_call" | custom-call | flops 2147483648 | bytes 4194304 | tf_op jit(solution)/shard_map/pallas_call | solution.py:469
  215.2 0.8 collective-permute-start
  216.7 0.6 collective-permute-done
  217.3 0.8 add_convert_fusion
  218.1 10.7 %all-to-all-start.4 = ((bf16[8,40,512]{2,1,0:T(8,128)(2,1)}), bf16[8,40,512]{2,1,0:T(8,128)(2,1)S(1)}, u32[]{:S(2)}, u32[]{:S(2)}) async-start(bf16[8,40,512]{2,1,0:T(8,128)(2,1)} %add_convert_fusion), calls=%async_computation.4 | async-start | bytes 655360 | tf_op jit(solution)/shard_map/all_to_all | solution.py:73
  228.8 0.6 divide_bitcast_fusion
  229.6 10.0 %all-to-all-done.4 = bf16[8,40,512]{2,1,0:T(8,128)(2,1)S(1)} async-done(((bf16[8,40,512]{2,1,0:T(8,128)(2,1)}), bf16[8,40,512]{2,1,0:T(8,128)(2,1)S(1)}, u32[]{:S(2)}, u32[]{:S(2)}) %all-to-all-start.4) | async-done | bytes 327712 | tf_op jit(solution)/shard_map/all_to_all | solution.py:73
  239.7 0.7 broadcast_in_dim.41
  240.4 3.6 %all-to-all-start.5 = ((bf16[8,32,512]{2,1,0:T(8,128)(2,1)}), bf16[8,32,512]{2,1,0:T(8,128)(2,1)S(1)}, u32[]{:S(2)}, u32[]{:S(2)}) async-start(bf16[8,32,512]{2,1,0:T(8,128)(2,1)} %broadcast_in_dim.41), calls=%async_computation.5 | async-start | bytes 524288 | tf_op jit(solution)/shard_map/all_to_all | solution.py:73
  244.8 0.8 collective-permute-done.2
  245.7 7.5 %all-to-all-done.5 = bf16[8,32,512]{2,1,0:T(8,128)(2,1)S(1)} async-done(((bf16[8,32,512]{2,1,0:T(8,128)(2,1)}), bf16[8,32,512]{2,1,0:T(8,128)(2,1)S(1)}, u32[]{:S(2)}, u32[]{:S(2)}) %all-to-all-start.5) | async-done | bytes 262176 | tf_op jit(solution)/shard_map/all_to_all | solution.py:73
  253.5 0.7 copy.29
  254.7 8.4 %shard_map.109 = bf16[512,2,2048]{2,1,0:T(2,128)(2,1)} custom-call(s32[1]{0:T(128)} %bitcast.core_ref, bf16[256,512]{1,0:T(8,128)(2,1)S(1)} %bitcast.44, bf16[256,512]{1,0:T(8,128)(2,1)S(1)} %collective-permute-done.1.other_ref, bf16[512,2048]{1,0:T(8,128)(2,1)S(1)} %bitcast.42, bf16[512,2048]{1,0:T(8,128)(2,1)} %bitcast.4.trial_ref.refs_1_), custom_call_target="tpu_custom_call" | custom-call | flops 4294967296 | bytes 8388608 | tf_op jit(solution)/shard_map/pallas_call | solution.py:523
  (75 shorter events, 5.8 us)
Async XLA Ops:
  4.3 49.2 %all-to-all-start.1 = ((bf16[16,65,2,512]{3,2,1,0:T(2,128)(2,1)}), bf16[16,65,2,512]{3,2,1,0:T(2,128)(2,1)}, u32[]{:S(2)}, u32[]{:S(2)}) async-start(bf16[16,65,2,512]{3,2,1,0:T(2,128)(2,1)} %shard_map.104), calls=%async_computation.1 | async-start | bytes 4259840 | tf_op jit(solution)/shard_map/all_to_all | solution.py:73
  53.5 12.3 %copy-start.1 = (f32[1,32768]{1,0:T(1,128)S(1)}, f32[1,32768]{1,0:T(1,128)}, u32[]{:S(2)}) copy-start(f32[1,32768]{1,0:T(1,128)} %param.12) | copy-start | bytes 393220
  53.5 56.0 %all-to-all-start = ((bf16[16,16,2,2048]{3,2,1,0:T(2,128)(2,1)}), bf16[16,16,2,2048]{3,2,1,0:T(2,128)(2,1)}, u32[]{:S(2)}, u32[]{:S(2)}) async-start(bf16[16,16,2,2048]{3,2,1,0:T(2,128)(2,1)} %bitcast.1), calls=%async_computation | async-start | bytes 4194304 | tf_op jit(solution)/shard_map/all_to_all | solution.py:73
  109.5 49.0 %all-to-all-start.3 = ((bf16[16,2,16,2048]{3,2,1,0:T(8,128)(2,1)}), bf16[16,2,16,2048]{3,2,1,0:T(8,128)(2,1)S(1)}, u32[]{:S(2)}, u32[]{:S(2)}) async-start(bf16[16,2,16,2048]{3,2,1,0:T(8,128)(2,1)} %get-tuple-element.11), calls=%async_computation.3 | async-start | bytes 4194304 | tf_op jit(solution)/shard_map/all_to_all | solution.py:73
  151.3 18.7 %copy-start = (f32[32,3,48]{2,0,1:T(8,128)S(1)}, f32[32,3,48]{2,0,1:T(8,128)}, u32[]{:S(2)}) copy-start(f32[32,3,48]{2,0,1:T(8,128)} %param.9) | copy-start | bytes 55300
  158.6 12.3 %copy-start.2 = (f32[3,8,256]{2,1,0:T(8,128)S(1)}, f32[3,8,256]{2,1,0:T(8,128)}, u32[]{:S(2)}) copy-start(f32[3,8,256]{2,1,0:T(8,128)} %get-tuple-element.9) | copy-start | bytes 73732
  158.6 12.3 %copy-start.3 = (f32[3,8,256]{2,1,0:T(8,128)S(1)}, f32[3,8,256]{2,1,0:T(8,128)}, u32[]{:S(2)}) copy-start(f32[3,8,256]{2,1,0:T(8,128)} %get-tuple-element.10) | copy-start | bytes 73732
  158.6 52.6 %all-to-all-start.2 = ((bf16[16,2,16,2048]{3,2,1,0:T(8,128)(2,1)}), bf16[16,2,16,2048]{3,2,1,0:T(8,128)(2,1)}, u32[]{:S(2)}, u32[]{:S(2)}) async-start(bf16[16,2,16,2048]{3,2,1,0:T(8,128)(2,1)} %get-tuple-element.8), calls=%async_computation.2 | async-start | bytes 4194304 | tf_op jit(solution)/shard_map/all_to_all | solution.py:73
  211.1 4.9 %copy-start.4 = (s32[1,32]{1,0:T(1,128)S(1)}, s32[1,32]{1,0:T(1,128)}, u32[]{:S(2)}) copy-start(s32[1,32]{1,0:T(1,128)} %weights_ref.1) | copy-start | bytes 388
  215.2 2.1 collective-permute-start
  218.1 21.4 %all-to-all-start.4 = ((bf16[8,40,512]{2,1,0:T(8,128)(2,1)}), bf16[8,40,512]{2,1,0:T(8,128)(2,1)S(1)}, u32[]{:S(2)}, u32[]{:S(2)}) async-start(bf16[8,40,512]{2,1,0:T(8,128)(2,1)} %add_convert_fusion), calls=%async_computation.4 | async-start | bytes 655360 | tf_op jit(solution)/shard_map/all_to_all | solution.py:73
  240.4 12.7 %all-to-all-start.5 = ((bf16[8,32,512]{2,1,0:T(8,128)(2,1)}), bf16[8,32,512]{2,1,0:T(8,128)(2,1)S(1)}, u32[]{:S(2)}, u32[]{:S(2)}) async-start(bf16[8,32,512]{2,1,0:T(8,128)(2,1)} %broadcast_in_dim.41), calls=%async_computation.5 | async-start | bytes 524288 | tf_op jit(solution)/shard_map/all_to_all | solution.py:73
  244.4 1.2 collective-permute-start.2
  253.2 1.5 collective-permute-start.1

commit v7 on v6

--- a/solution.py
+++ b/solution.py
@@ -448,9 +448,21 @@
     mine = packed[pl.ds(pl.multiple_of(core * half, half), half), :]
     others = packed[pl.ds(pl.multiple_of((1 - core) * half, half), half), :]
     mine_ref[:, :rows, :] = mine.reshape(chips, rows, bands)
-    mine_ref[:, rows:, :] = pieces_ref[...]
     other_ref[:, :rows, :] = others.reshape(chips, rows, bands).astype(bf16)
-    other_ref[:, rows:, :] = jnp.zeros((chips, GROUP, bands), bf16)
+
+    row = lax.broadcasted_iota(jnp.int32, (half, bands), 0)
+    column = lax.broadcasted_iota(jnp.int32, (half, bands), 1)
+    place = lax.broadcasted_iota(jnp.int32, (chips, GROUP, bands), 1)
+
+    def diagonal(block, which, spot):
+        found = jnp.where(row + which * half == column, block, 0.0)
+        found = jnp.sum(found.reshape(chips, rows, bands), axis=1, keepdims=True)
+        high = found.astype(bf16).astype(f32)
+        placed = jnp.where(place == spot, high, 0.0)
+        return jnp.where(place == spot + 1, found - high, placed)
+
+    mine_ref[:, rows:, :] = pieces_ref[...] + diagonal(mine, core, GROUP - 2)
+    other_ref[:, rows:, :] = diagonal(others, 1 - core, GROUP - 4).astype(bf16)
 
 
 def make_margin(first, last, bands, core, trial, pieces, before, margin):
@@ -594,13 +606,14 @@
         before = trial
     pair = (margin + other_core(others[0], parts).astype(f32)).astype(bf16)
     summed = jnp.sum(exchange(pair, same_core).astype(f32), axis=0)
+    diagonal = jnp.sum(summed[rows + GROUP - 4 :], axis=0, keepdims=True)
     summed, found = summed[:rows], summed[rows:].reshape(-1)[: 9 * near_chip]
     found = jnp.sum(found.reshape(3, 3, near_chip), axis=0)
     found = (found + other_core(found, parts)).reshape(3, 2, near_chip // 2)
     oxygen_force = lax.dynamic_index_in_dim(found, core, 1, keepdims=False)
     row = (core * chips + chip) * rows + lax.broadcasted_iota(jnp.int32, (rows, bands), 0)
     column = lax.broadcasted_iota(jnp.int32, (rows, bands), 1)
-    own_mixer = (jnp.where(row == column, 1.5, 0.0) - 0.5 * summed).astype(bf16)
+    own_mixer = jnp.where(row == column, 1.5 - 0.5 * diagonal, -0.5 * summed).astype(bf16)
     half_mixer = exchange(
         jnp.broadcast_to(own_mixer[None], (chips, rows, bands)), same_core
     ).reshape(bands // 2, bands)

time: 264 us -> 264 us (level)
  no operation moved by 1% of the time
where the time goes in v7:
time: 264 us; the launch traced here: 263 us
  waiting for transfers between devices  103 us (39%)
  Pallas kernels  85.8 us (32%)
  starting transfers between devices  53.5 us (20%)
  local copies, waits for them, and re-layouts  12.2 us (5%)
  other arithmetic  8.31 us (3%)
    all_to_all x6, waiting for transfers between devices, exchange(): lax.all_to_all(blocks, 'ga', split_axis=0, concat_axis=0, tiled=True, axi...  101 us
    pallas_call x2, Pallas kernels, make_trial(): pl.pallas_call(functools.partial(wave_kernel, band_count), grid=(steps,),...  68.1 us
    all_to_all x6, starting transfers between devices, exchange(): lax.all_to_all(blocks, 'ga', split_axis=0, concat_axis=0, tiled=True, axi...  52.6 us
    pallas_call x1, Pallas kernels, update_waves(): pl.pallas_call(functools.partial(update_kernel, count), grid=(local_g //...  8.41 us
    pallas_call x2, Pallas kernels, make_margin(): pl.pallas_call(functools.partial(margin_kernel, first, last), in_specs=[p...  5.6 us
  transfers between devices with their start and end apart: 9, of which 8 were waited for; matrix products, arithmetic and copies ran while one was open for 7% of the time, Pallas kernels for 26%

profile of v7, /device:TPU:0, one launch (start us, length us, event | category | flops | bytes accessed | tf_op | source)
XLA Modules:
  0.0 263.4 jit_solution(1257381502732862605)
XLA Ops:
  0.6 3.7 %shard_map.104 = bf16[16,65,2,512]{3,2,1,0:T(2,128)(2,1)} custom-call(f32[3,32,48]{2,1,0:T(8,128)} %bitcast.46, s32[1,32]{1,0:T(1,128)} %weights_ref.1, bf16[1,512,2,2048]{3,2,1,0:T(2,128)(2,1)} %psi_ref.1), custom_call_target="tpu_custom_call" | custom-call | bytes 4194304 | tf_op jit(solution)/shard_map/pallas_call | solution.py:190
  4.3 7.4 %all-to-all-start.1 = ((bf16[16,65,2,512]{3,2,1,0:T(2,128)(2,1)}), bf16[16,65,2,512]{3,2,1,0:T(2,128)(2,1)}, u32[]{:S(2)}, u32[]{:S(2)}) async-start(bf16[16,65,2,512]{3,2,1,0:T(2,128)(2,1)} %shard_map.104), calls=%async_computation.1 | async-start | bytes 4259840 | tf_op jit(solution)/shard_map/all_to_all | solution.py:73
  11.8 4.4 %slice.61 = bf16[1,256,2,2048]{3,2,1,0:T(2,128)(2,1)} slice(bf16[1,512,2,2048]{3,2,1,0:T(2,128)(2,1)} %psi_ref.1), slice={[0:1], [256:512], [0:2], [0:2048]} | slice | bytes 4194304 | tf_op jit(solution)/shard_map/slice | solution.py:569
  16.2 37.3 %all-to-all-done.1.wave_ref = bf16[16,65,2,512]{3,2,1,0:T(2,128)(2,1)} async-done(((bf16[16,65,2,512]{3,2,1,0:T(2,128)(2,1)}), bf16[16,65,2,512]{3,2,1,0:T(2,128)(2,1)}, u32[]{:S(2)}, u32[]{:S(2)}) %all-to-all-start.1) | async-done | bytes 2129952 | tf_op jit(solution)/shard_map/all_to_all | solution.py:73
  53.5 11.5 %all-to-all-start = ((bf16[16,16,2,2048]{3,2,1,0:T(2,128)(2,1)}), bf16[16,16,2,2048]{3,2,1,0:T(2,128)(2,1)}, u32[]{:S(2)}, u32[]{:S(2)}) async-start(bf16[16,16,2,2048]{3,2,1,0:T(2,128)(2,1)} %bitcast.1), calls=%async_computation | async-start | bytes 4194304 | tf_op jit(solution)/shard_map/all_to_all | solution.py:73
  66.2 0.7 mul.925.pot_ref
  66.9 0.7 multiply_subtract_fusion.kept_ref
  67.6 0.8 slice.79
  68.5 1.8 slice.64
  70.8 0.7 pad_maximum_fusion.3.along_ref
  71.5 1.5 fusion.7
  73.5 1.9 pad_maximum_fusion.in_plane_ref
  75.3 34.2 %shard_map.106 = (bf16[16,2,16,2048]{3,2,1,0:T(8,128)(2,1)}, f32[3,8,256]{2,1,0:T(8,128)}) custom-call(bf16[16,65,2,512]{3,2,1,0:T(2,128)(2,1)} %all-to-all-done.1.wave_ref, bf16[1024,1024]{1,0:T(8,128)(2,1)} %constant.38.clone.cos_ref, bf16[1024,1024]{1,0:T(8,128)(2,1)} %constant.39.clone.sin_ref, bf16[512,1024]{1,0:T(8,128)(2,1)} %constant.130.clone.back_ref, ...), custom_call_target="tpu_custom_call" | custom-call | flops 17179869184 | bytes 16777216 | tf_op jit(solution)/shard_map/pallas_call | solution.py:370
  109.5 7.9 %all-to-all-start.3 = ((bf16[16,2,16,2048]{3,2,1,0:T(8,128)(2,1)}), bf16[16,2,16,2048]{3,2,1,0:T(8,128)(2,1)S(1)}, u32[]{:S(2)}, u32[]{:S(2)}) async-start(bf16[16,2,16,2048]{3,2,1,0:T(8,128)(2,1)} %get-tuple-element.11), calls=%async_computation.3 | async-start | bytes 4194304 | tf_op jit(solution)/shard_map/all_to_all | solution.py:73
  117.5 33.8 %shard_map.105 = (bf16[16,2,16,2048]{3,2,1,0:T(8,128)(2,1)}, f32[3,8,256]{2,1,0:T(8,128)}) custom-call(bf16[16,16,2,2048]{3,2,1,0:T(2,128)(2,1)} %all-to-all-done.wave_ref, bf16[1024,1024]{1,0:T(8,128)(2,1)} %constant.38.clone.cos_ref, bf16[1024,1024]{1,0:T(8,128)(2,1)} %constant.39.clone.sin_ref, bf16[512,1024]{1,0:T(8,128)(2,1)} %constant.130.clone.back_ref, ...), custom_call_target="tpu_custom_call" | custom-call | flops 17179869184 | bytes 16777216 | tf_op jit(solution)/shard_map/pallas_call | solution.py:370
  151.3 7.2 %all-to-all-done.3 = bf16[16,2,16,2048]{3,2,1,0:T(8,128)(2,1)S(1)} async-done(((bf16[16,2,16,2048]{3,2,1,0:T(8,128)(2,1)}), bf16[16,2,16,2048]{3,2,1,0:T(8,128)(2,1)S(1)}, u32[]{:S(2)}, u32[]{:S(2)}) %all-to-all-start.3) | async-done | bytes 2097184 | tf_op jit(solution)/shard_map/all_to_all | solution.py:73
  158.6 11.4 %all-to-all-start.2 = ((bf16[16,2,16,2048]{3,2,1,0:T(8,128)(2,1)}), bf16[16,2,16,2048]{3,2,1,0:T(8,128)(2,1)}, u32[]{:S(2)}, u32[]{:S(2)}) async-start(bf16[16,2,16,2048]{3,2,1,0:T(8,128)(2,1)} %get-tuple-element.8), calls=%async_computation.2 | async-start | bytes 4194304 | tf_op jit(solution)/shard_map/all_to_all | solution.py:73
  171.2 1.3 shard_map.107.refs_2_
  172.5 38.6 %all-to-all-done.2 = bf16[16,2,16,2048]{3,2,1,0:T(8,128)(2,1)} async-done(((bf16[16,2,16,2048]{3,2,1,0:T(8,128)(2,1)}), bf16[16,2,16,2048]{3,2,1,0:T(8,128)(2,1)}, u32[]{:S(2)}, u32[]{:S(2)}) %all-to-all-start.2) | async-done | bytes 2097184 | tf_op jit(solution)/shard_map/all_to_all | solution.py:73
  211.1 4.3 %shard_map.108 = (f32[8,40,512]{2,1,0:T(8,128)S(1)}, bf16[8,40,512]{2,1,0:T(8,128)(2,1)S(1)}) custom-call(s32[1]{0:T(128)} %bitcast.core_ref, bf16[512,2048]{1,0:T(8,128)(2,1)} %bitcast.4.trial_ref.refs_1_, f32[8,8,512]{2,1,0:T(8,128)S(1)} %bitcast.45, bf16[512,2048]{1,0:T(8,128)(2,1)S(1)} %bitcast.41, f32[256,256]{1,0:T(8,128)S(1)} %shard_map.107.refs_2_), custom_call_target="tpu_custom_call" | custom-call | flops 2147483648 | bytes 4194304 | tf_op jit(solution)/shard_map/pallas_call | solution.py:481
  215.5 0.8 collective-permute-start
  216.9 0.6 collective-permute-done
  217.5 0.8 add_convert_fusion
  218.4 10.7 %all-to-all-start.4 = ((bf16[8,40,512]{2,1,0:T(8,128)(2,1)}), bf16[8,40,512]{2,1,0:T(8,128)(2,1)S(1)}, u32[]{:S(2)}, u32[]{:S(2)}) async-start(bf16[8,40,512]{2,1,0:T(8,128)(2,1)} %add_convert_fusion), calls=%async_computation.4 | async-start | bytes 655360 | tf_op jit(solution)/shard_map/all_to_all | solution.py:73
  229.1 0.6 divide_bitcast_fusion
  229.8 10.0 %all-to-all-done.4 = bf16[8,40,512]{2,1,0:T(8,128)(2,1)S(1)} async-done(((bf16[8,40,512]{2,1,0:T(8,128)(2,1)}), bf16[8,40,512]{2,1,0:T(8,128)(2,1)S(1)}, u32[]{:S(2)}, u32[]{:S(2)}) %all-to-all-start.4) | async-done | bytes 327712 | tf_op jit(solution)/shard_map/all_to_all | solution.py:73
  240.0 0.7 broadcast_in_dim.22
  240.7 3.6 %all-to-all-start.5 = ((bf16[8,32,512]{2,1,0:T(8,128)(2,1)}), bf16[8,32,512]{2,1,0:T(8,128)(2,1)S(1)}, u32[]{:S(2)}, u32[]{:S(2)}) async-start(bf16[8,32,512]{2,1,0:T(8,128)(2,1)} %broadcast_in_dim.22), calls=%async_computation.5 | async-start | bytes 524288 | tf_op jit(solution)/shard_map/all_to_all | solution.py:73
  245.1 0.8 collective-permute-done.2
  246.0 7.5 %all-to-all-done.5 = bf16[8,32,512]{2,1,0:T(8,128)(2,1)S(1)} async-done(((bf16[8,32,512]{2,1,0:T(8,128)(2,1)}), bf16[8,32,512]{2,1,0:T(8,128)(2,1)S(1)}, u32[]{:S(2)}, u32[]{:S(2)}) %all-to-all-start.5) | async-done | bytes 262176 | tf_op jit(solution)/shard_map/all_to_all | solution.py:73
  253.8 0.7 copy.29
  255.0 8.4 %shard_map.109 = bf16[512,2,2048]{2,1,0:T(2,128)(2,1)} custom-call(s32[1]{0:T(128)} %bitcast.core_ref, bf16[256,512]{1,0:T(8,128)(2,1)S(1)} %bitcast.44, bf16[256,512]{1,0:T(8,128)(2,1)S(1)} %collective-permute-done.1.other_ref, bf16[512,2048]{1,0:T(8,128)(2,1)S(1)} %bitcast.42, bf16[512,2048]{1,0:T(8,128)(2,1)} %bitcast.4.trial_ref.refs_1_), custom_call_target="tpu_custom_call" | custom-call | flops 4294967296 | bytes 8388608 | tf_op jit(solution)/shard_map/pallas_call | solution.py:535
  (77 shorter events, 5.8 us)
Async XLA Ops:
  4.3 49.2 %all-to-all-start.1 = ((bf16[16,65,2,512]{3,2,1,0:T(2,128)(2,1)}), bf16[16,65,2,512]{3,2,1,0:T(2,128)(2,1)}, u32[]{:S(2)}, u32[]{:S(2)}) async-start(bf16[16,65,2,512]{3,2,1,0:T(2,128)(2,1)} %shard_map.104), calls=%async_computation.1 | async-start | bytes 4259840 | tf_op jit(solution)/shard_map/all_to_all | solution.py:73
  53.5 12.3 %copy-start.1 = (f32[1,32768]{1,0:T(1,128)S(1)}, f32[1,32768]{1,0:T(1,128)}, u32[]{:S(2)}) copy-start(f32[1,32768]{1,0:T(1,128)} %param.12) | copy-start | bytes 393220
  53.5 56.0 %all-to-all-start = ((bf16[16,16,2,2048]{3,2,1,0:T(2,128)(2,1)}), bf16[16,16,2,2048]{3,2,1,0:T(2,128)(2,1)}, u32[]{:S(2)}, u32[]{:S(2)}) async-start(bf16[16,16,2,2048]{3,2,1,0:T(2,128)(2,1)} %bitcast.1), calls=%async_computation | async-start | bytes 4194304 | tf_op jit(solution)/shard_map/all_to_all | solution.py:73
  109.5 49.0 %all-to-all-start.3 = ((bf16[16,2,16,2048]{3,2,1,0:T(8,128)(2,1)}), bf16[16,2,16,2048]{3,2,1,0:T(8,128)(2,1)S(1)}, u32[]{:S(2)}, u32[]{:S(2)}) async-start(bf16[16,2,16,2048]{3,2,1,0:T(8,128)(2,1)} %get-tuple-element.11), calls=%async_computation.3 | async-start | bytes 4194304 | tf_op jit(solution)/shard_map/all_to_all | solution.py:73
  151.3 18.7 %copy-start = (f32[32,3,48]{2,0,1:T(8,128)S(1)}, f32[32,3,48]{2,0,1:T(8,128)}, u32[]{:S(2)}) copy-start(f32[32,3,48]{2,0,1:T(8,128)} %param.9) | copy-start | bytes 55300
  158.6 12.3 %copy-start.2 = (f32[3,8,256]{2,1,0:T(8,128)S(1)}, f32[3,8,256]{2,1,0:T(8,128)}, u32[]{:S(2)}) copy-start(f32[3,8,256]{2,1,0:T(8,128)} %get-tuple-element.9) | copy-start | bytes 73732
  158.6 12.3 %copy-start.3 = (f32[3,8,256]{2,1,0:T(8,128)S(1)}, f32[3,8,256]{2,1,0:T(8,128)}, u32[]{:S(2)}) copy-start(f32[3,8,256]{2,1,0:T(8,128)} %get-tuple-element.10) | copy-start | bytes 73732
  158.6 52.6 %all-to-all-start.2 = ((bf16[16,2,16,2048]{3,2,1,0:T(8,128)(2,1)}), bf16[16,2,16,2048]{3,2,1,0:T(8,128)(2,1)}, u32[]{:S(2)}, u32[]{:S(2)}) async-start(bf16[16,2,16,2048]{3,2,1,0:T(8,128)(2,1)} %get-tuple-element.8), calls=%async_computation.2 | async-start | bytes 4194304 | tf_op jit(solution)/shard_map/all_to_all | solution.py:73
  211.1 5.2 %copy-start.4 = (s32[1,32]{1,0:T(1,128)S(1)}, s32[1,32]{1,0:T(1,128)}, u32[]{:S(2)}) copy-start(s32[1,32]{1,0:T(1,128)} %weights_ref.1) | copy-start | bytes 388
  215.5 2.1 collective-permute-start
  218.4 21.4 %all-to-all-start.4 = ((bf16[8,40,512]{2,1,0:T(8,128)(2,1)}), bf16[8,40,512]{2,1,0:T(8,128)(2,1)S(1)}, u32[]{:S(2)}, u32[]{:S(2)}) async-start(bf16[8,40,512]{2,1,0:T(8,128)(2,1)} %add_convert_fusion), calls=%async_computation.4 | async-start | bytes 655360 | tf_op jit(solution)/shard_map/all_to_all | solution.py:73
  240.7 12.7 %all-to-all-start.5 = ((bf16[8,32,512]{2,1,0:T(8,128)(2,1)}), bf16[8,32,512]{2,1,0:T(8,128)(2,1)S(1)}, u32[]{:S(2)}, u32[]{:S(2)}) async-start(bf16[8,32,512]{2,1,0:T(8,128)(2,1)} %broadcast_in_dim.22), calls=%async_computation.5 | async-start | bytes 524288 | tf_op jit(solution)/shard_map/all_to_all | solution.py:73
  244.7 1.2 collective-permute-start.2
  253.4 1.5 collective-permute-start.1

commit v8 on v7

--- a/solution.py
+++ b/solution.py
@@ -426,7 +426,9 @@
         odd = inner(imag, other_real) - inner(real, other_imag)
         return even * (1.0 / GVECS), odd * (1.0 / GVECS)
 
-    even, odd = margins(real, imag)
+    even = (inner(real, real) + inner(imag, imag)) * (1.0 / GVECS)
+    odd = inner(imag, real) * (1.0 / GVECS)
+    odd = odd - odd.T
     row = lax.broadcasted_iota(jnp.int32, (share, share), 0)
     column = lax.broadcasted_iota(jnp.int32, (share, share), 1)
     own = jnp.where(row <= column, even, odd)
@@ -498,7 +500,7 @@
 
     @pl.when(pl.program_id(0) == 0)
     def _():
-        mine, others = mine_ref[...].astype(f32), other_ref[...].astype(f32)
+        mine, others = mine_ref[...], other_ref[...]
         first = core_ref[0] == 0
         packed = jnp.concatenate(
             [jnp.where(first, mine, others), jnp.where(first, others, mine)], 0
@@ -510,21 +512,22 @@
         for lower, down in enumerate(spans):
             own = packed[down, down]
             flipped = own.T
-            even[down, down] = jnp.where(row <= column, own, flipped).astype(bf16)
-            above = jnp.where(row == column, 0.0, -flipped)
-            odd[down, down] = jnp.where(row > column, own, above).astype(bf16)
+            even[down, down] = jnp.where(row <= column, own, flipped)
+            above = jnp.where(row == column, jnp.zeros_like(own), -flipped)
+            odd[down, down] = jnp.where(row > column, own, above)
             for over in spans[:lower]:
                 both, opposite = packed[over, down], packed[down, over]
-                even[down, over] = both.astype(bf16)
-                even[over, down] = both.T.astype(bf16)
-                odd[down, over] = opposite.astype(bf16)
-                odd[over, down] = -opposite.T.astype(bf16)
+                even[down, over] = both
+                even[over, down] = both.T
+                odd[down, over] = opposite
+                odd[over, down] = -opposite.T
 
     parted = [split_rows(trial[...]) for trial in trials]
     real = jnp.concatenate([part[0] for part in parted], 0)
     imag = jnp.concatenate([part[1] for part in parted], 0)
-    out_ref[:, 0, :] = (matmul(even[...], real) - matmul(odd[...], imag)).astype(bf16)
-    out_ref[:, 1, :] = (matmul(even[...], imag) + matmul(odd[...], real)).astype(bf16)
+    both = jnp.concatenate([real, imag], 0)
+    out_ref[:, 0, :] = matmul(jnp.concatenate([even[...], -odd[...]], 1), both).astype(bf16)
+    out_ref[:, 1, :] = matmul(jnp.concatenate([odd[...], even[...]], 1), both).astype(bf16)
 
 
 def update_waves(core, mine, others, trials):

time: 264 us -> 264 us (level)
  no operation moved by 1% of the time
where the time goes in v8:
time: 264 us; the launch traced here: 263 us
  waiting for transfers between devices  103 us (39%)
  Pallas kernels  85.2 us (32%)
  starting transfers between devices  53.5 us (20%)
  local copies, waits for them, and re-layouts  12.2 us (5%)
  other arithmetic  8.31 us (3%)
    all_to_all x6, waiting for transfers between devices, exchange(): lax.all_to_all(blocks, 'ga', split_axis=0, concat_axis=0, tiled=True, axi...  101 us
    pallas_call x2, Pallas kernels, make_trial(): pl.pallas_call(functools.partial(wave_kernel, band_count), grid=(steps,),...  68.1 us
    all_to_all x6, starting transfers between devices, exchange(): lax.all_to_all(blocks, 'ga', split_axis=0, concat_axis=0, tiled=True, axi...  52.6 us
    pallas_call x1, Pallas kernels, update_waves(): pl.pallas_call(functools.partial(update_kernel, count), grid=(local_g //...  8.34 us
  transfers between devices with their start and end apart: 9, of which 8 were waited for; matrix products, arithmetic and copies ran while one was open for 7% of the time, Pallas kernels for 26%

profile of v8, /device:TPU:0, one launch (start us, length us, event | category | flops | bytes accessed | tf_op | source)
XLA Modules:
  0.0 263.0 jit_solution(18237446222654868353)
XLA Ops:
  0.6 3.7 %shard_map.104 = bf16[16,65,2,512]{3,2,1,0:T(2,128)(2,1)} custom-call(f32[3,32,48]{2,1,0:T(8,128)} %bitcast.46, s32[1,32]{1,0:T(1,128)} %weights_ref.1, bf16[1,512,2,2048]{3,2,1,0:T(2,128)(2,1)} %psi_ref.1), custom_call_target="tpu_custom_call" | custom-call | bytes 4194304 | tf_op jit(solution)/shard_map/pallas_call | solution.py:190
  4.3 7.4 %all-to-all-start.1 = ((bf16[16,65,2,512]{3,2,1,0:T(2,128)(2,1)}), bf16[16,65,2,512]{3,2,1,0:T(2,128)(2,1)}, u32[]{:S(2)}, u32[]{:S(2)}) async-start(bf16[16,65,2,512]{3,2,1,0:T(2,128)(2,1)} %shard_map.104), calls=%async_computation.1 | async-start | bytes 4259840 | tf_op jit(solution)/shard_map/all_to_all | solution.py:73
  11.8 4.4 %slice.61 = bf16[1,256,2,2048]{3,2,1,0:T(2,128)(2,1)} slice(bf16[1,512,2,2048]{3,2,1,0:T(2,128)(2,1)} %psi_ref.1), slice={[0:1], [256:512], [0:2], [0:2048]} | slice | bytes 4194304 | tf_op jit(solution)/shard_map/slice | solution.py:572
  16.2 37.3 %all-to-all-done.1.wave_ref = bf16[16,65,2,512]{3,2,1,0:T(2,128)(2,1)} async-done(((bf16[16,65,2,512]{3,2,1,0:T(2,128)(2,1)}), bf16[16,65,2,512]{3,2,1,0:T(2,128)(2,1)}, u32[]{:S(2)}, u32[]{:S(2)}) %all-to-all-start.1) | async-done | bytes 2129952 | tf_op jit(solution)/shard_map/all_to_all | solution.py:73
  53.5 11.5 %all-to-all-start = ((bf16[16,16,2,2048]{3,2,1,0:T(2,128)(2,1)}), bf16[16,16,2,2048]{3,2,1,0:T(2,128)(2,1)}, u32[]{:S(2)}, u32[]{:S(2)}) async-start(bf16[16,16,2,2048]{3,2,1,0:T(2,128)(2,1)} %bitcast.1), calls=%async_computation | async-start | bytes 4194304 | tf_op jit(solution)/shard_map/all_to_all | solution.py:73
  66.2 0.7 mul.925.pot_ref
  66.9 0.7 multiply_subtract_fusion.kept_ref
  67.6 0.8 slice.79
  68.5 1.8 slice.64
  70.8 0.7 pad_maximum_fusion.3.along_ref
  71.5 1.5 fusion.7
  73.5 1.9 pad_maximum_fusion.in_plane_ref
  75.3 34.2 %shard_map.106 = (bf16[16,2,16,2048]{3,2,1,0:T(8,128)(2,1)}, f32[3,8,256]{2,1,0:T(8,128)}) custom-call(bf16[16,65,2,512]{3,2,1,0:T(2,128)(2,1)} %all-to-all-done.1.wave_ref, bf16[1024,1024]{1,0:T(8,128)(2,1)} %constant.38.clone.cos_ref, bf16[1024,1024]{1,0:T(8,128)(2,1)} %constant.39.clone.sin_ref, bf16[512,1024]{1,0:T(8,128)(2,1)} %constant.130.clone.back_ref, ...), custom_call_target="tpu_custom_call" | custom-call | flops 17179869184 | bytes 16777216 | tf_op jit(solution)/shard_map/pallas_call | solution.py:370
  109.5 7.9 %all-to-all-start.3 = ((bf16[16,2,16,2048]{3,2,1,0:T(8,128)(2,1)}), bf16[16,2,16,2048]{3,2,1,0:T(8,128)(2,1)S(1)}, u32[]{:S(2)}, u32[]{:S(2)}) async-start(bf16[16,2,16,2048]{3,2,1,0:T(8,128)(2,1)} %get-tuple-element.11), calls=%async_computation.3 | async-start | bytes 4194304 | tf_op jit(solution)/shard_map/all_to_all | solution.py:73
  117.5 33.8 %shard_map.105 = (bf16[16,2,16,2048]{3,2,1,0:T(8,128)(2,1)}, f32[3,8,256]{2,1,0:T(8,128)}) custom-call(bf16[16,16,2,2048]{3,2,1,0:T(2,128)(2,1)} %all-to-all-done.wave_ref, bf16[1024,1024]{1,0:T(8,128)(2,1)} %constant.38.clone.cos_ref, bf16[1024,1024]{1,0:T(8,128)(2,1)} %constant.39.clone.sin_ref, bf16[512,1024]{1,0:T(8,128)(2,1)} %constant.130.clone.back_ref, ...), custom_call_target="tpu_custom_call" | custom-call | flops 17179869184 | bytes 16777216 | tf_op jit(solution)/shard_map/pallas_call | solution.py:370
  151.3 7.2 %all-to-all-done.3 = bf16[16,2,16,2048]{3,2,1,0:T(8,128)(2,1)S(1)} async-done(((bf16[16,2,16,2048]{3,2,1,0:T(8,128)(2,1)}), bf16[16,2,16,2048]{3,2,1,0:T(8,128)(2,1)S(1)}, u32[]{:S(2)}, u32[]{:S(2)}) %all-to-all-start.3) | async-done | bytes 2097184 | tf_op jit(solution)/shard_map/all_to_all | solution.py:73
  158.6 11.4 %all-to-all-start.2 = ((bf16[16,2,16,2048]{3,2,1,0:T(8,128)(2,1)}), bf16[16,2,16,2048]{3,2,1,0:T(8,128)(2,1)}, u32[]{:S(2)}, u32[]{:S(2)}) async-start(bf16[16,2,16,2048]{3,2,1,0:T(8,128)(2,1)} %get-tuple-element.8), calls=%async_computation.2 | async-start | bytes 4194304 | tf_op jit(solution)/shard_map/all_to_all | solution.py:73
  171.2 1.1 shard_map.107.refs_2_
  172.3 38.9 %all-to-all-done.2 = bf16[16,2,16,2048]{3,2,1,0:T(8,128)(2,1)} async-done(((bf16[16,2,16,2048]{3,2,1,0:T(8,128)(2,1)}), bf16[16,2,16,2048]{3,2,1,0:T(8,128)(2,1)}, u32[]{:S(2)}, u32[]{:S(2)}) %all-to-all-start.2) | async-done | bytes 2097184 | tf_op jit(solution)/shard_map/all_to_all | solution.py:73
  211.1 4.0 %shard_map.108 = (f32[8,40,512]{2,1,0:T(8,128)S(1)}, bf16[8,40,512]{2,1,0:T(8,128)(2,1)S(1)}) custom-call(s32[1]{0:T(128)} %bitcast.core_ref, bf16[512,2048]{1,0:T(8,128)(2,1)} %bitcast.4.trial_ref.refs_1_, f32[8,8,512]{2,1,0:T(8,128)S(1)} %bitcast.45, bf16[512,2048]{1,0:T(8,128)(2,1)S(1)} %bitcast.41, f32[256,256]{1,0:T(8,128)S(1)} %shard_map.107.refs_2_), custom_call_target="tpu_custom_call" | custom-call | flops 2147483648 | bytes 4194304 | tf_op jit(solution)/shard_map/pallas_call | solution.py:483
  215.2 0.8 collective-permute-start
  216.6 0.6 collective-permute-done
  217.3 0.8 add_convert_fusion
  218.1 10.7 %all-to-all-start.4 = ((bf16[8,40,512]{2,1,0:T(8,128)(2,1)}), bf16[8,40,512]{2,1,0:T(8,128)(2,1)S(1)}, u32[]{:S(2)}, u32[]{:S(2)}) async-start(bf16[8,40,512]{2,1,0:T(8,128)(2,1)} %add_convert_fusion), calls=%async_computation.4 | async-start | bytes 655360 | tf_op jit(solution)/shard_map/all_to_all | solution.py:73
  228.8 0.6 divide_bitcast_fusion
  229.5 10.0 %all-to-all-done.4 = bf16[8,40,512]{2,1,0:T(8,128)(2,1)S(1)} async-done(((bf16[8,40,512]{2,1,0:T(8,128)(2,1)}), bf16[8,40,512]{2,1,0:T(8,128)(2,1)S(1)}, u32[]{:S(2)}, u32[]{:S(2)}) %all-to-all-start.4) | async-done | bytes 327712 | tf_op jit(solution)/shard_map/all_to_all | solution.py:73
  239.7 0.7 broadcast_in_dim.22
  240.4 3.6 %all-to-all-start.5 = ((bf16[8,32,512]{2,1,0:T(8,128)(2,1)}), bf16[8,32,512]{2,1,0:T(8,128)(2,1)S(1)}, u32[]{:S(2)}, u32[]{:S(2)}) async-start(bf16[8,32,512]{2,1,0:T(8,128)(2,1)} %broadcast_in_dim.22), calls=%async_computation.5 | async-start | bytes 524288 | tf_op jit(solution)/shard_map/all_to_all | solution.py:73
  244.8 0.8 collective-permute-done.2
  245.7 7.5 %all-to-all-done.5 = bf16[8,32,512]{2,1,0:T(8,128)(2,1)S(1)} async-done(((bf16[8,32,512]{2,1,0:T(8,128)(2,1)}), bf16[8,32,512]{2,1,0:T(8,128)(2,1)S(1)}, u32[]{:S(2)}, u32[]{:S(2)}) %all-to-all-start.5) | async-done | bytes 262176 | tf_op jit(solution)/shard_map/all_to_all | solution.py:73
  253.5 0.7 copy.29
  254.7 8.3 %shard_map.109 = bf16[512,2,2048]{2,1,0:T(2,128)(2,1)} custom-call(s32[1]{0:T(128)} %bitcast.core_ref, bf16[256,512]{1,0:T(8,128)(2,1)S(1)} %bitcast.44, bf16[256,512]{1,0:T(8,128)(2,1)S(1)} %collective-permute-done.1.other_ref, bf16[512,2048]{1,0:T(8,128)(2,1)S(1)} %bitcast.42, bf16[512,2048]{1,0:T(8,128)(2,1)} %bitcast.4.trial_ref.refs_1_), custom_call_target="tpu_custom_call" | custom-call | flops 4294967296 | bytes 8388608 | tf_op jit(solution)/shard_map/pallas_call | solution.py:538
  (77 shorter events, 5.8 us)
Async XLA Ops:
  4.3 49.2 %all-to-all-start.1 = ((bf16[16,65,2,512]{3,2,1,0:T(2,128)(2,1)}), bf16[16,65,2,512]{3,2,1,0:T(2,128)(2,1)}, u32[]{:S(2)}, u32[]{:S(2)}) async-start(bf16[16,65,2,512]{3,2,1,0:T(2,128)(2,1)} %shard_map.104), calls=%async_computation.1 | async-start | bytes 4259840 | tf_op jit(solution)/shard_map/all_to_all | solution.py:73
  53.5 12.3 %copy-start.1 = (f32[1,32768]{1,0:T(1,128)S(1)}, f32[1,32768]{1,0:T(1,128)}, u32[]{:S(2)}) copy-start(f32[1,32768]{1,0:T(1,128)} %param.12) | copy-start | bytes 393220
  53.5 56.0 %all-to-all-start = ((bf16[16,16,2,2048]{3,2,1,0:T(2,128)(2,1)}), bf16[16,16,2,2048]{3,2,1,0:T(2,128)(2,1)}, u32[]{:S(2)}, u32[]{:S(2)}) async-start(bf16[16,16,2,2048]{3,2,1,0:T(2,128)(2,1)} %bitcast.1), calls=%async_computation | async-start | bytes 4194304 | tf_op jit(solution)/shard_map/all_to_all | solution.py:73
  109.5 49.0 %all-to-all-start.3 = ((bf16[16,2,16,2048]{3,2,1,0:T(8,128)(2,1)}), bf16[16,2,16,2048]{3,2,1,0:T(8,128)(2,1)S(1)}, u32[]{:S(2)}, u32[]{:S(2)}) async-start(bf16[16,2,16,2048]{3,2,1,0:T(8,128)(2,1)} %get-tuple-element.11), calls=%async_computation.3 | async-start | bytes 4194304 | tf_op jit(solution)/shard_map/all_to_all | solution.py:73
  151.3 18.7 %copy-start = (f32[32,3,48]{2,0,1:T(8,128)S(1)}, f32[32,3,48]{2,0,1:T(8,128)}, u32[]{:S(2)}) copy-start(f32[32,3,48]{2,0,1:T(8,128)} %param.9) | copy-start | bytes 55300
  158.6 12.3 %copy-start.2 = (f32[3,8,256]{2,1,0:T(8,128)S(1)}, f32[3,8,256]{2,1,0:T(8,128)}, u32[]{:S(2)}) copy-start(f32[3,8,256]{2,1,0:T(8,128)} %get-tuple-element.9) | copy-start | bytes 73732
  158.6 12.3 %copy-start.3 = (f32[3,8,256]{2,1,0:T(8,128)S(1)}, f32[3,8,256]{2,1,0:T(8,128)}, u32[]{:S(2)}) copy-start(f32[3,8,256]{2,1,0:T(8,128)} %get-tuple-element.10) | copy-start | bytes 73732
  158.6 52.6 %all-to-all-start.2 = ((bf16[16,2,16,2048]{3,2,1,0:T(8,128)(2,1)}), bf16[16,2,16,2048]{3,2,1,0:T(8,128)(2,1)}, u32[]{:S(2)}, u32[]{:S(2)}) async-start(bf16[16,2,16,2048]{3,2,1,0:T(8,128)(2,1)} %get-tuple-element.8), calls=%async_computation.2 | async-start | bytes 4194304 | tf_op jit(solution)/shard_map/all_to_all | solution.py:73
  211.1 4.9 %copy-start.4 = (s32[1,32]{1,0:T(1,128)S(1)}, s32[1,32]{1,0:T(1,128)}, u32[]{:S(2)}) copy-start(s32[1,32]{1,0:T(1,128)} %weights_ref.1) | copy-start | bytes 388
  215.2 2.1 collective-permute-start
  218.1 21.5 %all-to-all-start.4 = ((bf16[8,40,512]{2,1,0:T(8,128)(2,1)}), bf16[8,40,512]{2,1,0:T(8,128)(2,1)S(1)}, u32[]{:S(2)}, u32[]{:S(2)}) async-start(bf16[8,40,512]{2,1,0:T(8,128)(2,1)} %add_convert_fusion), calls=%async_computation.4 | async-start | bytes 655360 | tf_op jit(solution)/shard_map/all_to_all | solution.py:73
  240.4 12.7 %all-to-all-start.5 = ((bf16[8,32,512]{2,1,0:T(8,128)(2,1)}), bf16[8,32,512]{2,1,0:T(8,128)(2,1)S(1)}, u32[]{:S(2)}, u32[]{:S(2)}) async-start(bf16[8,32,512]{2,1,0:T(8,128)(2,1)} %broadcast_in_dim.22), calls=%async_computation.5 | async-start | bytes 524288 | tf_op jit(solution)/shard_map/all_to_all | solution.py:73
  244.4 1.2 collective-permute-start.2
  253.2 1.5 collective-permute-start.1

commit v9 on v8

--- a/solution.py
+++ b/solution.py
@@ -31,7 +31,7 @@
 GROUP = 8
 SLAB = 128
 LANES = 256
-WIDE = 1024
+WIDE = 512
 PIECE = 512
 VMEM_BYTES = 56 * 2**20
 TAIL_VMEM_BYTES = 60 * 2**20

time: 264 us -> 264 us (level)
  no operation moved by 1% of the time
where the time goes in v9:
time: 264 us; the launch traced here: 263 us
  waiting for transfers between devices  103 us (39%)
  Pallas kernels  85.3 us (32%)
  starting transfers between devices  53.5 us (20%)
  local copies, waits for them, and re-layouts  12.2 us (5%)
  other arithmetic  8.31 us (3%)
    all_to_all x6, waiting for transfers between devices, exchange(): lax.all_to_all(blocks, 'ga', split_axis=0, concat_axis=0, tiled=True, axi...  101 us
    pallas_call x2, Pallas kernels, make_trial(): pl.pallas_call(functools.partial(wave_kernel, band_count), grid=(steps,),...  68.1 us
    all_to_all x6, starting transfers between devices, exchange(): lax.all_to_all(blocks, 'ga', split_axis=0, concat_axis=0, tiled=True, axi...  52.6 us
    pallas_call x1, Pallas kernels, update_waves(): pl.pallas_call(functools.partial(update_kernel, count), grid=(local_g //...  8.44 us
  transfers between devices with their start and end apart: 9, of which 8 were waited for; matrix products, arithmetic and copies ran while one was open for 7% of the time, Pallas kernels for 26%

profile of v9, /device:TPU:0, one launch (start us, length us, event | category | flops | bytes accessed | tf_op | source)
XLA Modules:
  0.0 263.1 jit_solution(12064068445269950953)
XLA Ops:
  0.6 3.7 %shard_map.104 = bf16[16,65,2,512]{3,2,1,0:T(2,128)(2,1)} custom-call(f32[3,32,48]{2,1,0:T(8,128)} %bitcast.46, s32[1,32]{1,0:T(1,128)} %weights_ref.1, bf16[1,512,2,2048]{3,2,1,0:T(2,128)(2,1)} %psi_ref.1), custom_call_target="tpu_custom_call" | custom-call | bytes 4194304 | tf_op jit(solution)/shard_map/pallas_call | solution.py:190
  4.3 7.4 %all-to-all-start.1 = ((bf16[16,65,2,512]{3,2,1,0:T(2,128)(2,1)}), bf16[16,65,2,512]{3,2,1,0:T(2,128)(2,1)}, u32[]{:S(2)}, u32[]{:S(2)}) async-start(bf16[16,65,2,512]{3,2,1,0:T(2,128)(2,1)} %shard_map.104), calls=%async_computation.1 | async-start | bytes 4259840 | tf_op jit(solution)/shard_map/all_to_all | solution.py:73
  11.8 4.4 %slice.61 = bf16[1,256,2,2048]{3,2,1,0:T(2,128)(2,1)} slice(bf16[1,512,2,2048]{3,2,1,0:T(2,128)(2,1)} %psi_ref.1), slice={[0:1], [256:512], [0:2], [0:2048]} | slice | bytes 4194304 | tf_op jit(solution)/shard_map/slice | solution.py:572
  16.2 37.3 %all-to-all-done.1.wave_ref = bf16[16,65,2,512]{3,2,1,0:T(2,128)(2,1)} async-done(((bf16[16,65,2,512]{3,2,1,0:T(2,128)(2,1)}), bf16[16,65,2,512]{3,2,1,0:T(2,128)(2,1)}, u32[]{:S(2)}, u32[]{:S(2)}) %all-to-all-start.1) | async-done | bytes 2129952 | tf_op jit(solution)/shard_map/all_to_all | solution.py:73
  53.5 11.5 %all-to-all-start = ((bf16[16,16,2,2048]{3,2,1,0:T(2,128)(2,1)}), bf16[16,16,2,2048]{3,2,1,0:T(2,128)(2,1)}, u32[]{:S(2)}, u32[]{:S(2)}) async-start(bf16[16,16,2,2048]{3,2,1,0:T(2,128)(2,1)} %bitcast.1), calls=%async_computation | async-start | bytes 4194304 | tf_op jit(solution)/shard_map/all_to_all | solution.py:73
  66.2 0.7 mul.925.pot_ref
  66.9 0.7 multiply_subtract_fusion.kept_ref
  67.6 0.8 slice.79
  68.5 1.8 slice.64
  70.8 0.7 pad_maximum_fusion.3.along_ref
  71.5 1.5 fusion.7
  73.5 1.9 pad_maximum_fusion.in_plane_ref
  75.3 34.2 %shard_map.106 = (bf16[16,2,16,2048]{3,2,1,0:T(8,128)(2,1)}, f32[3,8,256]{2,1,0:T(8,128)}) custom-call(bf16[16,65,2,512]{3,2,1,0:T(2,128)(2,1)} %all-to-all-done.1.wave_ref, bf16[1024,1024]{1,0:T(8,128)(2,1)} %constant.38.clone.cos_ref, bf16[1024,1024]{1,0:T(8,128)(2,1)} %constant.39.clone.sin_ref, bf16[512,1024]{1,0:T(8,128)(2,1)} %constant.130.clone.back_ref, ...), custom_call_target="tpu_custom_call" | custom-call | flops 17179869184 | bytes 16777216 | tf_op jit(solution)/shard_map/pallas_call | solution.py:370
  109.5 7.9 %all-to-all-start.3 = ((bf16[16,2,16,2048]{3,2,1,0:T(8,128)(2,1)}), bf16[16,2,16,2048]{3,2,1,0:T(8,128)(2,1)S(1)}, u32[]{:S(2)}, u32[]{:S(2)}) async-start(bf16[16,2,16,2048]{3,2,1,0:T(8,128)(2,1)} %get-tuple-element.11), calls=%async_computation.3 | async-start | bytes 4194304 | tf_op jit(solution)/shard_map/all_to_all | solution.py:73
  117.5 33.8 %shard_map.105 = (bf16[16,2,16,2048]{3,2,1,0:T(8,128)(2,1)}, f32[3,8,256]{2,1,0:T(8,128)}) custom-call(bf16[16,16,2,2048]{3,2,1,0:T(2,128)(2,1)} %all-to-all-done.wave_ref, bf16[1024,1024]{1,0:T(8,128)(2,1)} %constant.38.clone.cos_ref, bf16[1024,1024]{1,0:T(8,128)(2,1)} %constant.39.clone.sin_ref, bf16[512,1024]{1,0:T(8,128)(2,1)} %constant.130.clone.back_ref, ...), custom_call_target="tpu_custom_call" | custom-call | flops 17179869184 | bytes 16777216 | tf_op jit(solution)/shard_map/pallas_call | solution.py:370
  151.3 7.2 %all-to-all-done.3 = bf16[16,2,16,2048]{3,2,1,0:T(8,128)(2,1)S(1)} async-done(((bf16[16,2,16,2048]{3,2,1,0:T(8,128)(2,1)}), bf16[16,2,16,2048]{3,2,1,0:T(8,128)(2,1)S(1)}, u32[]{:S(2)}, u32[]{:S(2)}) %all-to-all-start.3) | async-done | bytes 2097184 | tf_op jit(solution)/shard_map/all_to_all | solution.py:73
  158.6 11.4 %all-to-all-start.2 = ((bf16[16,2,16,2048]{3,2,1,0:T(8,128)(2,1)}), bf16[16,2,16,2048]{3,2,1,0:T(8,128)(2,1)}, u32[]{:S(2)}, u32[]{:S(2)}) async-start(bf16[16,2,16,2048]{3,2,1,0:T(8,128)(2,1)} %get-tuple-element.8), calls=%async_computation.2 | async-start | bytes 4194304 | tf_op jit(solution)/shard_map/all_to_all | solution.py:73
  171.2 1.1 shard_map.107.refs_2_
  172.3 38.9 %all-to-all-done.2 = bf16[16,2,16,2048]{3,2,1,0:T(8,128)(2,1)} async-done(((bf16[16,2,16,2048]{3,2,1,0:T(8,128)(2,1)}), bf16[16,2,16,2048]{3,2,1,0:T(8,128)(2,1)}, u32[]{:S(2)}, u32[]{:S(2)}) %all-to-all-start.2) | async-done | bytes 2097184 | tf_op jit(solution)/shard_map/all_to_all | solution.py:73
  211.1 4.0 %shard_map.108 = (f32[8,40,512]{2,1,0:T(8,128)S(1)}, bf16[8,40,512]{2,1,0:T(8,128)(2,1)S(1)}) custom-call(s32[1]{0:T(128)} %bitcast.core_ref, bf16[512,2048]{1,0:T(8,128)(2,1)} %bitcast.4.trial_ref.refs_1_, f32[8,8,512]{2,1,0:T(8,128)S(1)} %bitcast.45, bf16[512,2048]{1,0:T(8,128)(2,1)S(1)} %bitcast.41, f32[256,256]{1,0:T(8,128)S(1)} %shard_map.107.refs_2_), custom_call_target="tpu_custom_call" | custom-call | flops 2147483648 | bytes 4194304 | tf_op jit(solution)/shard_map/pallas_call | solution.py:483
  215.2 0.8 collective-permute-start
  216.6 0.6 collective-permute-done
  217.3 0.8 add_convert_fusion
  218.1 10.7 %all-to-all-start.4 = ((bf16[8,40,512]{2,1,0:T(8,128)(2,1)}), bf16[8,40,512]{2,1,0:T(8,128)(2,1)S(1)}, u32[]{:S(2)}, u32[]{:S(2)}) async-start(bf16[8,40,512]{2,1,0:T(8,128)(2,1)} %add_convert_fusion), calls=%async_computation.4 | async-start | bytes 655360 | tf_op jit(solution)/shard_map/all_to_all | solution.py:73
  228.8 0.6 divide_bitcast_fusion
  229.5 10.0 %all-to-all-done.4 = bf16[8,40,512]{2,1,0:T(8,128)(2,1)S(1)} async-done(((bf16[8,40,512]{2,1,0:T(8,128)(2,1)}), bf16[8,40,512]{2,1,0:T(8,128)(2,1)S(1)}, u32[]{:S(2)}, u32[]{:S(2)}) %all-to-all-start.4) | async-done | bytes 327712 | tf_op jit(solution)/shard_map/all_to_all | solution.py:73
  239.7 0.7 broadcast_in_dim.22
  240.4 3.6 %all-to-all-start.5 = ((bf16[8,32,512]{2,1,0:T(8,128)(2,1)}), bf16[8,32,512]{2,1,0:T(8,128)(2,1)S(1)}, u32[]{:S(2)}, u32[]{:S(2)}) async-start(bf16[8,32,512]{2,1,0:T(8,128)(2,1)} %broadcast_in_dim.22), calls=%async_computation.5 | async-start | bytes 524288 | tf_op jit(solution)/shard_map/all_to_all | solution.py:73
  244.8 0.8 collective-permute-done.2
  245.7 7.5 %all-to-all-done.5 = bf16[8,32,512]{2,1,0:T(8,128)(2,1)S(1)} async-done(((bf16[8,32,512]{2,1,0:T(8,128)(2,1)}), bf16[8,32,512]{2,1,0:T(8,128)(2,1)S(1)}, u32[]{:S(2)}, u32[]{:S(2)}) %all-to-all-start.5) | async-done | bytes 262176 | tf_op jit(solution)/shard_map/all_to_all | solution.py:73
  253.5 0.7 copy.29
  254.7 8.4 %shard_map.109 = bf16[512,2,2048]{2,1,0:T(2,128)(2,1)} custom-call(s32[1]{0:T(128)} %bitcast.core_ref, bf16[256,512]{1,0:T(8,128)(2,1)S(1)} %bitcast.44, bf16[256,512]{1,0:T(8,128)(2,1)S(1)} %collective-permute-done.1.other_ref, bf16[512,2048]{1,0:T(8,128)(2,1)S(1)} %bitcast.42, bf16[512,2048]{1,0:T(8,128)(2,1)} %bitcast.4.trial_ref.refs_1_), custom_call_target="tpu_custom_call" | custom-call | flops 4294967296 | bytes 8388608 | tf_op jit(solution)/shard_map/pallas_call | solution.py:538
  (77 shorter events, 5.8 us)
Async XLA Ops:
  4.3 49.2 %all-to-all-start.1 = ((bf16[16,65,2,512]{3,2,1,0:T(2,128)(2,1)}), bf16[16,65,2,512]{3,2,1,0:T(2,128)(2,1)}, u32[]{:S(2)}, u32[]{:S(2)}) async-start(bf16[16,65,2,512]{3,2,1,0:T(2,128)(2,1)} %shard_map.104), calls=%async_computation.1 | async-start | bytes 4259840 | tf_op jit(solution)/shard_map/all_to_all | solution.py:73
  53.5 12.3 %copy-start.1 = (f32[1,32768]{1,0:T(1,128)S(1)}, f32[1,32768]{1,0:T(1,128)}, u32[]{:S(2)}) copy-start(f32[1,32768]{1,0:T(1,128)} %param.12) | copy-start | bytes 393220
  53.5 56.0 %all-to-all-start = ((bf16[16,16,2,2048]{3,2,1,0:T(2,128)(2,1)}), bf16[16,16,2,2048]{3,2,1,0:T(2,128)(2,1)}, u32[]{:S(2)}, u32[]{:S(2)}) async-start(bf16[16,16,2,2048]{3,2,1,0:T(2,128)(2,1)} %bitcast.1), calls=%async_computation | async-start | bytes 4194304 | tf_op jit(solution)/shard_map/all_to_all | solution.py:73
  109.5 49.0 %all-to-all-start.3 = ((bf16[16,2,16,2048]{3,2,1,0:T(8,128)(2,1)}), bf16[16,2,16,2048]{3,2,1,0:T(8,128)(2,1)S(1)}, u32[]{:S(2)}, u32[]{:S(2)}) async-start(bf16[16,2,16,2048]{3,2,1,0:T(8,128)(2,1)} %get-tuple-element.11), calls=%async_computation.3 | async-start | bytes 4194304 | tf_op jit(solution)/shard_map/all_to_all | solution.py:73
  151.3 18.7 %copy-start = (f32[32,3,48]{2,0,1:T(8,128)S(1)}, f32[32,3,48]{2,0,1:T(8,128)}, u32[]{:S(2)}) copy-start(f32[32,3,48]{2,0,1:T(8,128)} %param.9) | copy-start | bytes 55300
  158.6 12.3 %copy-start.2 = (f32[3,8,256]{2,1,0:T(8,128)S(1)}, f32[3,8,256]{2,1,0:T(8,128)}, u32[]{:S(2)}) copy-start(f32[3,8,256]{2,1,0:T(8,128)} %get-tuple-element.9) | copy-start | bytes 73732
  158.6 12.3 %copy-start.3 = (f32[3,8,256]{2,1,0:T(8,128)S(1)}, f32[3,8,256]{2,1,0:T(8,128)}, u32[]{:S(2)}) copy-start(f32[3,8,256]{2,1,0:T(8,128)} %get-tuple-element.10) | copy-start | bytes 73732
  158.6 52.6 %all-to-all-start.2 = ((bf16[16,2,16,2048]{3,2,1,0:T(8,128)(2,1)}), bf16[16,2,16,2048]{3,2,1,0:T(8,128)(2,1)}, u32[]{:S(2)}, u32[]{:S(2)}) async-start(bf16[16,2,16,2048]{3,2,1,0:T(8,128)(2,1)} %get-tuple-element.8), calls=%async_computation.2 | async-start | bytes 4194304 | tf_op jit(solution)/shard_map/all_to_all | solution.py:73
  211.1 4.9 %copy-start.4 = (s32[1,32]{1,0:T(1,128)S(1)}, s32[1,32]{1,0:T(1,128)}, u32[]{:S(2)}) copy-start(s32[1,32]{1,0:T(1,128)} %weights_ref.1) | copy-start | bytes 388
  215.2 2.1 collective-permute-start
  218.1 21.5 %all-to-all-start.4 = ((bf16[8,40,512]{2,1,0:T(8,128)(2,1)}), bf16[8,40,512]{2,1,0:T(8,128)(2,1)S(1)}, u32[]{:S(2)}, u32[]{:S(2)}) async-start(bf16[8,40,512]{2,1,0:T(8,128)(2,1)} %add_convert_fusion), calls=%async_computation.4 | async-start | bytes 655360 | tf_op jit(solution)/shard_map/all_to_all | solution.py:73
  240.4 12.7 %all-to-all-start.5 = ((bf16[8,32,512]{2,1,0:T(8,128)(2,1)}), bf16[8,32,512]{2,1,0:T(8,128)(2,1)S(1)}, u32[]{:S(2)}, u32[]{:S(2)}) async-start(bf16[8,32,512]{2,1,0:T(8,128)(2,1)} %broadcast_in_dim.22), calls=%async_computation.5 | async-start | bytes 524288 | tf_op jit(solution)/shard_map/all_to_all | solution.py:73
  244.4 1.2 collective-permute-start.2
  253.2 1.5 collective-permute-start.1
